TPU v7x, 32 devices: a whole 2x2x4 slice. The times are simulated.
32 devices in a mesh: rows: 4 (over x, core), seq: 8 (over z, y).
Axes of the slice: x: 2, y: 2, z: 4, core: 2. Of those that a mesh axis runs over, the one named last changes fastest.
Arguments:
- inputs: bfloat16 [8, 1024, 2048], P('rows', 'seq'), may hold values from -6 to 6
- cotangent: bfloat16 [8, 1024, 2048], P('rows', 'seq'), may hold values from -6 to 6
- positions: int32 [8, 1024], P('rows', 'seq'), may hold values from 0 to 4095, as said below
- segment_ids: int32 [8, 1024], P('rows', 'seq'), may hold values from 0 to 3, as said below
- w_query: bfloat16 [2048, 1280], P(('rows', 'seq')), may hold values from -0.125 to 0.125
- w_key: bfloat16 [2048, 320], P(('rows', 'seq')), may hold values from -0.125 to 0.125
- w_value: bfloat16 [2048, 320], P(('rows', 'seq')), may hold values from -0.125 to 0.125
- w_out: bfloat16 [1280, 2048], P(('rows', 'seq')), may hold values from -0.625 to 0.625
- w_gate: bfloat16 [2048, 6656], P('seq', 'rows'), may hold values from -0.125 to 0.125
- w_up: bfloat16 [2048, 6656], P('seq', 'rows'), may hold values from -0.125 to 0.125
- w_down: bfloat16 [6656, 2048], P('rows', 'seq'), may hold values from -0.078125 to 0.078125
- gain_attn: bfloat16 [2048], P(('rows', 'seq')), may hold values from 0.5 to 1.5
- gain_query: bfloat16 [64], replicated, may hold values from 0.099609375 to 1.8984375
- gain_key: bfloat16 [64], replicated, may hold values from 0.099609375 to 1.8984375
- gain_ffn: bfloat16 [2048], P(('rows', 'seq')), may hold values from 0.5 to 1.5
Outputs:
- output: bfloat16 [8, 1024, 2048], P('rows', 'seq')
- grad_inputs: float32 [8, 1024, 2048], P('rows', 'seq')
- grad_query: float32 [2048, 1280], P(('rows', 'seq'))
- grad_key: float32 [2048, 320], P(('rows', 'seq'))
- grad_value: float32 [2048, 320], P(('rows', 'seq'))
- grad_out: float32 [1280, 2048], P(('rows', 'seq'))
- grad_gate: float32 [2048, 6656], P('seq', 'rows')
- grad_up: float32 [2048, 6656], P('seq', 'rows')
- grad_down: float32 [6656, 2048], P('rows', 'seq')
- grad_gain_attn: float32 [2048], P(('rows', 'seq'))
- grad_gain_query: float32 [64], replicated
- grad_gain_key: float32 [64], replicated
- grad_gain_ffn: float32 [2048], P(('rows', 'seq'))
Inputs may be any that keep to these rules, and one draw needn't show every extreme that they name: `segment_ids`: within a packed row the ids never fall, start at 0, and every row holds exactly 4 documents of one token or more. Inside a document the positions rise by one from token to token; each document starts at its own position.
All inputs are finite; a program needn't handle non-finite values.
Results may differ from a plain program's by a relative error of at most 0.02.
Values may be sent and summed in bfloat16 or wider, within the bound.
No kernel may reach another device: no remote copies, remote signals or barrier semaphores. Data moves between devices by JAX's collectives and lax.ppermute only.
A program may use at most 256 MiB of HBM per device.

v0:
```python
import jax
import jax.numpy as jnp
from jax import lax
from jax.sharding import PartitionSpec as P

norm_eps = 1e-06
masked_score = -1e30


def rms_apply(values, gain_vec):
    row_scale = lax.rsqrt(jnp.mean(values * values, axis=-1, keepdims=True) + norm_eps)
    return values * row_scale * gain_vec


def rms_back(values, gain_vec, grad_in):
    row_scale = lax.rsqrt(jnp.mean(values * values, axis=-1, keepdims=True) + norm_eps)
    weighted = grad_in * gain_vec
    inner_sum = jnp.sum(weighted * values, axis=-1, keepdims=True)
    grad_values = (
        row_scale * weighted
        - values * (row_scale * row_scale * row_scale) * inner_sum / values.shape[-1]
    )
    return (grad_values, grad_in * values * row_scale)


def rotary_tables(positions, head_dim):
    half_dim = head_dim // 2
    frequencies = 10000.0 ** (-2.0 * jnp.arange(half_dim).astype(jnp.float32) / head_dim)
    angles = positions.astype(jnp.float32)[..., None] * frequencies
    angles = jnp.concatenate([angles, angles], axis=-1)
    return (jnp.cos(angles), jnp.sin(angles))


def rotate(values, cosine, sine):
    half_dim = values.shape[-1] // 2
    turned = jnp.concatenate([-values[..., half_dim:], values[..., :half_dim]], axis=-1)
    return values * cosine + turned * sine


def rotate_back(grad_in, cosine, sine):
    half_dim = grad_in.shape[-1] // 2
    moved_part = grad_in * sine
    turned = jnp.concatenate([moved_part[..., half_dim:], -moved_part[..., :half_dim]], axis=-1)
    return grad_in * cosine + turned


def times_transposed(left, right):
    return lax.dot_general(
        left, right, (((1,), (1,)), ((), ())), preferred_element_type=jnp.float32
    )


def transposed_times(left, right):
    return lax.dot_general(
        left, right, (((0,), (0,)), ((), ())), preferred_element_type=jnp.float32
    )


def local(
    inputs,
    cotangent,
    positions,
    segment_ids,
    w_query,
    w_key,
    w_value,
    w_out,
    w_gate,
    w_up,
    w_down,
    gain_attn,
    gain_query,
    gain_key,
    gain_ffn,
):
    rows_here, seg_tok, feature_count = inputs.shape
    tokens_here = rows_here * seg_tok
    head_dim = gain_query.shape[0]
    heads_query = w_query.shape[1] // head_dim
    heads_kv = w_key.shape[1] // head_dim
    grouping = heads_query // heads_kv
    row_len = seg_tok * lax.axis_size("seq")
    key_block = min(512, row_len)
    block_total = row_len // key_block
    score_scale = head_dim ** (-0.5)
    seq_place = lax.axis_index("seq")
    query_full, key_full, value_full, out_full, attn_gain_full, ffn_gain_full = (
        lax.all_gather(w_query, ("rows", "seq"), axis=0, tiled=True),
        lax.all_gather(w_key, ("rows", "seq"), axis=0, tiled=True),
        lax.all_gather(w_value, ("rows", "seq"), axis=0, tiled=True),
        lax.all_gather(w_out, ("rows", "seq"), axis=0, tiled=True),
        lax.all_gather(gain_attn, ("rows", "seq"), axis=0, tiled=True),
        lax.all_gather(gain_ffn, ("rows", "seq"), axis=0, tiled=True),
    )
    residual = inputs.astype(jnp.float32).reshape(tokens_here, feature_count)
    normed = rms_apply(residual, attn_gain_full.astype(jnp.float32)).astype(jnp.bfloat16)
    query_pre = jnp.dot(normed, query_full, preferred_element_type=jnp.float32)
    key_pre = jnp.dot(normed, key_full, preferred_element_type=jnp.float32)
    value_pre = jnp.dot(normed, value_full, preferred_element_type=jnp.float32)
    cosine, sine = rotary_tables(positions.reshape(tokens_here), head_dim)
    cosine = cosine[:, None, :]
    sine = sine[:, None, :]
    query_heads = query_pre.reshape(tokens_here, heads_query, head_dim)
    key_heads = key_pre.reshape(tokens_here, heads_kv, head_dim)
    gain_q = gain_query.astype(jnp.float32)
    gain_k = gain_key.astype(jnp.float32)
    query_b = rotate(rms_apply(query_heads, gain_q), cosine, sine).astype(jnp.bfloat16)
    query_b = query_b.reshape(rows_here, seg_tok, heads_kv, grouping, head_dim)
    key_b = rotate(rms_apply(key_heads, gain_k), cosine, sine).astype(jnp.bfloat16)
    key_b = key_b.reshape(rows_here, seg_tok, heads_kv * head_dim)
    value_b = value_pre.astype(jnp.bfloat16).reshape(rows_here, seg_tok, heads_kv * head_dim)
    seg_float = segment_ids.astype(jnp.bfloat16)
    keys_all, values_all, seg_keys = (
        lax.all_gather(key_b, "seq", axis=1, tiled=True),
        lax.all_gather(value_b, "seq", axis=1, tiled=True),
        lax.all_gather(seg_float, "seq", axis=1, tiled=True),
    )
    seg_query = segment_ids.astype(jnp.float32)
    query_spots = seq_place * seg_tok + jnp.arange(seg_tok, dtype=jnp.int32)
    stat_shape = (rows_here, heads_kv, grouping, seg_tok)

    def block_keys(block_start):
        keys_blk = lax.dynamic_slice_in_dim(keys_all, block_start, key_block, 1)
        values_blk = lax.dynamic_slice_in_dim(values_all, block_start, key_block, 1)
        shape_blk = (rows_here, key_block, heads_kv, head_dim)
        return (keys_blk.reshape(shape_blk), values_blk.reshape(shape_blk))

    def block_scores(block_start, keys_blk):
        scores = (
            jnp.einsum("rqhgd,rkhd->rhgqk", query_b, keys_blk, preferred_element_type=jnp.float32)
            * score_scale
        )
        key_spots = block_start + jnp.arange(key_block, dtype=jnp.int32)
        seg_blk = lax.dynamic_slice_in_dim(seg_keys, block_start, key_block, 1).astype(jnp.float32)
        allowed = (key_spots[None, None, :] <= query_spots[None, :, None]) & (
            seg_blk[:, None, :] == seg_query[:, :, None]
        )
        return jnp.where(allowed[:, None, None], scores, masked_score)

    def stats_step(block_index, state_in):
        running_max, running_sum = state_in
        block_start = block_index * key_block
        keys_blk, values_blk = block_keys(block_start)
        scores = block_scores(block_start, keys_blk)
        new_max = jnp.maximum(running_max, jnp.max(scores, axis=-1))
        running_sum = running_sum * jnp.exp(running_max - new_max) + jnp.sum(
            jnp.exp(scores - new_max[..., None]), axis=-1
        )
        return (new_max, running_sum)

    running_max, running_sum = lax.fori_loop(
        0,
        block_total,
        stats_step,
        (jnp.full(stat_shape, masked_score, jnp.float32), jnp.zeros(stat_shape, jnp.float32)),
    )
    log_total = running_max + jnp.log(running_sum)

    def output_step(block_index, accum_in):
        block_start = block_index * key_block
        keys_blk, values_blk = block_keys(block_start)
        prob_blk = jnp.exp(block_scores(block_start, keys_blk) - log_total[..., None]).astype(
            jnp.bfloat16
        )
        return accum_in + jnp.einsum(
            "rhgqk,rkhd->rqhgd", prob_blk, values_blk, preferred_element_type=jnp.float32
        )

    attended = lax.fori_loop(
        0,
        block_total,
        output_step,
        jnp.zeros((rows_here, seg_tok, heads_kv, grouping, head_dim), jnp.float32),
    )
    attended_b = attended.reshape(tokens_here, heads_query * head_dim).astype(jnp.bfloat16)
    middle = residual + jnp.dot(attended_b, out_full, preferred_element_type=jnp.float32)
    gate_loc, up_loc, down_loc = (
        lax.all_gather(w_gate, "seq", axis=0, tiled=True),
        lax.all_gather(w_up, "seq", axis=0, tiled=True),
        lax.all_gather(w_down, "seq", axis=1, tiled=True),
    )
    ffn_in = rms_apply(middle, ffn_gain_full.astype(jnp.float32)).astype(jnp.bfloat16)
    grad_top_b = cotangent.reshape(tokens_here, feature_count)
    ffn_all, cot_all = (
        lax.all_gather(ffn_in, "rows", axis=0, tiled=True),
        lax.all_gather(grad_top_b, "rows", axis=0, tiled=True),
    )
    gate_val = jnp.dot(ffn_all, gate_loc, preferred_element_type=jnp.float32)
    up_val = jnp.dot(ffn_all, up_loc, preferred_element_type=jnp.float32)
    hidden_b = (jax.nn.silu(gate_val) * up_val).astype(jnp.bfloat16)
    down_terms = jnp.dot(hidden_b, down_loc, preferred_element_type=jnp.float32)
    down_mine = lax.psum_scatter(
        down_terms.astype(jnp.bfloat16), "rows", scatter_dimension=0, tiled=True
    ).astype(jnp.float32)
    output = middle + down_mine
    output_b = output.astype(jnp.bfloat16).reshape(rows_here, seg_tok, feature_count)
    gate_back, up_back, down_back = (
        lax.all_gather(w_gate, "seq", axis=0, tiled=True),
        lax.all_gather(w_up, "seq", axis=0, tiled=True),
        lax.all_gather(w_down, "seq", axis=1, tiled=True),
    )
    query_back, key_back, value_back, out_back, attn_gain_back, ffn_gain_back = (
        lax.all_gather(w_query, ("rows", "seq"), axis=0, tiled=True),
        lax.all_gather(w_key, ("rows", "seq"), axis=0, tiled=True),
        lax.all_gather(w_value, ("rows", "seq"), axis=0, tiled=True),
        lax.all_gather(w_out, ("rows", "seq"), axis=0, tiled=True),
        lax.all_gather(gain_attn, ("rows", "seq"), axis=0, tiled=True),
        lax.all_gather(gain_ffn, ("rows", "seq"), axis=0, tiled=True),
    )
    grad_hidden = times_transposed(cot_all, down_back)
    grad_down_w = transposed_times(hidden_b, cot_all)
    sigma_gate = jax.nn.sigmoid(gate_val)
    grad_gate_b = (
        grad_hidden * up_val * sigma_gate * (1.0 + gate_val * (1.0 - sigma_gate))
    ).astype(jnp.bfloat16)
    grad_up_b = (grad_hidden * gate_val * sigma_gate).astype(jnp.bfloat16)
    ffn_in_terms = times_transposed(grad_gate_b, gate_back) + times_transposed(grad_up_b, up_back)
    grad_gate_w = transposed_times(ffn_all, grad_gate_b)
    grad_up_w = transposed_times(ffn_all, grad_up_b)
    ffn_sums = (
        lax.psum_scatter(
            grad_gate_w.astype(jnp.bfloat16), "seq", scatter_dimension=0, tiled=True
        ).astype(jnp.float32),
        lax.psum_scatter(
            grad_up_w.astype(jnp.bfloat16), "seq", scatter_dimension=0, tiled=True
        ).astype(jnp.float32),
        lax.psum_scatter(
            grad_down_w.astype(jnp.bfloat16), "seq", scatter_dimension=1, tiled=True
        ).astype(jnp.float32),
    )
    grad_ffn_in = lax.psum_scatter(
        ffn_in_terms.astype(jnp.bfloat16), "rows", scatter_dimension=0, tiled=True
    ).astype(jnp.float32)
    grad_mid_ffn, gain_ffn_rows = rms_back(middle, ffn_gain_back.astype(jnp.float32), grad_ffn_in)
    grad_middle = grad_top_b.astype(jnp.float32) + grad_mid_ffn
    grad_gain_ffn = jnp.sum(gain_ffn_rows, axis=0)
    grad_branch = grad_middle.astype(jnp.bfloat16)
    grad_out_w = transposed_times(attended_b, grad_branch)
    grad_attended = times_transposed(grad_branch, out_back).astype(jnp.bfloat16)
    grad_att = grad_attended.reshape(rows_here, seg_tok, heads_kv, grouping, head_dim)

    def delta_step(block_index, accum_in):
        block_start = block_index * key_block
        keys_blk, values_blk = block_keys(block_start)
        prob_blk = jnp.exp(block_scores(block_start, keys_blk) - log_total[..., None])
        grad_probs = jnp.einsum(
            "rqhgd,rkhd->rhgqk", grad_att, values_blk, preferred_element_type=jnp.float32
        )
        return accum_in + jnp.sum(prob_blk * grad_probs, axis=-1)

    delta_row = lax.fori_loop(0, block_total, delta_step, jnp.zeros(stat_shape, jnp.float32))
    kv_shape = (rows_here, row_len, heads_kv, head_dim)

    def grad_step(block_index, state_in):
        grad_query_acc, grad_keys_acc, grad_values_acc = state_in
        block_start = block_index * key_block
        keys_blk, values_blk = block_keys(block_start)
        prob_blk = jnp.exp(block_scores(block_start, keys_blk) - log_total[..., None])
        grad_probs = jnp.einsum(
            "rqhgd,rkhd->rhgqk", grad_att, values_blk, preferred_element_type=jnp.float32
        )
        grad_scores = (prob_blk * (grad_probs - delta_row[..., None])).astype(jnp.bfloat16)
        grad_query_acc = (
            grad_query_acc
            + jnp.einsum(
                "rhgqk,rkhd->rqhgd", grad_scores, keys_blk, preferred_element_type=jnp.float32
            )
            * score_scale
        )
        key_part = (
            jnp.einsum(
                "rhgqk,rqhgd->rkhd", grad_scores, query_b, preferred_element_type=jnp.float32
            )
            * score_scale
        )
        value_part = jnp.einsum(
            "rhgqk,rqhgd->rkhd",
            prob_blk.astype(jnp.bfloat16),
            grad_att,
            preferred_element_type=jnp.float32,
        )
        grad_keys_acc = lax.dynamic_update_slice_in_dim(grad_keys_acc, key_part, block_start, 1)
        grad_values_acc = lax.dynamic_update_slice_in_dim(
            grad_values_acc, value_part, block_start, 1
        )
        return (grad_query_acc, grad_keys_acc, grad_values_acc)

    grad_query_rot, grad_keys_full, grad_values_full = lax.fori_loop(
        0,
        block_total,
        grad_step,
        (
            jnp.zeros((rows_here, seg_tok, heads_kv, grouping, head_dim), jnp.float32),
            jnp.zeros(kv_shape, jnp.float32),
            jnp.zeros(kv_shape, jnp.float32),
        ),
    )
    grad_keys_mine, grad_values_mine = (
        lax.psum_scatter(
            grad_keys_full.astype(jnp.bfloat16), "seq", scatter_dimension=1, tiled=True
        ).astype(jnp.float32),
        lax.psum_scatter(
            grad_values_full.astype(jnp.bfloat16), "seq", scatter_dimension=1, tiled=True
        ).astype(jnp.float32),
    )
    grad_value_b = grad_values_mine.reshape(tokens_here, heads_kv * head_dim).astype(jnp.bfloat16)
    grad_key_norm = rotate_back(
        grad_keys_mine.reshape(tokens_here, heads_kv, head_dim), cosine, sine
    )
    grad_key_pre, gain_k_rows = rms_back(key_heads, gain_k, grad_key_norm)
    grad_key_b = grad_key_pre.reshape(tokens_here, heads_kv * head_dim).astype(jnp.bfloat16)
    grad_query_norm = rotate_back(
        grad_query_rot.reshape(tokens_here, heads_query, head_dim), cosine, sine
    )
    grad_query_pre, gain_q_rows = rms_back(query_heads, gain_q, grad_query_norm)
    grad_query_b = grad_query_pre.reshape(tokens_here, heads_query * head_dim).astype(jnp.bfloat16)
    gain_sums = lax.psum(
        (jnp.sum(gain_q_rows, axis=(0, 1)), jnp.sum(gain_k_rows, axis=(0, 1))), ("rows", "seq")
    )
    grad_query_w = transposed_times(normed, grad_query_b)
    grad_key_w = transposed_times(normed, grad_key_b)
    grad_value_w = transposed_times(normed, grad_value_b)
    grad_normed = (
        times_transposed(grad_query_b, query_back)
        + times_transposed(grad_key_b, key_back)
        + times_transposed(grad_value_b, value_back)
    )
    grad_resid_attn, gain_attn_rows = rms_back(
        residual, attn_gain_back.astype(jnp.float32), grad_normed
    )
    grad_inputs = (grad_middle + grad_resid_attn).reshape(rows_here, seg_tok, feature_count)
    grad_gain_attn = jnp.sum(gain_attn_rows, axis=0)
    attn_sums = (
        lax.psum_scatter(grad_query_w, ("rows", "seq"), scatter_dimension=0, tiled=True),
        lax.psum_scatter(grad_key_w, ("rows", "seq"), scatter_dimension=0, tiled=True),
        lax.psum_scatter(grad_value_w, ("rows", "seq"), scatter_dimension=0, tiled=True),
        lax.psum_scatter(grad_out_w, ("rows", "seq"), scatter_dimension=0, tiled=True),
        lax.psum_scatter(grad_gain_attn, ("rows", "seq"), scatter_dimension=0, tiled=True),
        lax.psum_scatter(grad_gain_ffn, ("rows", "seq"), scatter_dimension=0, tiled=True),
    )
    return (
        output_b,
        grad_inputs,
        attn_sums[0],
        attn_sums[1],
        attn_sums[2],
        attn_sums[3],
        ffn_sums[0],
        ffn_sums[1],
        ffn_sums[2],
        attn_sums[4],
        gain_sums[0],
        gain_sums[1],
        attn_sums[5],
    )


def solution(mesh):
    return jax.shard_map(
        local,
        mesh=mesh,
        in_specs=(
            P("rows", "seq", None),
            P("rows", "seq", None),
            P("rows", "seq"),
            P("rows", "seq"),
            P(("rows", "seq"), None),
            P(("rows", "seq"), None),
            P(("rows", "seq"), None),
            P(("rows", "seq"), None),
            P("seq", "rows"),
            P("seq", "rows"),
            P("rows", "seq"),
            P(("rows", "seq")),
            P(),
            P(),
            P(("rows", "seq")),
        ),
        out_specs=(
            P("rows", "seq", None),
            P("rows", "seq", None),
            P(("rows", "seq"), None),
            P(("rows", "seq"), None),
            P(("rows", "seq"), None),
            P(("rows", "seq"), None),
            P("seq", "rows"),
            P("seq", "rows"),
            P("rows", "seq"),
            P(("rows", "seq")),
            P(),
            P(),
            P(("rows", "seq")),
        ),
        check_vma=False,
    )
```

profile of v0, /device:TPU:0, one launch (start us, length us, event | category | flops | bytes accessed | tf_op | source)
XLA Modules:
  0.0 2154.2 jit_solution(15456615657566478420)
XLA Ops:
  11.2 42.2 %all-reduce.5 = (bf16[2048]{0:T(1024)(128)(2,1)S(1)}, bf16[2048]{0:T(1024)(128)(2,1)S(1)}) all-reduce(bf16[2048]{0:T(1024)(128)(2,1)S(1)} %dynamic-update-slice, bf16[2048]{0:T(1024)(128)(2,1)S(1)} %dynamic-update-slice.1), channel_id=1, replica_groups=mesh['rows'=4,'seq'=8] {'rows','seq'}, use_global_device_ids=true, to_apply=%add | all-reduce | flops 4096 | bytes 16384
  56.9 11.9 all-gather.16.cloned.1.call-done
  76.3 49.5 %all-gather.12.cloned.1.call-done = bf16[2048,320]{1,0:T(8,128)(2,1)} async-done(((bf16[64,320]{1,0:T(8,128)(2,1)}), bf16[2048,320]{1,0:T(8,128)(2,1)}) %all-gather.12.cloned.1.call-update) | async-done | bytes 1310736 | tf_op jit(solution)/shard_map/all_gather | solution.py:90
  130.3 19.4 all_gather.54
  149.8 43.1 %all-gather.20.cloned.1.call-done = bf16[2048,1280]{1,0:T(8,128)(2,1)} async-done(((bf16[64,1280]{1,0:T(8,128)(2,1)}), bf16[2048,1280]{1,0:T(8,128)(2,1)}) %all-gather.20.cloned.1.call-update) | async-done | bytes 5242896 | tf_op jit(solution)/shard_map/all_gather | solution.py:88
  192.9 7.9 copy.69
  207.1 29.4 %all-gather.18.cloned.1.call-done = bf16[2,1024,320]{1,2,0:T(8,128)(2,1)} async-done(((bf16[2,128,320]{1,2,0:T(8,128)(2,1)}), bf16[2,1024,320]{1,2,0:T(8,128)(2,1)}) %all-gather.18.cloned.1.call-update) | async-done | bytes 1310736 | tf_op jit(solution)/shard_map/all_gather | solution.py:114
  236.5 27.0 %while.62 = (s32[]{:T(128)}, f32[2,5,4,128]{3,2,1,0:T(4,128)S(1)}, f32[2,5,4,128]{3,2,1,0:T(4,128)S(1)}, bf16[2,1024]{1,0:T(2,128)(2,1)S(1)}, f32[2,128]{1,0:T(2...) while((s32[]{:T(128)}, f32[2,5,4,128]{3,2,1,0:T(4,128)S(1)}, ...), condition=%wide.region_6.7_spmd.clone, body=%wide.region_3.6_spmd.clone.sunk | while | flops 354249344 | bytes 24400060 | solution.py:151
  243.6 6.5 exponential_reduce_fusion.2
  257.2 6.3 exponential_reduce_fusion.2
  263.6 16.4 all-gather.14.cloned.1.call-done
  280.0 13.8 while.63
  295.9 50.9 %all-gather.22.cloned.1.call-done = bf16[1280,2048]{1,0:T(8,128)(2,1)} async-done(((bf16[40,2048]{1,0:T(8,128)(2,1)}), bf16[1280,2048]{1,0:T(8,128)(2,1)}) %all-gather.22.cloned.1.call-update) | async-done | bytes 5242896 | tf_op jit(solution)/shard_map/all_gather | solution.py:91
  355.5 97.8 %all-gather.26.cloned.1.call-done = bf16[2048,1664]{1,0:T(8,128)(2,1)} async-done(((bf16[256,1664]{1,0:T(8,128)(2,1)}), bf16[2048,1664]{1,0:T(8,128)(2,1)}) %all-gather.26.cloned.1.call-update) | async-done | bytes 6815760 | tf_op jit(solution)/shard_map/all_gather | solution.py:178
  453.4 34.8 %all-gather.24.cloned.1.call-done = bf16[1024,2048]{1,0:T(8,128)(2,1)} async-done(((bf16[256,2048]{1,0:T(8,128)(2,1)}), bf16[1024,2048]{1,0:T(8,128)(2,1)}) %all-gather.24.cloned.1.call-update) | async-done | bytes 4194320 | tf_op jit(solution)/shard_map/all_gather | solution.py:185
  488.2 13.4 fusion.110
  501.6 94.4 %all-gather.28.cloned.1.call-done = bf16[2048,1664]{1,0:T(8,128)(2,1)} async-done(((bf16[256,1664]{1,0:T(8,128)(2,1)}), bf16[2048,1664]{1,0:T(8,128)(2,1)}) %all-gather.28.cloned.1.call-update) | async-done | bytes 6815760 | tf_op jit(solution)/shard_map/all_gather | solution.py:179
  596.0 13.2 fusion.111
  609.2 20.9 all-gather.32.cloned.1.call-done
  630.1 108.4 %all-gather.30.cloned.1.call-done = bf16[1664,2048]{1,0:T(8,128)(2,1)} async-done(((bf16[1664,256]{1,0:T(8,128)(2,1)}), bf16[1664,2048]{1,0:T(8,128)(2,1)}) %all-gather.30.cloned.1.call-update) | async-done | bytes 6815760 | tf_op jit(solution)/shard_map/all_gather | solution.py:180
  738.5 19.0 multiply_convert_fusion
  757.5 11.6 fusion.112
  769.1 9.4 add_convert_fusion
  778.6 12.3 convolution_convert_fusion.3
  790.9 30.4 %reduce-scatter.18.cloned.1.call-done = bf16[256,2048]{1,0:T(8,128)(2,1)} async-done(((bf16[1024,2048]{1,0:T(8,128)(2,1)}), bf16[256,2048]{1,0:T(8,128)(2,1)}) %reduce-scatter.18.cloned.1.call-update) | async-done | bytes 1048592 | tf_op jit(solution)/shard_map/reduce_scatter | solution.py:231
  823.8 44.7 %reduce-scatter.16.cloned.1.call-done = bf16[256,2048]{1,0:T(8,128)(2,1)} async-done(((bf16[1024,2048]{1,0:T(8,128)(2,1)}), bf16[256,2048]{1,0:T(8,128)(2,1)}) %reduce-scatter.16.cloned.1.call-update) | async-done | bytes 1048592 | tf_op jit(solution)/shard_map/reduce_scatter | solution.py:192
  882.2 13.8 while.64
  898.5 48.0 %while.65 = (s32[]{:T(128)}, f32[2,128,5,4,64]{1,4,3,2,0:T(8,128)}, bf16[2,1024,5,64]{1,3,2,0:T(8,128)(2,1)}, bf16[2,1024,5,64]{1,3,2,0:T(8,128)(2,1)}, bf16[2,1...) while((s32[]{:T(128)}, f32[2,128,5,4,64]{1,4,3,2,0:T(8,128)}, ...), condition=%wide.region_17.18_spmd.clone, body=%wide.region_16.17_spmd.clone.sunk | while | flops 1705576064 | bytes 123154720 | solution.py:288
  915.0 7.3 fusion.229
  939.2 7.3 fusion.229
  946.5 6.0 copy.94
  952.4 6.2 reshape.515
  958.7 6.0 copy.96
  964.7 6.2 reshape.517
  971.0 11.4 convolution_convert_fusion.2
  984.4 11.4 convolution_convert_fusion.1
  997.8 12.4 convolution_convert_fusion
  1010.3 12.8 reduce-scatter.34.cloned.1.call-done
  1028.2 61.6 %reduce-scatter.36.cloned.1.call-done = bf16[128,640]{1,0:T(8,128)(2,1)} async-done(((bf16[1024,640]{1,0:T(8,128)(2,1)}), bf16[128,640]{1,0:T(8,128)(2,1)}) %reduce-scatter.36.cloned.1.call-update) | async-done | bytes 163856
  1094.9 7.2 fusion.83
  1125.2 42.9 %all-reduce.4 = (f32[2048]{0:T(1024)S(1)}, f32[64]{0:T(128)}, f32[64]{0:T(128)}, f32[2048]{0:T(1024)S(1)}) all-reduce(f32[2048]{0:T(1024)S(1)} %get-tuple-element.965, f32[64]{0:T(128)S(1)} %get-tuple-element.1055, f32[64]{0:T(128)S(1)} %get-tuple-element.1053, ...), channel_id=13, replica_groups=mesh['rows'=4,'seq'=8] {'rows','seq'}, use_global_device_ids=true, to_apply=%region_31.32.clone | all-reduce | flops 4224 | bytes 33792
  1172.8 45.8 %reduce-scatter.28.cloned.1.call-done = bf16[256,1664]{1,0:T(8,128)(2,1)} async-done(((bf16[2048,1664]{1,0:T(8,128)(2,1)}), bf16[256,1664]{1,0:T(8,128)(2,1)}) %reduce-scatter.28.cloned.1.call-update) | async-done | bytes 851984 | tf_op jit(solution)/shard_map/reduce_scatter | solution.py:221
  1221.1 125.5 %reduce-scatter.30.cloned.1.call-done = bf16[256,1664]{1,0:T(8,128)(2,1)} async-done(((bf16[2048,1664]{1,0:T(8,128)(2,1)}), bf16[256,1664]{1,0:T(8,128)(2,1)}) %reduce-scatter.30.cloned.1.call-update) | async-done | bytes 851984 | tf_op jit(solution)/shard_map/reduce_scatter | solution.py:224
  1349.1 125.9 %reduce-scatter.32.cloned.1.call-done = bf16[1664,256]{1,0:T(8,128)(2,1)} async-done(((bf16[1664,2048]{1,0:T(8,128)(2,1)}), bf16[1664,256]{1,0:T(8,128)(2,1)}) %reduce-scatter.32.cloned.1.call-update) | async-done | bytes 851984 | tf_op jit(solution)/shard_map/reduce_scatter | solution.py:227
  1477.4 104.1 %reduce-scatter.22.cloned.1.call-done = f32[64,320]{1,0:T(8,128)} async-done(((f32[2048,320]{1,0:T(8,128)}), f32[64,320]{1,0:T(8,128)}) %reduce-scatter.22.cloned.1.call-update) | async-done | bytes 81936 | tf_op jit(solution)/shard_map/reduce_scatter | solution.py:335
  1581.6 106.3 %reduce-scatter.24.cloned.1.call-done = f32[64,320]{1,0:T(8,128)} async-done(((f32[2048,320]{1,0:T(8,128)}), f32[64,320]{1,0:T(8,128)}) %reduce-scatter.24.cloned.1.call-update) | async-done | bytes 81936 | tf_op jit(solution)/shard_map/reduce_scatter | solution.py:336
  1687.8 229.6 %reduce-scatter.26.cloned.1.call-done = f32[40,2048]{1,0:T(8,128)} async-done(((f32[1280,2048]{1,0:T(8,128)}), f32[40,2048]{1,0:T(8,128)}) %reduce-scatter.26.cloned.1.call-update) | async-done | bytes 327696 | tf_op jit(solution)/shard_map/reduce_scatter | solution.py:337
  1917.5 229.7 %reduce-scatter.20.cloned.1.call-done = f32[64,1280]{1,0:T(8,128)} async-done(((f32[2048,1280]{1,0:T(8,128)}), f32[64,1280]{1,0:T(8,128)}) %reduce-scatter.20.cloned.1.call-update) | async-done | bytes 327696 | tf_op jit(solution)/shard_map/reduce_scatter | solution.py:334
  (295 shorter events, 178.8 us)
Async XLA Ops:
  7.2 49.4 %copy-start.4 = (bf16[2,128,2048]{2,1,0:T(8,128)(2,1)S(1)}, bf16[2,128,2048]{2,1,0:T(8,128)(2,1)}, u32[]{:S(2)}) copy-start(bf16[2,128,2048]{2,1,0:T(8,128)(2,1)} %param.23) | copy-start | bytes 3145732
  7.2 61.6 %all-gather.16.cloned.1.call-start = ((), (), s32[]{:S(2)}) async-start(), calls=%async_computation.13 | async-start | bytes 1622016 | tf_op jit(solution)/shard_map/all_gather | solution.py:89
  7.9 117.8 %all-gather.12.cloned.1.call-start = ((), (), s32[]{:S(2)}) async-start(), calls=%async_computation.11 | async-start | bytes 1622016 | tf_op jit(solution)/shard_map/all_gather | solution.py:90
  8.7 184.2 %all-gather.20.cloned.1.call-start = ((), (), s32[]{:S(2)}) async-start(), calls=%async_computation.15 | async-start | bytes 5406720 | tf_op jit(solution)/shard_map/all_gather | solution.py:88
  9.4 227.1 %all-gather.18.cloned.1.call-start = ((), (), s32[]{:S(2)}) async-start(), calls=%async_computation.14 | async-start | bytes 1474560 | tf_op jit(solution)/shard_map/all_gather | solution.py:114
  53.3 21.6 %copy-start.26 = (f32[2048]{0:T(1024)}, f32[2048]{0:T(1024)S(1)}, u32[]{:S(2)}) copy-start(f32[2048]{0:T(1024)S(1)} %convert_element_type.198) | copy-start | bytes 24580
  54.0 20.0 copy-start.37
  54.9 151.2 %copy-start.20 = (f32[256,64]{0,1:T(8,128)}, f32[256,64]{0,1:T(8,128)S(1)}, u32[]{:S(2)}) copy-start(f32[256,64]{0,1:T(8,128)S(1)} %get-tuple-element.1078) | copy-start | bytes 196612
  54.9 151.2 %copy-start.22 = (f32[256,64]{0,1:T(8,128)}, f32[256,64]{0,1:T(8,128)S(1)}, u32[]{:S(2)}) copy-start(f32[256,64]{0,1:T(8,128)S(1)} %get-tuple-element.1079) | copy-start | bytes 196612
  56.5 14.8 copy-start.34
  56.5 18.4 copy-start.32
  56.9 143.9 %copy-start.8 = (bf16[2,128,2048]{2,1,0:T(8,128)(2,1)}, bf16[2,128,2048]{2,1,0:T(8,128)(2,1)S(1)}, u32[]{:S(2)}) copy-start(bf16[2,128,2048]{2,1,0:T(8,128)(2,1)S(1)} %fusion.61) | copy-start | bytes 3145732
  74.9 205.1 %all-gather.14.cloned.1.call-start = ((), (), s32[]{:S(2)}) async-start(), calls=%async_computation.12 | async-start | bytes 1474560 | tf_op jit(solution)/shard_map/all_gather | solution.py:115
  76.3 54.0 %copy-start.43 = (bf16[64]{0:T(256)(128)(2,1)S(1)}, bf16[64]{0:T(256)(128)(2,1)}, u32[]{:S(2)}) copy-start(bf16[64]{0:T(256)(128)(2,1)} %param.35) | copy-start | bytes 388
  76.3 54.0 %copy-start.41 = (s32[2,128]{1,0:T(2,128)S(1)}, s32[2,128]{1,0:T(2,128)}, u32[]{:S(2)}) copy-start(s32[2,128]{1,0:T(2,128)} %param.26) | copy-start | bytes 3076
  128.8 217.9 %all-gather.22.cloned.1.call-start = ((), (), s32[]{:S(2)}) async-start(), calls=%async_computation.16 | async-start | bytes 5406720 | tf_op jit(solution)/shard_map/all_gather | solution.py:91
  129.4 324.0 %all-gather.26.cloned.1.call-start = ((), (), s32[]{:S(2)}) async-start(), calls=%async_computation.18 | async-start | bytes 7667712 | tf_op jit(solution)/shard_map/all_gather | solution.py:178
  130.2 358.0 %all-gather.24.cloned.1.call-start = ((), (), s32[]{:S(2)}) async-start(), calls=%async_computation.17 | async-start | bytes 5242880 | tf_op jit(solution)/shard_map/all_gather | solution.py:185
  130.3 75.9 %copy-start.39 = (f32[64]{0:T(128)}, f32[64]{0:T(128)S(1)}, u32[]{:S(2)}) copy-start(f32[64]{0:T(128)S(1)} %convert_element_type.210) | copy-start | bytes 772
  295.8 55.0 %copy-start.14 = (bf16[2,128,5,4,64]{1,0,4,3,2:T(2,128)(2,1)}, bf16[2,128,5,4,64]{1,0,4,3,2:T(2,128)(2,1)S(1)}, u32[]{:S(2)}) copy-start(bf16[2,128,5,4,64]{1,0,4,3,2:T(2,128)(2,1)S(1)} %copy.72) | copy-start | bytes 1966084
  353.4 242.6 %all-gather.28.cloned.1.call-start = ((), (), s32[]{:S(2)}) async-start(), calls=%async_computation.19 | async-start | bytes 7667712 | tf_op jit(solution)/shard_map/all_gather | solution.py:179
  354.2 275.9 %all-gather.32.cloned.1.call-start = ((), (), s32[]{:S(2)}) async-start(), calls=%async_computation.22 | async-start | bytes 5242880 | tf_op jit(solution)/shard_map/all_gather | solution.py:186
  354.8 383.7 %all-gather.30.cloned.1.call-start = ((), (), s32[]{:S(2)}) async-start(), calls=%async_computation.20 | async-start | bytes 7667712 | tf_op jit(solution)/shard_map/all_gather | solution.py:180
  355.5 465.8 %reduce-scatter.18.cloned.1.call-start = ((), (), s32[]{:S(2)}) async-start(), calls=%async_computation.23 | async-start | bytes 5242880 | tf_op jit(solution)/shard_map/reduce_scatter | solution.py:231
  757.5 11.6 copy-start.42
  757.5 11.6 copy-start.46
  778.5 90.0 %reduce-scatter.16.cloned.1.call-start = ((), (), s32[]{:S(2)}) async-start(), calls=%async_computation.21 | async-start | bytes 5242880 | tf_op jit(solution)/shard_map/reduce_scatter | solution.py:192
  790.8 30.5 %copy-start.7 = (f32[256,2048]{1,0:T(8,128)S(1)}, f32[256,2048]{1,0:T(8,128)}, u32[]{:S(2)}) copy-start(f32[256,2048]{1,0:T(8,128)} %copy-done.6) | copy-start | bytes 6291460
  790.9 232.3 %reduce-scatter.34.cloned.1.call-start = ((), (), s32[]{:S(2)}) async-start(), calls=%async_computation.31 | async-start | bytes 1474560
  877.6 4.6 copy-start.2
  901.6 3.9 copy-start.1
  958.7 131.0 %reduce-scatter.36.cloned.1.call-start = ((), (), s32[]{:S(2)}) async-start(), calls=%async_computation.32 | async-start | bytes 1474560
  964.7 6.3 copy-start.45
  971.0 247.7 %reduce-scatter.28.cloned.1.call-start = ((), (), s32[]{:S(2)}) async-start(), calls=%async_computation.28 | async-start | bytes 7667712 | tf_op jit(solution)/shard_map/reduce_scatter | solution.py:221
  982.5 364.2 %reduce-scatter.30.cloned.1.call-start = ((), (), s32[]{:S(2)}) async-start(), calls=%async_computation.29 | async-start | bytes 7667712 | tf_op jit(solution)/shard_map/reduce_scatter | solution.py:224
  995.8 479.1 %reduce-scatter.32.cloned.1.call-start = ((), (), s32[]{:S(2)}) async-start(), calls=%async_computation.30 | async-start | bytes 7667712 | tf_op jit(solution)/shard_map/reduce_scatter | solution.py:227
  1010.2 14.6 copy-start.23
  1010.2 14.6 copy-start.19
  1010.3 14.6 copy-start.21
  1010.3 14.6 copy-start.29
  1010.3 14.8 copy-start.36
  1010.3 14.8 copy-start.38
  1010.3 571.3 %reduce-scatter.22.cloned.1.call-start = ((), (), s32[]{:S(2)}) async-start(), calls=%async_computation.25 | async-start | bytes 3244032 | tf_op jit(solution)/shard_map/reduce_scatter | solution.py:335
  1028.1 659.7 %reduce-scatter.24.cloned.1.call-start = ((), (), s32[]{:S(2)}) async-start(), calls=%async_computation.26 | async-start | bytes 3244032 | tf_op jit(solution)/shard_map/reduce_scatter | solution.py:336
  1093.9 823.6 %reduce-scatter.26.cloned.1.call-start = ((), (), s32[]{:S(2)}) async-start(), calls=%async_computation.27 | async-start | bytes 10813440 | tf_op jit(solution)/shard_map/reduce_scatter | solution.py:337
  1102.2 1045.0 %reduce-scatter.20.cloned.1.call-start = ((), (), s32[]{:S(2)}) async-start(), calls=%async_computation.24 | async-start | bytes 10813440 | tf_op jit(solution)/shard_map/reduce_scatter | solution.py:334
  1116.8 4.2 copy-start.16
  1122.8 46.4 %copy-start.11 = (f32[256,2048]{1,0:T(8,128)S(1)}, f32[256,2048]{1,0:T(8,128)}, u32[]{:S(2)}) copy-start(f32[256,2048]{1,0:T(8,128)} %copy-done.10) | copy-start | bytes 6291460
  (24 other events, 37.7 us)
Sparse Core Ops, SparseCore 0:
  10.9 57.8 all-gather.15
  71.7 53.9 all-gather.11
  128.6 64.2 all-gather.19
  195.3 41.1 all-gather.17
  239.0 40.9 all-gather.13
  282.7 64.0 all-gather.21
  348.9 104.4 all-gather.25
  455.5 32.6 all-gather.23
  490.4 105.5 all-gather.27
  597.4 32.6 all-gather.31
  632.2 106.2 all-gather.29
  778.6 42.6 reduce-scatter.17
  824.0 44.4 reduce-scatter.15
  958.8 64.2 reduce-scatter.33
  1026.4 63.3 reduce-scatter.35
  1093.2 125.3 reduce-scatter.27
  1222.1 124.4 reduce-scatter.29
  1350.1 124.7 reduce-scatter.31
  1481.0 100.5 reduce-scatter.21
  1587.4 100.3 reduce-scatter.23
  1690.7 226.6 reduce-scatter.25
  1920.3 226.7 reduce-scatter.19
where the time goes:
time: 2160 us; the launch traced here: 2150 us
  waiting for transfers between devices  1680 us (78%)
  matrix products  226 us (10%)
  blocking collectives  104 us (5%)
  local copies, waits for them, and re-layouts  83.1 us (4%)
  other arithmetic  44.3 us (2%)
    reduce_scatter x1, waiting for transfers between devices, local(): lax.psum_scatter(grad_query_w, ('rows', 'seq'), scatter_dimension=0, tile...  230 us
    reduce_scatter x1, waiting for transfers between devices, local(): lax.psum_scatter(grad_out_w, ('rows', 'seq'), scatter_dimension=0, tiled=...  230 us
    reduce_scatter x1, waiting for transfers between devices, local(): lax.psum_scatter(grad_down_w.astype(jnp.bfloat16), 'seq', scatter_dimensi...  126 us
    reduce_scatter x1, waiting for transfers between devices, local(): lax.psum_scatter(grad_up_w.astype(jnp.bfloat16), 'seq', scatter_dimension...  126 us
    all_gather x1, waiting for transfers between devices, local(): lax.all_gather(w_down, 'seq', axis=1, tiled=True)  108 us
    reduce_scatter x1, waiting for transfers between devices, local(): lax.psum_scatter(grad_value_w, ('rows', 'seq'), scatter_dimension=0, tile...  106 us
    reduce_scatter x1, waiting for transfers between devices, local(): lax.psum_scatter(grad_key_w, ('rows', 'seq'), scatter_dimension=0, tiled=...  104 us
    all_gather x1, waiting for transfers between devices, local(): lax.all_gather(w_gate, 'seq', axis=0, tiled=True)  97.8 us
  transfers between devices with their start and end apart: 22, of which 22 were waited for; matrix products, arithmetic and copies ran while one was open for 10% of the time, Pallas kernels for 0%

commit v1 on v0

--- a/solution.py
+++ b/solution.py
@@ -54,6 +54,155 @@
     return lax.dot_general(
         left, right, (((0,), (0,)), ((), ())), preferred_element_type=jnp.float32
     )
+
+
+def swap(values, axis_name, bit):
+    count = lax.axis_size(axis_name)
+    return lax.ppermute(values, axis_name, [(i, i ^ bit) for i in range(count)])
+
+
+def ring(values, shift):
+    count = lax.axis_size("seq")
+    return lax.ppermute(values, "seq", [(i, (i + 2 * shift) % count) for i in range(count)])
+
+
+def core_swap(values):
+    return swap(values, "rows", 1)
+
+
+def x_swap(values):
+    return swap(values, "rows", 2)
+
+
+def y_swap(values):
+    return swap(values, "seq", 1)
+
+
+def sum_all(values):
+    for axis_name in ("rows", "seq"):
+        bit = 1
+        while bit < lax.axis_size(axis_name):
+            values = values + swap(values, axis_name, bit)
+            bit *= 2
+    return values
+
+
+def places():
+    row_place = lax.axis_index("rows")
+    seq_place = lax.axis_index("seq")
+    return (row_place // 2, row_place % 2, seq_place // 2, seq_place % 2)
+
+
+def in_order(first, other, bit, axis):
+    return jnp.where(
+        bit == 0, jnp.stack([first, other], axis=axis), jnp.stack([other, first], axis=axis)
+    )
+
+
+def ring_gather(values):
+    pieces = [values]
+    for _ in range(lax.axis_size("seq") // 2 - 1):
+        pieces.append(ring(pieces[-1], -1))
+    return pieces
+
+
+def ring_scatter(pieces):
+    count = len(pieces)
+    moving = None
+    for step in range(1, count):
+        block = pieces[count - step]
+        if moving is not None:
+            block = (block.astype(jnp.float32) + moving.astype(jnp.float32)).astype(jnp.bfloat16)
+        moving = ring(block, 1)
+    return pieces[0].astype(jnp.float32) + moving.astype(jnp.float32)
+
+
+def turn(values, start):
+    count = values.shape[0]
+    return lax.dynamic_slice_in_dim(jnp.concatenate([values, values], axis=0), start, count, 0)
+
+
+def turn_columns(values, start, width):
+    return lax.dynamic_slice_in_dim(
+        jnp.concatenate([values, values], axis=1), start * width, values.shape[1], 1
+    )
+
+
+def gather_weights(values, x_first):
+    x_at, core_at, z_at, y_at = places()
+    planes = lax.axis_size("seq") // 2
+    size, width = values.shape
+    block = turn(jnp.stack(ring_gather(values)), (planes - z_at) % planes)
+    if x_first:
+        other = x_swap(block)
+        block = in_order(block, other, x_at, 0)
+        other = y_swap(block)
+        block = in_order(block, other, y_at, 2)
+    else:
+        other = y_swap(block)
+        block = in_order(block, other, y_at, 1)
+        other = x_swap(block)
+        block = in_order(block, other, x_at, 0)
+    other = core_swap(block)
+    return in_order(block, other, core_at, 1).reshape(8 * planes * size, width)
+
+
+def pick(values, bit, axis):
+    return (
+        lax.dynamic_index_in_dim(values, bit, axis, keepdims=False),
+        lax.dynamic_index_in_dim(values, 1 - bit, axis, keepdims=False),
+    )
+
+
+def add_low(left, right):
+    return (left.astype(jnp.float32) + right.astype(jnp.float32)).astype(jnp.bfloat16)
+
+
+def scatter_weights(values, x_first):
+    x_at, core_at, z_at, y_at = places()
+    planes = lax.axis_size("seq") // 2
+    width = values.shape[1]
+    block = values.reshape(2, 2, planes, 2, -1, width)
+    keep, send = pick(block, core_at, 1)
+    block = add_low(keep, core_swap(send.astype(jnp.bfloat16)))
+    if x_first:
+        keep, send = pick(block, x_at, 0)
+        block = add_low(keep, x_swap(send))
+        keep, send = pick(block, y_at, 1)
+        block = add_low(keep, y_swap(send))
+    else:
+        keep, send = pick(block, y_at, 2)
+        block = add_low(keep, y_swap(send))
+        keep, send = pick(block, x_at, 0)
+        block = add_low(keep, x_swap(send))
+    block = turn(block, z_at)
+    return ring_scatter([block[t] for t in range(planes)])
+
+
+def gather_tokens(values):
+    half = values.shape[1] // 2
+    from_x = x_swap(values)
+    from_y = y_swap(values)
+    from_xy = jnp.concatenate([y_swap(from_x[:, :half]), x_swap(from_y[:, half:])], axis=1)
+    blocks = [values, from_x, from_y, from_xy]
+    return jnp.concatenate(blocks + [core_swap(block) for block in blocks], axis=0)
+
+
+def scatter_tokens(values):
+    count = values.shape[0] // 8
+    half = values.shape[1] // 2
+    near = values[: 4 * count]
+    far = core_swap(values[4 * count :].astype(jnp.bfloat16))
+    total = near.astype(jnp.float32) + far.astype(jnp.float32)
+    own, to_x, to_y, to_xy = [total[i * count : (i + 1) * count] for i in range(4)]
+    corner = to_xy.astype(jnp.bfloat16)
+    via_x = x_swap(corner[:, :half]).astype(jnp.float32)
+    via_y = y_swap(corner[:, half:]).astype(jnp.float32)
+    to_y = jnp.concatenate([to_y[:, :half] + via_x, to_y[:, half:]], axis=1)
+    to_x = jnp.concatenate([to_x[:, :half], to_x[:, half:] + via_y], axis=1)
+    from_x = x_swap(to_x.astype(jnp.bfloat16)).astype(jnp.float32)
+    from_y = y_swap(to_y.astype(jnp.bfloat16)).astype(jnp.float32)
+    return own + from_x + from_y
 
 
 def local(
@@ -84,19 +233,41 @@
     block_total = row_len // key_block
     score_scale = head_dim ** (-0.5)
     seq_place = lax.axis_index("seq")
-    query_full, key_full, value_full, out_full, attn_gain_full, ffn_gain_full = (
-        lax.all_gather(w_query, ("rows", "seq"), axis=0, tiled=True),
-        lax.all_gather(w_key, ("rows", "seq"), axis=0, tiled=True),
-        lax.all_gather(w_value, ("rows", "seq"), axis=0, tiled=True),
-        lax.all_gather(w_out, ("rows", "seq"), axis=0, tiled=True),
-        lax.all_gather(gain_attn, ("rows", "seq"), axis=0, tiled=True),
-        lax.all_gather(gain_ffn, ("rows", "seq"), axis=0, tiled=True),
+    x_at, core_at, z_at, y_at = places()
+    planes = lax.axis_size("seq") // 2
+    place = lax.axis_index("rows") * lax.axis_size("seq") + seq_place
+    gain_size = gain_attn.shape[0]
+    gains = jnp.zeros((2 * feature_count,), jnp.float32)
+    gains = lax.dynamic_update_slice_in_dim(
+        gains, gain_attn.astype(jnp.float32), place * gain_size, 0
+    )
+    gains = lax.dynamic_update_slice_in_dim(
+        gains, gain_ffn.astype(jnp.float32), feature_count + place * gain_size, 0
+    )
+    gains = sum_all(gains.reshape(-1, 128)).reshape(-1)
+    attn_gain_full = gains[:feature_count]
+    ffn_gain_full = gains[feature_count:]
+    width_q, width_k = w_query.shape[1], w_key.shape[1]
+    qkv_here = jnp.concatenate([w_query, w_key, w_value], axis=1)
+    qkv_cut = 1024
+    qkv_full = jnp.concatenate(
+        [
+            gather_weights(qkv_here[:, :qkv_cut], True),
+            gather_weights(qkv_here[:, qkv_cut:], False),
+        ],
+        axis=1,
+    )
+    out_cut = feature_count // 2
+    out_full = jnp.concatenate(
+        [gather_weights(w_out[:, :out_cut], True), gather_weights(w_out[:, out_cut:], False)],
+        axis=1,
     )
     residual = inputs.astype(jnp.float32).reshape(tokens_here, feature_count)
-    normed = rms_apply(residual, attn_gain_full.astype(jnp.float32)).astype(jnp.bfloat16)
-    query_pre = jnp.dot(normed, query_full, preferred_element_type=jnp.float32)
-    key_pre = jnp.dot(normed, key_full, preferred_element_type=jnp.float32)
-    value_pre = jnp.dot(normed, value_full, preferred_element_type=jnp.float32)
+    normed = rms_apply(residual, attn_gain_full).astype(jnp.bfloat16)
+    qkv_pre = jnp.dot(normed, qkv_full, preferred_element_type=jnp.float32)
+    query_pre = qkv_pre[:, :width_q]
+    key_pre = qkv_pre[:, width_q : width_q + width_k]
+    value_pre = qkv_pre[:, width_q + width_k :]
     cosine, sine = rotary_tables(positions.reshape(tokens_here), head_dim)
     cosine = cosine[:, None, :]
     sine = sine[:, None, :]
@@ -109,12 +280,22 @@
     key_b = rotate(rms_apply(key_heads, gain_k), cosine, sine).astype(jnp.bfloat16)
     key_b = key_b.reshape(rows_here, seg_tok, heads_kv * head_dim)
     value_b = value_pre.astype(jnp.bfloat16).reshape(rows_here, seg_tok, heads_kv * head_dim)
-    seg_float = segment_ids.astype(jnp.bfloat16)
-    keys_all, values_all, seg_keys = (
-        lax.all_gather(key_b, "seq", axis=1, tiled=True),
-        lax.all_gather(value_b, "seq", axis=1, tiled=True),
-        lax.all_gather(seg_float, "seq", axis=1, tiled=True),
-    )
+    kv_width = 2 * heads_kv * head_dim
+    kv_here = jnp.concatenate([key_b, value_b], axis=2)
+
+    def gather_seq(values):
+        pieces = ring_gather(values)
+        pieces = [in_order(piece, y_swap(piece), y_at, 0) for piece in pieces]
+        return turn(jnp.stack(pieces), (planes - z_at) % planes)
+
+    def row_of(values):
+        moved = jnp.moveaxis(values, 2, 0)
+        return moved.reshape((rows_here, row_len) + values.shape[4:])
+
+    kv_all = row_of(gather_seq(kv_here))
+    keys_all = kv_all[..., : kv_width // 2]
+    values_all = kv_all[..., kv_width // 2 :]
+    seg_keys = row_of(gather_seq(segment_ids))
     seg_query = segment_ids.astype(jnp.float32)
     query_spots = seq_place * seg_tok + jnp.arange(seg_tok, dtype=jnp.int32)
     stat_shape = (rows_here, heads_kv, grouping, seg_tok)
@@ -174,69 +355,73 @@
     )
     attended_b = attended.reshape(tokens_here, heads_query * head_dim).astype(jnp.bfloat16)
     middle = residual + jnp.dot(attended_b, out_full, preferred_element_type=jnp.float32)
-    gate_loc, up_loc, down_loc = (
-        lax.all_gather(w_gate, "seq", axis=0, tiled=True),
-        lax.all_gather(w_up, "seq", axis=0, tiled=True),
-        lax.all_gather(w_down, "seq", axis=1, tiled=True),
-    )
-    ffn_in = rms_apply(middle, ffn_gain_full.astype(jnp.float32)).astype(jnp.bfloat16)
+    ffn_here = w_gate.shape[1] // 2
+
+    def ffn_columns(weight):
+        first, second = weight[:, :ffn_here], weight[:, ffn_here:]
+        keep = jnp.where(y_at == 0, first, second)
+        send = jnp.where(y_at == 0, second, first)
+        block = in_order(keep, y_swap(send), y_at, 0).reshape(-1, ffn_here)
+        return jnp.concatenate(ring_gather(block), axis=0)
+
+    def ffn_rows(weight):
+        first, second = weight[:ffn_here], weight[ffn_here:]
+        keep = jnp.where(y_at == 0, first, second)
+        send = jnp.where(y_at == 0, second, first)
+        block = in_order(keep, y_swap(send), y_at, 1).reshape(ffn_here, -1)
+        return jnp.concatenate(ring_gather(block), axis=1)
+
+    gate_loc, up_loc, down_loc = ffn_columns(w_gate), ffn_columns(w_up), ffn_rows(w_down)
+    plane_width = feature_count // planes
+    ffn_in = rms_apply(middle, ffn_gain_full).astype(jnp.bfloat16)
     grad_top_b = cotangent.reshape(tokens_here, feature_count)
-    ffn_all, cot_all = (
-        lax.all_gather(ffn_in, "rows", axis=0, tiled=True),
-        lax.all_gather(grad_top_b, "rows", axis=0, tiled=True),
-    )
+    ffn_all = gather_tokens(turn_columns(ffn_in, z_at, plane_width))
+    cot_all = gather_tokens(turn_columns(grad_top_b, z_at, plane_width))
+    z_back = (planes - z_at) % planes
     gate_val = jnp.dot(ffn_all, gate_loc, preferred_element_type=jnp.float32)
     up_val = jnp.dot(ffn_all, up_loc, preferred_element_type=jnp.float32)
     hidden_b = (jax.nn.silu(gate_val) * up_val).astype(jnp.bfloat16)
     down_terms = jnp.dot(hidden_b, down_loc, preferred_element_type=jnp.float32)
-    down_mine = lax.psum_scatter(
-        down_terms.astype(jnp.bfloat16), "rows", scatter_dimension=0, tiled=True
-    ).astype(jnp.float32)
+    down_mine = turn_columns(scatter_tokens(down_terms), z_back, plane_width)
     output = middle + down_mine
     output_b = output.astype(jnp.bfloat16).reshape(rows_here, seg_tok, feature_count)
-    gate_back, up_back, down_back = (
-        lax.all_gather(w_gate, "seq", axis=0, tiled=True),
-        lax.all_gather(w_up, "seq", axis=0, tiled=True),
-        lax.all_gather(w_down, "seq", axis=1, tiled=True),
-    )
-    query_back, key_back, value_back, out_back, attn_gain_back, ffn_gain_back = (
-        lax.all_gather(w_query, ("rows", "seq"), axis=0, tiled=True),
-        lax.all_gather(w_key, ("rows", "seq"), axis=0, tiled=True),
-        lax.all_gather(w_value, ("rows", "seq"), axis=0, tiled=True),
-        lax.all_gather(w_out, ("rows", "seq"), axis=0, tiled=True),
-        lax.all_gather(gain_attn, ("rows", "seq"), axis=0, tiled=True),
-        lax.all_gather(gain_ffn, ("rows", "seq"), axis=0, tiled=True),
-    )
-    grad_hidden = times_transposed(cot_all, down_back)
+    grad_hidden = times_transposed(cot_all, down_loc)
     grad_down_w = transposed_times(hidden_b, cot_all)
     sigma_gate = jax.nn.sigmoid(gate_val)
     grad_gate_b = (
         grad_hidden * up_val * sigma_gate * (1.0 + gate_val * (1.0 - sigma_gate))
     ).astype(jnp.bfloat16)
     grad_up_b = (grad_hidden * gate_val * sigma_gate).astype(jnp.bfloat16)
-    ffn_in_terms = times_transposed(grad_gate_b, gate_back) + times_transposed(grad_up_b, up_back)
+    ffn_in_terms = times_transposed(grad_gate_b, gate_loc) + times_transposed(grad_up_b, up_loc)
     grad_gate_w = transposed_times(ffn_all, grad_gate_b)
     grad_up_w = transposed_times(ffn_all, grad_up_b)
-    ffn_sums = (
-        lax.psum_scatter(
-            grad_gate_w.astype(jnp.bfloat16), "seq", scatter_dimension=0, tiled=True
-        ).astype(jnp.float32),
-        lax.psum_scatter(
-            grad_up_w.astype(jnp.bfloat16), "seq", scatter_dimension=0, tiled=True
-        ).astype(jnp.float32),
-        lax.psum_scatter(
-            grad_down_w.astype(jnp.bfloat16), "seq", scatter_dimension=1, tiled=True
-        ).astype(jnp.float32),
-    )
-    grad_ffn_in = lax.psum_scatter(
-        ffn_in_terms.astype(jnp.bfloat16), "rows", scatter_dimension=0, tiled=True
-    ).astype(jnp.float32)
-    grad_mid_ffn, gain_ffn_rows = rms_back(middle, ffn_gain_back.astype(jnp.float32), grad_ffn_in)
+
+    def columns_home(grad):
+        low = grad.astype(jnp.bfloat16).reshape(planes, plane_width, ffn_here)
+        mine = ring_scatter([low[t] for t in range(planes)]).reshape(2, -1, ffn_here)
+        keep, send = pick(mine, y_at, 0)
+        got = y_swap(send.astype(jnp.bfloat16)).astype(jnp.float32)
+        return in_order(keep, got, y_at, 1).reshape(-1, 2 * ffn_here)
+
+    def rows_home(grad):
+        low = grad.astype(jnp.bfloat16)
+        mine = ring_scatter(
+            [low[:, t * plane_width : (t + 1) * plane_width] for t in range(planes)]
+        )
+        first, second = mine[:, : plane_width // 2], mine[:, plane_width // 2 :]
+        keep = jnp.where(y_at == 0, first, second)
+        send = jnp.where(y_at == 0, second, first)
+        got = y_swap(send.astype(jnp.bfloat16)).astype(jnp.float32)
+        return in_order(keep, got, y_at, 0).reshape(2 * ffn_here, -1)
+
+    ffn_sums = (columns_home(grad_gate_w), columns_home(grad_up_w), rows_home(grad_down_w))
+    grad_ffn_in = turn_columns(scatter_tokens(ffn_in_terms), z_back, plane_width)
+    grad_mid_ffn, gain_ffn_rows = rms_back(middle, ffn_gain_full, grad_ffn_in)
     grad_middle = grad_top_b.astype(jnp.float32) + grad_mid_ffn
     grad_gain_ffn = jnp.sum(gain_ffn_rows, axis=0)
     grad_branch = grad_middle.astype(jnp.bfloat16)
     grad_out_w = transposed_times(attended_b, grad_branch)
-    grad_attended = times_transposed(grad_branch, out_back).astype(jnp.bfloat16)
+    grad_attended = times_transposed(grad_branch, out_full).astype(jnp.bfloat16)
     grad_att = grad_attended.reshape(rows_here, seg_tok, heads_kv, grouping, head_dim)
 
     def delta_step(block_index, accum_in):
@@ -295,14 +480,19 @@
             jnp.zeros(kv_shape, jnp.float32),
         ),
     )
-    grad_keys_mine, grad_values_mine = (
-        lax.psum_scatter(
-            grad_keys_full.astype(jnp.bfloat16), "seq", scatter_dimension=1, tiled=True
-        ).astype(jnp.float32),
-        lax.psum_scatter(
-            grad_values_full.astype(jnp.bfloat16), "seq", scatter_dimension=1, tiled=True
-        ).astype(jnp.float32),
-    )
+    grad_kv = jnp.concatenate(
+        [
+            grad_keys_full.reshape(rows_here, row_len, -1),
+            grad_values_full.reshape(rows_here, row_len, -1),
+        ],
+        axis=2,
+    ).astype(jnp.bfloat16)
+    grad_kv = jnp.moveaxis(grad_kv.reshape(rows_here, planes, 2, seg_tok, kv_width), 0, 2)
+    keep, send = pick(grad_kv, y_at, 1)
+    grad_kv = turn(add_low(keep, y_swap(send)), z_at)
+    grad_kv_mine = ring_scatter([grad_kv[t] for t in range(planes)])
+    grad_keys_mine = grad_kv_mine[..., : kv_width // 2]
+    grad_values_mine = grad_kv_mine[..., kv_width // 2 :]
     grad_value_b = grad_values_mine.reshape(tokens_here, heads_kv * head_dim).astype(jnp.bfloat16)
     grad_key_norm = rotate_back(
         grad_keys_mine.reshape(tokens_here, heads_kv, head_dim), cosine, sine
@@ -314,44 +504,51 @@
     )
     grad_query_pre, gain_q_rows = rms_back(query_heads, gain_q, grad_query_norm)
     grad_query_b = grad_query_pre.reshape(tokens_here, heads_query * head_dim).astype(jnp.bfloat16)
-    gain_sums = lax.psum(
-        (jnp.sum(gain_q_rows, axis=(0, 1)), jnp.sum(gain_k_rows, axis=(0, 1))), ("rows", "seq")
-    )
-    grad_query_w = transposed_times(normed, grad_query_b)
-    grad_key_w = transposed_times(normed, grad_key_b)
-    grad_value_w = transposed_times(normed, grad_value_b)
-    grad_normed = (
-        times_transposed(grad_query_b, query_back)
-        + times_transposed(grad_key_b, key_back)
-        + times_transposed(grad_value_b, value_back)
-    )
+    grad_qkv_b = jnp.concatenate([grad_query_b, grad_key_b, grad_value_b], axis=1)
+    grad_qkv_w = transposed_times(normed, grad_qkv_b)
+    grad_normed = times_transposed(grad_qkv_b, qkv_full)
     grad_resid_attn, gain_attn_rows = rms_back(
-        residual, attn_gain_back.astype(jnp.float32), grad_normed
+        residual, attn_gain_full, grad_normed
     )
     grad_inputs = (grad_middle + grad_resid_attn).reshape(rows_here, seg_tok, feature_count)
     grad_gain_attn = jnp.sum(gain_attn_rows, axis=0)
-    attn_sums = (
-        lax.psum_scatter(grad_query_w, ("rows", "seq"), scatter_dimension=0, tiled=True),
-        lax.psum_scatter(grad_key_w, ("rows", "seq"), scatter_dimension=0, tiled=True),
-        lax.psum_scatter(grad_value_w, ("rows", "seq"), scatter_dimension=0, tiled=True),
-        lax.psum_scatter(grad_out_w, ("rows", "seq"), scatter_dimension=0, tiled=True),
-        lax.psum_scatter(grad_gain_attn, ("rows", "seq"), scatter_dimension=0, tiled=True),
-        lax.psum_scatter(grad_gain_ffn, ("rows", "seq"), scatter_dimension=0, tiled=True),
-    )
+    grad_qkv_mine = jnp.concatenate(
+        [
+            scatter_weights(grad_qkv_w[:, :qkv_cut], True),
+            scatter_weights(grad_qkv_w[:, qkv_cut:], False),
+        ],
+        axis=1,
+    )
+    grad_out_mine = jnp.concatenate(
+        [
+            scatter_weights(grad_out_w[:, :out_cut], True),
+            scatter_weights(grad_out_w[:, out_cut:], False),
+        ],
+        axis=1,
+    )
+    small = jnp.concatenate(
+        [
+            grad_gain_attn,
+            grad_gain_ffn,
+            jnp.sum(gain_q_rows, axis=(0, 1)),
+            jnp.sum(gain_k_rows, axis=(0, 1)),
+        ]
+    )
+    small = sum_all(small.reshape(-1, 128)).reshape(-1)
     return (
         output_b,
         grad_inputs,
-        attn_sums[0],
-        attn_sums[1],
-        attn_sums[2],
-        attn_sums[3],
+        grad_qkv_mine[:, :width_q],
+        grad_qkv_mine[:, width_q : width_q + width_k],
+        grad_qkv_mine[:, width_q + width_k :],
+        grad_out_mine,
         ffn_sums[0],
         ffn_sums[1],
         ffn_sums[2],
-        attn_sums[4],
-        gain_sums[0],
-        gain_sums[1],
-        attn_sums[5],
+        lax.dynamic_slice_in_dim(small, place * gain_size, gain_size),
+        small[2 * feature_count : 2 * feature_count + head_dim],
+        small[2 * feature_count + head_dim :],
+        lax.dynamic_slice_in_dim(small, feature_count + place * gain_size, gain_size),
     )
 
 

time: 2160 us -> 1050 us (0.49)
  waiting for transfers between devices: 1680 us -> 334 us
  starting transfers between devices: 0.89 us -> 135 us
  local copies, waits for them, and re-layouts: 83.1 us -> 215 us
  other arithmetic: 44.3 us -> 166 us
  blocking collectives: 104 us -> 0 us
  matrix products: 226 us -> 186 us
    reduce_scatter x9 -> x0, waiting for transfers between devices: 1040 us -> none  [the longest x1 230 us: local(): lax.psum_scatter(grad_query_w, ('rows', 'seq'), scatter_dimension=0, tile...]
    all_gather x11 -> x0, waiting for transfers between devices: 558 us -> none  [the longest x1 108 us: local(): lax.all_gather(w_down, 'seq', axis=1, tiled=True)]
    ppermute x0 -> x126, waiting for transfers between devices: none -> 334 us  [the longest x51 205 us: ring(): lax.ppermute(values, 'seq', [(i, (i + 2 * shift) % count) for i in range(...]
    ppermute x0 -> x126, starting transfers between devices: none -> 135 us  [the longest x51 73.1 us: ring(): lax.ppermute(values, 'seq', [(i, (i + 2 * shift) % count) for i in range(...]
    unnamed x2 -> x0, blocking collectives: 85 us -> none
    unnamed x24 -> x0, waiting for transfers between devices: 79.8 us -> none
    slice x0 -> x26, local copies, waits for them, and re-layouts: none -> 44.5 us  [the longest x2 9.02 us: scatter_tokens(): far = core_swap(values[4 * count:].astype(jnp.bfloat16))]
    another operation x0 -> x18, other arithmetic: none -> 38.9 us
  transfers between devices with their start and end apart: 22 -> 126, of which waited for: 22 -> 60; matrix products, arithmetic and copies ran while one was open for 10% -> 42% of each run, Pallas kernels for 0% -> 0%
where the time goes in v1:
time: 1050 us; the launch traced here: 1040 us
  waiting for transfers between devices  334 us (32%)
  local copies, waits for them, and re-layouts  215 us (20%)
  matrix products  186 us (18%)
  other arithmetic  166 us (16%)
  starting transfers between devices  135 us (13%)
    ppermute x51, waiting for transfers between devices, ring(): lax.ppermute(values, 'seq', [(i, (i + 2 * shift) % count) for i in range(...  205 us
    ppermute x75, waiting for transfers between devices, swap(): return lax.ppermute(values, axis_name, [(i, i ^ bit) for i in range(count)])  129 us
    ppermute x51, starting transfers between devices, ring(): lax.ppermute(values, 'seq', [(i, (i + 2 * shift) % count) for i in range(...  73.1 us
    unnamed x359, local copies, waits for them, and re-layouts  63 us
    ppermute x75, starting transfers between devices, swap(): return lax.ppermute(values, axis_name, [(i, i ^ bit) for i in range(count)])  61.7 us
    dot_general x5, matrix products, times_transposed(): lax.dot_general(left, right, (((1,), (1,)), ((), ())), preferred_element_...  53.6 us
    dot_general x5, matrix products, transposed_times(): lax.dot_general(left, right, (((0,), (0,)), ((), ())), preferred_element_...  36.2 us
    another operation x4, other arithmetic  24.6 us
  transfers between devices with their start and end apart: 126, of which 60 were waited for; matrix products, arithmetic and copies ran while one was open for 42% of the time, Pallas kernels for 0%

profile of v1, /device:TPU:0, one launch (start us, length us, event | category | flops | bytes accessed | tf_op | source)
XLA Modules:
  0.0 1041.3 jit_solution(4988185398195657322)
XLA Ops:
  118.4 4.8 collective-permute-done.13
  183.7 10.5 %collective-permute-done.15 = bf16[4,2,64,896]{3,2,1,0:T(8,128)(2,1)S(1)} collective-permute-done((bf16[4,2,64,896]{3,2,1,0:T(8,128)(2,1)S(1)}, bf16[4,2,64,896]{3,2,1,0:T(8,128)(2,1)S(1)}, u32[]{:S(2)}, u32[]{:S(2)}) %collective-permute-start.15) | collective-permute-done | bytes 917536 | tf_op jit(solution)/shard_map/ppermute | solution.py:61
  194.6 6.9 collective-permute-done.9
  201.6 6.2 collective-permute-done.70
  283.3 6.1 copy.356
  293.6 9.1 while.62
  304.4 15.0 %while.63 = (s32[]{:T(128)}, f32[2,128,5,4,64]{1,4,3,2,0:T(8,128)}, bf16[2,1024,320]{1,2,0:T(8,128)(2,1)S(1)}, s32[2,1024]{1,0:T(2,128)S(1)}, f32[2,128]{1,0:T(2...) while((s32[]{:T(128)}, f32[2,128,5,4,64]{1,4,3,2,0:T(8,128)}, ...), condition=%wide.region_8.9_spmd.clone, body=%wide.region_7.8_spmd.clone.sunk | while | flops 682559104 | bytes 7641293 | solution.py:350
  306.2 5.6 fusion.255
  313.4 6.1 fusion.255
  342.5 10.5 %collective-permute-done.56 = bf16[512,832]{0,1:T(8,128)(2,1)} collective-permute-done((bf16[512,832]{0,1:T(8,128)(2,1)S(1)}, bf16[512,832]{0,1:T(8,128)(2,1)}, u32[]{:S(2)}, u32[]{:S(2)}) %collective-permute-start.56) | collective-permute-done | bytes 852000 | tf_op jit(solution)/shard_map/ppermute | solution.py:66
  357.9 13.3 %collective-permute-done.62 = bf16[832,512]{1,0:T(8,128)(2,1)S(1)} collective-permute-done((bf16[832,512]{1,0:T(8,128)(2,1)}, bf16[832,512]{1,0:T(8,128)(2,1)S(1)}, u32[]{:S(2)}, u32[]{:S(2)}) %collective-permute-start.62) | collective-permute-done | bytes 852000 | tf_op jit(solution)/shard_map/ppermute | solution.py:66
  374.4 11.4 %fusion.166 = f32[2048,832]{0,1:T(8,128)} fusion(bf16[2048,2048]{1,0:T(8,128)(2,1)} %constant_dynamic-update-slice_fusion.60, bf16[832,2048]{1,0:T(8,128)(2,1)S(1)} %constant_dynamic-update-slice_fusion.56), kind=kOutput, calls=%fused_computation.514 | convolution fusion | flops 6979321856 | bytes 18612224 | tf_op jit(solution)/shard_map/dot_general | solution.py:48
  396.8 10.6 %collective-permute-done.57 = bf16[512,832]{0,1:T(8,128)(2,1)} collective-permute-done((bf16[512,832]{0,1:T(8,128)(2,1)}, bf16[512,832]{0,1:T(8,128)(2,1)}, u32[]{:S(2)}, u32[]{:S(2)}) %collective-permute-start.57) | collective-permute-done | bytes 852000 | tf_op jit(solution)/shard_map/ppermute | solution.py:66
  416.8 31.1 %collective-permute-done.58 = bf16[512,832]{0,1:T(8,128)(2,1)S(1)} collective-permute-done((bf16[512,832]{0,1:T(8,128)(2,1)}, bf16[512,832]{0,1:T(8,128)(2,1)S(1)}, u32[]{:S(2)}, u32[]{:S(2)}) %collective-permute-start.58) | collective-permute-done | bytes 852000 | tf_op jit(solution)/shard_map/ppermute | solution.py:66
  447.8 12.3 %fusion.110 = f32[2048,832]{0,1:T(8,128)} fusion(bf16[2048,2048]{1,0:T(8,128)(2,1)} %constant_dynamic-update-slice_fusion.48, bf16[512,832]{0,1:T(8,128)(2,1)S(1)} %collective-permute-done.58, bf16[512,832]{0,1:T(8,128)(2,1)} %collective-permute-done.57, bf16[512,832]{0,1:T(8,128)(2,1)} %collective-permute-done.56, bf16[512,832]{0,1:T(8,128)(2,1)S(1)} %copy-done.103), kind=kOutput, calls=%fused_computation.285 | convolution fusion | flops 6992953344 | bytes 18612224 | tf_op jit(solution)/shard_map/dot_general | solution.py:382
  460.1 17.7 %multiply_convert_fusion.1 = (bf16[2048,832]{0,1:T(8,128)(2,1)S(1)}, bf16[2048,832]{0,1:T(8,128)(2,1)}, bf16[2048,832]{0,1:T(8,128)(2,1)}) fusion(f32[2048,832]{0,1:T(8,128)} %fusion.166, f32[2048,832]{0,1:T(8,128)} %fusion.110, bf16[2048,2048]{1,0:T(8,128)(2,1)} %constant_dynamic-update-slice_fusion.48, bf16[512,832]{0,1:T(8,128)(2,1)S(1)} %collective-permute-done.54, ...), kind=kOutput, calls=%fused_computation.83 | convolution fusion | flops 7020216320 | bytes 35651584 | tf_op jit(solution)/shard_map/dot_general | solution.py:381
  477.9 11.9 %convolution_convert_fusion.2 = bf16[832,2048]{1,0:T(8,128)(2,1)S(1)} fusion(bf16[2048,832]{0,1:T(8,128)(2,1)} %get-tuple-element.1244, bf16[2048,2048]{1,0:T(8,128)(2,1)} %constant_dynamic-update-slice_fusion.60), kind=kOutput, calls=%fused_computation.103 | convolution fusion | flops 6981025792 | bytes 15204352 | tf_op jit(solution)/shard_map/dot_general | solution.py:54
  490.0 8.0 convolution_convert_fusion.1
  497.9 7.4 convolution_convert_fusion
  512.9 14.2 %fusion.109 = f32[2048,2048]{1,0:T(8,128)} fusion(bf16[2048,832]{0,1:T(8,128)(2,1)S(1)} %copy-done.149, bf16[512,832]{0,1:T(8,128)(2,1)S(1)} %copy-done.146, bf16[512,832]{0,1:T(8,128)(2,1)} %collective-permute-done.57, bf16[512,832]{0,1:T(8,128)(2,1)} %collective-permute-done.56, bf16[512,832]{0,1:T(8,128)(2,1)S(1)} %copy-done.103), kind=kOutput, calls=%fused_computation.284 | convolution fusion | flops 6992953344 | bytes 23592960 | tf_op jit(solution)/shard_map/dot_general | solution.py:48
  527.6 17.5 %convolution_add_fusion = f32[2048,2048]{1,0:T(8,128)} fusion(f32[2048,2048]{1,0:T(8,128)} %fusion.109, bf16[2048,832]{0,1:T(8,128)(2,1)} %copy-done.150, bf16[512,832]{0,1:T(8,128)(2,1)} %copy-done.144, bf16[512,832]{0,1:T(8,128)(2,1)} %collective-permute-done.53, bf16[512,832]{0,1:T(8,128)(2,1)} %collective-permute-done.52, bf16[512,832]{0,1:T(8,128)(2,1)} %copy.428), kind=kOutput, calls=%fused_computation.81 | convolution fusion | flops 6997147648 | bytes 40370176 | tf_op jit(solution)/shard_map/dot_general | solution.py:48
  545.1 6.0 slice.603
  556.1 12.4 %collective-permute-done.118 = bf16[832,512]{1,0:T(8,128)(2,1)} collective-permute-done((bf16[832,512]{1,0:T(8,128)(2,1)S(1)}, bf16[832,512]{1,0:T(8,128)(2,1)}, u32[]{:S(2)}, u32[]{:S(2)}) %collective-permute-start.118) | collective-permute-done | bytes 852000 | tf_op jit(solution)/shard_map/ppermute | solution.py:66
  570.7 9.2 fusion.165
  589.5 15.5 %collective-permute-done.114 = bf16[512,832]{0,1:T(8,128)(2,1)} collective-permute-done((bf16[512,832]{0,1:T(8,128)(2,1)}, bf16[512,832]{0,1:T(8,128)(2,1)}, u32[]{:S(2)}, u32[]{:S(2)}) %collective-permute-start.114) | collective-permute-done | bytes 852000 | tf_op jit(solution)/shard_map/ppermute | solution.py:66
  608.0 15.3 %collective-permute-done.119 = bf16[832,512]{1,0:T(8,128)(2,1)} collective-permute-done((bf16[832,512]{1,0:T(8,128)(2,1)S(1)}, bf16[832,512]{1,0:T(8,128)(2,1)}, u32[]{:S(2)}, u32[]{:S(2)}) %collective-permute-start.119) | collective-permute-done | bytes 852000 | tf_op jit(solution)/shard_map/ppermute | solution.py:66
  626.4 15.1 %collective-permute-done.111 = bf16[512,832]{0,1:T(8,128)(2,1)S(1)} collective-permute-done((bf16[512,832]{0,1:T(8,128)(2,1)S(1)}, bf16[512,832]{0,1:T(8,128)(2,1)S(1)}, u32[]{:S(2)}, u32[]{:S(2)}) %collective-permute-start.111) | collective-permute-done | bytes 852000 | tf_op jit(solution)/shard_map/ppermute | solution.py:66
  650.7 7.5 collective-permute-done.115
  671.5 4.6 collective-permute-done.116
  677.1 10.1 fusion.149
  688.8 10.2 fusion.151
  723.0 17.0 %collective-permute-done.80 = bf16[256,2048]{1,0:T(8,128)(2,1)} collective-permute-done((bf16[256,2048]{1,0:T(8,128)(2,1)}, bf16[256,2048]{1,0:T(8,128)(2,1)}, u32[]{:S(2)}, u32[]{:S(2)}) %collective-permute-start.80) | collective-permute-done | bytes 1048608 | tf_op jit(solution)/shard_map/ppermute | solution.py:61
  744.2 13.8 %collective-permute-done.67 = bf16[256,2048]{1,0:T(8,128)(2,1)S(1)} collective-permute-done((bf16[256,2048]{1,0:T(8,128)(2,1)S(1)}, bf16[256,2048]{1,0:T(8,128)(2,1)S(1)}, u32[]{:S(2)}, u32[]{:S(2)}) %collective-permute-start.67) | collective-permute-done | bytes 1048608 | tf_op jit(solution)/shard_map/ppermute | solution.py:61
  773.2 12.8 %while.64 = (s32[]{:T(128)}, f32[2,5,4,128]{3,2,1,0:T(4,128)S(1)}, s32[2,1024]{1,0:T(2,128)S(1)}, f32[2,128]{1,0:T(2,128)S(1)}, bf16[2,1024,320]{1,2,0:T(8,128)(...) while((s32[]{:T(128)}, f32[2,5,4,128]{3,2,1,0:T(4,128)S(1)}, ...), condition=%wide.region_13.14_spmd.clone, body=%wide.region_11.13_spmd.clone.sunk | while | flops 684530304 | bytes 29350128 | solution.py:436
  788.4 30.9 %while.65 = (s32[]{:T(128)}, f32[2,128,5,4,64]{1,4,3,2,0:T(8,128)}, bf16[2,1024,5,64]{1,3,2,0:T(8,128)(2,1)}, bf16[2,1024,5,64]{1,3,2,0:T(8,128)(2,1)}, bf16[2,1...) while((s32[]{:T(128)}, f32[2,128,5,4,64]{1,4,3,2,0:T(8,128)}, ...), condition=%wide.region_15.16_spmd.clone, body=%wide.region_14.15_spmd.clone.sunk | while | flops 1705576064 | bytes 83835264 | solution.py:473
  795.0 4.9 fusion.273
  810.3 4.9 fusion.273
  825.5 6.6 fusion.101
  855.3 8.0 fusion.153
  876.0 4.7 collective-permute-done.81
  900.8 6.1 collective-permute-done.83
  927.3 7.6 fusion.80
  983.1 12.1 %collective-permute-done.92 = bf16[2,4,64,896]{3,2,1,0:T(8,128)(2,1)S(1)} collective-permute-done((bf16[2,4,64,896]{3,2,1,0:T(8,128)(2,1)S(1)}, bf16[2,4,64,896]{3,2,1,0:T(8,128)(2,1)S(1)}, u32[]{:S(2)}, u32[]{:S(2)}) %collective-permute-start.92) | collective-permute-done | bytes 917536 | tf_op jit(solution)/shard_map/ppermute | solution.py:61
  996.8 8.6 collective-permute-done.86
  1011.5 6.7 collective-permute-done.94
  1019.3 5.9 collective-permute-done.95
  1026.7 5.2 collective-permute-done.96
  1034.3 6.0 collective-permute-done.90
  (980 shorter events, 600.8 us)
Async XLA Ops:
  0.7 30.8 %collective-permute-start.24 = (s32[2,128]{1,0:T(2,128)}, s32[2,128]{1,0:T(2,128)}, u32[]{:S(2)}, u32[]{:S(2)}) collective-permute-start(s32[2,128]{1,0:T(2,128)} %param.26), channel_id=1, source_target_pairs={{0,1},{1,0},{2,3},{3,2},{4,5},{5,4},{6,7},{7,6},{8,9},{9,8},{10,11... | collective-permute-start | bytes 3080 | tf_op jit(solution)/shard_map/ppermute | solution.py:61
  3.7 27.4 %collective-permute-start.25 = (s32[2,128]{1,0:T(2,128)}, s32[2,128]{1,0:T(2,128)}, u32[]{:S(2)}, u32[]{:S(2)}) collective-permute-start(s32[2,128]{1,0:T(2,128)} %param.26), channel_id=1, source_target_pairs={{0,6},{1,7},{2,0},{3,1},{4,2},{5,3},{6,4},{7,5},{8,14},{9,15},{10,... | collective-permute-start | bytes 3080 | tf_op jit(solution)/shard_map/ppermute | solution.py:66
  10.5 152.8 %collective-permute-start.69 = (bf16[256,2048]{1,0:T(8,128)(2,1)}, bf16[256,2048]{1,0:T(8,128)(2,1)}, u32[]{:S(2)}, u32[]{:S(2)}) collective-permute-start(bf16[256,2048]{1,0:T(8,128)(2,1)} %get-tuple-element.1230), channel_id=1, source_target_pairs={{0,1},{1,0},{2,3},{3,2},{4,5},{5,4},{6,7},{7,6},{8,9},{9,8},{10,11... | collective-permute-start | bytes 3145736 | tf_op jit(solution)/shard_map/ppermute | solution.py:61
  11.1 156.9 %collective-permute-start.68 = (bf16[256,2048]{1,0:T(8,128)(2,1)}, bf16[256,2048]{1,0:T(8,128)(2,1)}, u32[]{:S(2)}, u32[]{:S(2)}) collective-permute-start(bf16[256,2048]{1,0:T(8,128)(2,1)} %get-tuple-element.1230), channel_id=1, source_target_pairs={{0,16},{8,24},{16,0},{24,8},{1,17},{9,25},{17,1},{25,9},{2,18},{10... | collective-permute-start | bytes 3145736 | tf_op jit(solution)/shard_map/ppermute | solution.py:61
  12.8 34.0 %collective-permute-start = (f32[32,128]{1,0:T(8,128)S(1)}, f32[32,128]{1,0:T(8,128)S(1)}, u32[]{:S(2)}, u32[]{:S(2)}) collective-permute-start(f32[32,128]{1,0:T(8,128)S(1)} %bitcast.794), channel_id=1, source_target_pairs={{0,8},{8,0},{16,24},{24,16},{1,9},{9,1},{17,25},{25,17},{2,10},{10... | collective-permute-start | bytes 49160 | tf_op jit(solution)/shard_map/ppermute | solution.py:61
  39.4 34.7 %collective-permute-start.5 = (bf16[64,1024]{1,0:T(8,128)(2,1)}, bf16[64,1024]{1,0:T(8,128)(2,1)S(1)}, u32[]{:S(2)}, u32[]{:S(2)}) collective-permute-start(bf16[64,1024]{1,0:T(8,128)(2,1)} %slice.315), channel_id=1, source_target_pairs={{0,6},{1,7},{2,0},{3,1},{4,2},{5,3},{6,4},{7,5},{8,14},{9,15},{10,... | collective-permute-start | bytes 393224 | tf_op jit(solution)/shard_map/ppermute | solution.py:66
  68.2 63.7 %collective-permute-start.59 = (bf16[832,256]{1,0:T(8,128)(2,1)}, bf16[832,256]{1,0:T(8,128)(2,1)S(1)}, u32[]{:S(2)}, u32[]{:S(2)}) collective-permute-start(bf16[832,256]{1,0:T(8,128)(2,1)} %get-tuple-element.1277), channel_id=1, source_target_pairs={{0,1},{1,0},{2,3},{3,2},{4,5},{5,4},{6,7},{7,6},{8,9},{9,8},{10,11... | collective-permute-start | bytes 1277960 | tf_op jit(solution)/shard_map/ppermute | solution.py:61
  72.3 59.4 %collective-permute-start.51 = (bf16[256,832]{1,0:T(8,128)(2,1)}, bf16[256,832]{1,0:T(8,128)(2,1)S(1)}, u32[]{:S(2)}, u32[]{:S(2)}) collective-permute-start(bf16[256,832]{1,0:T(8,128)(2,1)} %get-tuple-element.1279), channel_id=1, source_target_pairs={{0,1},{1,0},{2,3},{3,2},{4,5},{5,4},{6,7},{7,6},{8,9},{9,8},{10,11... | collective-permute-start | bytes 1277960 | tf_op jit(solution)/shard_map/ppermute | solution.py:61
  131.7 196.7 %collective-permute-start.72 = (bf16[256,2048]{1,0:T(8,128)(2,1)}, bf16[256,2048]{1,0:T(8,128)(2,1)}, u32[]{:S(2)}, u32[]{:S(2)}) collective-permute-start(bf16[256,2048]{1,0:T(8,128)(2,1)} %get-tuple-element.1230), channel_id=1, source_target_pairs={{0,8},{8,0},{16,24},{24,16},{1,9},{9,1},{17,25},{25,17},{2,10},{10... | collective-permute-start | bytes 3145736 | tf_op jit(solution)/shard_map/ppermute | solution.py:61
  168.0 26.3 %collective-permute-start.15 = (bf16[4,2,64,896]{3,2,1,0:T(8,128)(2,1)S(1)}, bf16[4,2,64,896]{3,2,1,0:T(8,128)(2,1)S(1)}, u32[]{:S(2)}, u32[]{:S(2)}) collective-permute-start(bf16[4,2,64,896]{3,2,1,0:T(8,128)(2,1)S(1)} %maximum_select_fusion.14), channel_id=1, source_target_pairs={{0,16},{8,24},{16,0},{24,8},{1,17},{9,25},{17,1},{25,9},{2,18},{10... | collective-permute-start | bytes 2752520 | tf_op jit(solution)/shard_map/ppermute | solution.py:61
  175.4 26.1 %collective-permute-start.9 = (bf16[2,4,64,1024]{3,2,1,0:T(8,128)(2,1)S(1)}, bf16[2,4,64,1024]{3,2,1,0:T(8,128)(2,1)S(1)}, u32[]{:S(2)}, u32[]{:S(2)}) collective-permute-start(bf16[2,4,64,1024]{3,2,1,0:T(8,128)(2,1)S(1)} %maximum_select_fusion.13), channel_id=1, source_target_pairs={{0,1},{1,0},{2,3},{3,2},{4,5},{5,4},{6,7},{7,6},{8,9},{9,8},{10,11... | collective-permute-start | bytes 3145736 | tf_op jit(solution)/shard_map/ppermute | solution.py:61
  177.0 31.8 %collective-permute-start.71 = (bf16[256,1024]{1,0:T(8,128)(2,1)S(1)}, bf16[256,1024]{1,0:T(8,128)(2,1)S(1)}, u32[]{:S(2)}, u32[]{:S(2)}) collective-permute-start(bf16[256,1024]{1,0:T(8,128)(2,1)S(1)} %slice.430), channel_id=1, source_target_pairs={{0,16},{8,24},{16,0},{24,8},{1,17},{9,25},{17,1},{25,9},{2,18},{10... | collective-permute-start | bytes 1572872 | tf_op jit(solution)/shard_map/ppermute | solution.py:61
  181.9 25.9 %collective-permute-start.70 = (bf16[256,1024]{1,0:T(8,128)(2,1)S(1)}, bf16[256,1024]{1,0:T(8,128)(2,1)S(1)}, u32[]{:S(2)}, u32[]{:S(2)}) collective-permute-start(bf16[256,1024]{1,0:T(8,128)(2,1)S(1)} %slice.429), channel_id=1, source_target_pairs={{0,1},{1,0},{2,3},{3,2},{4,5},{5,4},{6,7},{7,6},{8,9},{9,8},{10,11... | collective-permute-start | bytes 1572872 | tf_op jit(solution)/shard_map/ppermute | solution.py:61
  212.2 118.9 %collective-permute-start.52 = (bf16[512,832]{0,1:T(8,128)(2,1)}, bf16[512,832]{0,1:T(8,128)(2,1)}, u32[]{:S(2)}, u32[]{:S(2)}) collective-permute-start(bf16[512,832]{0,1:T(8,128)(2,1)} %copy.428), channel_id=1, source_target_pairs={{0,6},{1,7},{2,0},{3,1},{4,2},{5,3},{6,4},{7,5},{8,14},{9,15},{10,... | collective-permute-start | bytes 2555912 | tf_op jit(solution)/shard_map/ppermute | solution.py:66
  232.0 24.9 %collective-permute-start.17 = (bf16[2,128,640]{1,0,2:T(2,128)(2,1)}, bf16[2,128,640]{1,0,2:T(2,128)(2,1)}, u32[]{:S(2)}, u32[]{:S(2)}) collective-permute-start(bf16[2,128,640]{1,0,2:T(2,128)(2,1)} %pad_maximum_fusion.32), channel_id=1, source_target_pairs={{0,1},{1,0},{2,3},{3,2},{4,5},{5,4},{6,7},{7,6},{8,9},{9,8},{10,11... | collective-permute-start | bytes 983048 | tf_op jit(solution)/shard_map/ppermute | solution.py:61
  260.1 73.1 %collective-permute-start.74 = (bf16[256,2048]{1,0:T(8,128)(2,1)}, bf16[256,2048]{1,0:T(8,128)(2,1)}, u32[]{:S(2)}, u32[]{:S(2)}) collective-permute-start(bf16[256,2048]{1,0:T(8,128)(2,1)} %collective-permute-done.69), channel_id=1, source_target_pairs={{0,8},{8,0},{16,24},{24,16},{1,9},{9,1},{17,25},{25,17},{2,10},{10... | collective-permute-start | bytes 3145736 | tf_op jit(solution)/shard_map/ppermute | solution.py:61
  267.6 66.1 %collective-permute-start.73 = (bf16[256,2048]{1,0:T(8,128)(2,1)}, bf16[256,2048]{1,0:T(8,128)(2,1)}, u32[]{:S(2)}, u32[]{:S(2)}) collective-permute-start(bf16[256,2048]{1,0:T(8,128)(2,1)} %collective-permute-done.68), channel_id=1, source_target_pairs={{0,8},{8,0},{16,24},{24,16},{1,9},{9,1},{17,25},{25,17},{2,10},{10... | collective-permute-start | bytes 3145736 | tf_op jit(solution)/shard_map/ppermute | solution.py:61
  272.6 63.5 %collective-permute-start.61 = (bf16[832,512]{1,0:T(8,128)(2,1)}, bf16[832,512]{1,0:T(8,128)(2,1)}, u32[]{:S(2)}, u32[]{:S(2)}) collective-permute-start(bf16[832,512]{1,0:T(8,128)(2,1)} %collective-permute-done.60), channel_id=1, source_target_pairs={{0,6},{1,7},{2,0},{3,1},{4,2},{5,3},{6,4},{7,5},{8,14},{9,15},{10,... | collective-permute-start | bytes 2555912 | tf_op jit(solution)/shard_map/ppermute | solution.py:66
  329.2 27.6 %collective-permute-start.75 = (bf16[256,2048]{1,0:T(8,128)(2,1)S(1)}, bf16[256,2048]{1,0:T(8,128)(2,1)S(1)}, u32[]{:S(2)}, u32[]{:S(2)}) collective-permute-start(bf16[256,2048]{1,0:T(8,128)(2,1)S(1)} %copy-done.95), channel_id=1, source_target_pairs={{0,8},{8,0},{16,24},{24,16},{1,9},{9,1},{17,25},{25,17},{2,10},{10... | collective-permute-start | bytes 3145736 | tf_op jit(solution)/shard_map/ppermute | solution.py:61
  333.1 38.2 %collective-permute-start.44 = (bf16[256,2048]{1,0:T(8,128)(2,1)}, bf16[256,2048]{1,0:T(8,128)(2,1)S(1)}, u32[]{:S(2)}, u32[]{:S(2)}) collective-permute-start(bf16[256,2048]{1,0:T(8,128)(2,1)} %get-tuple-element.1234), channel_id=1, source_target_pairs={{0,1},{1,0},{2,3},{3,2},{4,5},{5,4},{6,7},{7,6},{8,9},{9,8},{10,11... | collective-permute-start | bytes 3145736 | tf_op jit(solution)/shard_map/ppermute | solution.py:61
  333.7 38.7 %collective-permute-start.43 = (bf16[256,2048]{1,0:T(8,128)(2,1)}, bf16[256,2048]{1,0:T(8,128)(2,1)S(1)}, u32[]{:S(2)}, u32[]{:S(2)}) collective-permute-start(bf16[256,2048]{1,0:T(8,128)(2,1)} %get-tuple-element.1234), channel_id=1, source_target_pairs={{0,16},{8,24},{16,0},{24,8},{1,17},{9,25},{17,1},{25,9},{2,18},{10... | collective-permute-start | bytes 3145736 | tf_op jit(solution)/shard_map/ppermute | solution.py:61
  336.1 35.1 %collective-permute-start.62 = (bf16[832,512]{1,0:T(8,128)(2,1)}, bf16[832,512]{1,0:T(8,128)(2,1)S(1)}, u32[]{:S(2)}, u32[]{:S(2)}) collective-permute-start(bf16[832,512]{1,0:T(8,128)(2,1)} %collective-permute-done.61), channel_id=1, source_target_pairs={{0,6},{1,7},{2,0},{3,1},{4,2},{5,3},{6,4},{7,5},{8,14},{9,15},{10,... | collective-permute-start | bytes 2555912 | tf_op jit(solution)/shard_map/ppermute | solution.py:66
  353.0 38.8 %collective-permute-start.53 = (bf16[512,832]{0,1:T(8,128)(2,1)}, bf16[512,832]{0,1:T(8,128)(2,1)}, u32[]{:S(2)}, u32[]{:S(2)}) collective-permute-start(bf16[512,832]{0,1:T(8,128)(2,1)} %collective-permute-done.52), channel_id=1, source_target_pairs={{0,6},{1,7},{2,0},{3,1},{4,2},{5,3},{6,4},{7,5},{8,14},{9,15},{10,... | collective-permute-start | bytes 2555912 | tf_op jit(solution)/shard_map/ppermute | solution.py:66
  356.8 50.6 %collective-permute-start.57 = (bf16[512,832]{0,1:T(8,128)(2,1)}, bf16[512,832]{0,1:T(8,128)(2,1)}, u32[]{:S(2)}, u32[]{:S(2)}) collective-permute-start(bf16[512,832]{0,1:T(8,128)(2,1)} %collective-permute-done.56), channel_id=1, source_target_pairs={{0,6},{1,7},{2,0},{3,1},{4,2},{5,3},{6,4},{7,5},{8,14},{9,15},{10,... | collective-permute-start | bytes 2555912 | tf_op jit(solution)/shard_map/ppermute | solution.py:66
  371.3 39.9 %collective-permute-start.47 = (bf16[256,2048]{1,0:T(8,128)(2,1)}, bf16[256,2048]{1,0:T(8,128)(2,1)}, u32[]{:S(2)}, u32[]{:S(2)}) collective-permute-start(bf16[256,2048]{1,0:T(8,128)(2,1)} %get-tuple-element.1234), channel_id=1, source_target_pairs={{0,8},{8,0},{16,24},{24,16},{1,9},{9,1},{17,25},{25,17},{2,10},{10... | collective-permute-start | bytes 3145736 | tf_op jit(solution)/shard_map/ppermute | solution.py:61
  407.4 52.7 %collective-permute-start.54 = (bf16[512,832]{0,1:T(8,128)(2,1)}, bf16[512,832]{0,1:T(8,128)(2,1)S(1)}, u32[]{:S(2)}, u32[]{:S(2)}) collective-permute-start(bf16[512,832]{0,1:T(8,128)(2,1)} %collective-permute-done.53), channel_id=1, source_target_pairs={{0,6},{1,7},{2,0},{3,1},{4,2},{5,3},{6,4},{7,5},{8,14},{9,15},{10,... | collective-permute-start | bytes 2555912 | tf_op jit(solution)/shard_map/ppermute | solution.py:66
  411.2 36.7 %collective-permute-start.58 = (bf16[512,832]{0,1:T(8,128)(2,1)}, bf16[512,832]{0,1:T(8,128)(2,1)S(1)}, u32[]{:S(2)}, u32[]{:S(2)}) collective-permute-start(bf16[512,832]{0,1:T(8,128)(2,1)} %collective-permute-done.57), channel_id=1, source_target_pairs={{0,6},{1,7},{2,0},{3,1},{4,2},{5,3},{6,4},{7,5},{8,14},{9,15},{10,... | collective-permute-start | bytes 2555912 | tf_op jit(solution)/shard_map/ppermute | solution.py:66
  489.9 37.3 %collective-permute-start.117 = (bf16[832,512]{1,0:T(8,128)(2,1)S(1)}, bf16[832,512]{1,0:T(8,128)(2,1)S(1)}, u32[]{:S(2)}, u32[]{:S(2)}) collective-permute-start(bf16[832,512]{1,0:T(8,128)(2,1)S(1)} %slice.483), channel_id=1, source_target_pairs={{0,2},{1,3},{2,4},{3,5},{4,6},{5,7},{6,0},{7,1},{8,10},{9,11},{10,... | collective-permute-start | bytes 2555912 | tf_op jit(solution)/shard_map/ppermute | solution.py:66
  507.7 43.4 %collective-permute-start.109 = (bf16[512,832]{0,1:T(8,128)(2,1)}, bf16[512,832]{0,1:T(8,128)(2,1)S(1)}, u32[]{:S(2)}, u32[]{:S(2)}) collective-permute-start(bf16[512,832]{0,1:T(8,128)(2,1)} %slice.475), channel_id=1, source_target_pairs={{0,2},{1,3},{2,4},{3,5},{4,6},{5,7},{6,0},{7,1},{8,10},{9,11},{10,... | collective-permute-start | bytes 2555912 | tf_op jit(solution)/shard_map/ppermute | solution.py:66
  509.4 44.3 %collective-permute-start.113 = (bf16[512,832]{0,1:T(8,128)(2,1)}, bf16[512,832]{0,1:T(8,128)(2,1)S(1)}, u32[]{:S(2)}, u32[]{:S(2)}) collective-permute-start(bf16[512,832]{0,1:T(8,128)(2,1)} %slice.479), channel_id=1, source_target_pairs={{0,2},{1,3},{2,4},{3,5},{4,6},{5,7},{6,0},{7,1},{8,10},{9,11},{10,... | collective-permute-start | bytes 2555912 | tf_op jit(solution)/shard_map/ppermute | solution.py:66
  527.5 41.0 %collective-permute-start.118 = (bf16[832,512]{1,0:T(8,128)(2,1)S(1)}, bf16[832,512]{1,0:T(8,128)(2,1)}, u32[]{:S(2)}, u32[]{:S(2)}) collective-permute-start(bf16[832,512]{1,0:T(8,128)(2,1)S(1)} %add_convert_fusion.1), channel_id=1, source_target_pairs={{0,2},{1,3},{2,4},{3,5},{4,6},{5,7},{6,0},{7,1},{8,10},{9,11},{10,... | collective-permute-start | bytes 2555912 | tf_op jit(solution)/shard_map/ppermute | solution.py:66
  551.1 126.0 %collective-permute-start.76 = (bf16[1024,2048]{1,0:T(8,128)(2,1)}, bf16[1024,2048]{1,0:T(8,128)(2,1)}, u32[]{:S(2)}, u32[]{:S(2)}) collective-permute-start(bf16[1024,2048]{1,0:T(8,128)(2,1)} %slice.603), channel_id=1, source_target_pairs={{0,8},{8,0},{16,24},{24,16},{1,9},{9,1},{17,25},{25,17},{2,10},{10... | collective-permute-start | bytes 12582920 | tf_op jit(solution)/shard_map/ppermute | solution.py:61
  553.6 33.1 %collective-permute-start.110 = (bf16[512,832]{0,1:T(8,128)(2,1)}, bf16[512,832]{0,1:T(8,128)(2,1)S(1)}, u32[]{:S(2)}, u32[]{:S(2)}) collective-permute-start(bf16[512,832]{0,1:T(8,128)(2,1)} %add_convert_fusion.5), channel_id=1, source_target_pairs={{0,2},{1,3},{2,4},{3,5},{4,6},{5,7},{6,0},{7,1},{8,10},{9,11},{10,... | collective-permute-start | bytes 2555912 | tf_op jit(solution)/shard_map/ppermute | solution.py:66
  554.8 50.2 %collective-permute-start.114 = (bf16[512,832]{0,1:T(8,128)(2,1)}, bf16[512,832]{0,1:T(8,128)(2,1)}, u32[]{:S(2)}, u32[]{:S(2)}) collective-permute-start(bf16[512,832]{0,1:T(8,128)(2,1)} %add_convert_fusion.3), channel_id=1, source_target_pairs={{0,2},{1,3},{2,4},{3,5},{4,6},{5,7},{6,0},{7,1},{8,10},{9,11},{10,... | collective-permute-start | bytes 2555912 | tf_op jit(solution)/shard_map/ppermute | solution.py:66
  570.2 53.1 %collective-permute-start.119 = (bf16[832,512]{1,0:T(8,128)(2,1)S(1)}, bf16[832,512]{1,0:T(8,128)(2,1)}, u32[]{:S(2)}, u32[]{:S(2)}) collective-permute-start(bf16[832,512]{1,0:T(8,128)(2,1)S(1)} %add_convert_fusion), channel_id=1, source_target_pairs={{0,2},{1,3},{2,4},{3,5},{4,6},{5,7},{6,0},{7,1},{8,10},{9,11},{10,... | collective-permute-start | bytes 2555912 | tf_op jit(solution)/shard_map/ppermute | solution.py:66
  582.9 105.9 %collective-permute-start.63 = (bf16[1024,2048]{1,0:T(8,128)(2,1)}, bf16[1024,2048]{1,0:T(8,128)(2,1)}, u32[]{:S(2)}, u32[]{:S(2)}) collective-permute-start(bf16[1024,2048]{1,0:T(8,128)(2,1)} %slice.604), channel_id=1, source_target_pairs={{0,8},{8,0},{16,24},{24,16},{1,9},{9,1},{17,25},{25,17},{2,10},{10... | collective-permute-start | bytes 12582920 | tf_op jit(solution)/shard_map/ppermute | solution.py:61
  588.1 53.4 %collective-permute-start.111 = (bf16[512,832]{0,1:T(8,128)(2,1)S(1)}, bf16[512,832]{0,1:T(8,128)(2,1)S(1)}, u32[]{:S(2)}, u32[]{:S(2)}) collective-permute-start(bf16[512,832]{0,1:T(8,128)(2,1)S(1)} %add_convert_fusion.4), channel_id=1, source_target_pairs={{0,2},{1,3},{2,4},{3,5},{4,6},{5,7},{6,0},{7,1},{8,10},{9,11},{10,... | collective-permute-start | bytes 2555912 | tf_op jit(solution)/shard_map/ppermute | solution.py:66
  607.4 50.8 %collective-permute-start.115 = (bf16[512,832]{0,1:T(8,128)(2,1)}, bf16[512,832]{0,1:T(8,128)(2,1)}, u32[]{:S(2)}, u32[]{:S(2)}) collective-permute-start(bf16[512,832]{0,1:T(8,128)(2,1)} %add_convert_fusion.2), channel_id=1, source_target_pairs={{0,2},{1,3},{2,4},{3,5},{4,6},{5,7},{6,0},{7,1},{8,10},{9,11},{10,... | collective-permute-start | bytes 2555912 | tf_op jit(solution)/shard_map/ppermute | solution.py:66
  625.8 41.7 %collective-permute-start.120 = (bf16[832,256]{1,0:T(8,128)(2,1)}, bf16[832,256]{1,0:T(8,128)(2,1)}, u32[]{:S(2)}, u32[]{:S(2)}) collective-permute-start(bf16[832,256]{1,0:T(8,128)(2,1)} %select_convert_fusion), channel_id=1, source_target_pairs={{0,1},{1,0},{2,3},{3,2},{4,5},{5,4},{6,7},{7,6},{8,9},{9,8},{10,11... | collective-permute-start | bytes 1277960 | tf_op jit(solution)/shard_map/ppermute | solution.py:61
  706.9 33.0 %collective-permute-start.80 = (bf16[256,2048]{1,0:T(8,128)(2,1)}, bf16[256,2048]{1,0:T(8,128)(2,1)}, u32[]{:S(2)}, u32[]{:S(2)}) collective-permute-start(bf16[256,2048]{1,0:T(8,128)(2,1)} %pad_maximum_fusion.22), channel_id=1, source_target_pairs={{0,1},{1,0},{2,3},{3,2},{4,5},{5,4},{6,7},{7,6},{8,9},{9,8},{10,11... | collective-permute-start | bytes 3145736 | tf_op jit(solution)/shard_map/ppermute | solution.py:61
  708.6 31.4 %collective-permute-start.78 = (bf16[256,2048]{1,0:T(8,128)(2,1)}, bf16[256,2048]{1,0:T(8,128)(2,1)}, u32[]{:S(2)}, u32[]{:S(2)}) collective-permute-start(bf16[256,2048]{1,0:T(8,128)(2,1)} %pad_maximum_fusion.21), channel_id=1, source_target_pairs={{0,16},{8,24},{16,0},{24,8},{1,17},{9,25},{17,1},{25,9},{2,18},{10... | collective-permute-start | bytes 3145736 | tf_op jit(solution)/shard_map/ppermute | solution.py:61
  719.9 38.1 %collective-permute-start.67 = (bf16[256,2048]{1,0:T(8,128)(2,1)S(1)}, bf16[256,2048]{1,0:T(8,128)(2,1)S(1)}, u32[]{:S(2)}, u32[]{:S(2)}) collective-permute-start(bf16[256,2048]{1,0:T(8,128)(2,1)S(1)} %pad_maximum_fusion.19), channel_id=1, source_target_pairs={{0,1},{1,0},{2,3},{3,2},{4,5},{5,4},{6,7},{7,6},{8,9},{9,8},{10,11... | collective-permute-start | bytes 3145736 | tf_op jit(solution)/shard_map/ppermute | solution.py:61
  721.5 36.6 %collective-permute-start.65 = (bf16[256,2048]{1,0:T(8,128)(2,1)S(1)}, bf16[256,2048]{1,0:T(8,128)(2,1)S(1)}, u32[]{:S(2)}, u32[]{:S(2)}) collective-permute-start(bf16[256,2048]{1,0:T(8,128)(2,1)S(1)} %pad_maximum_fusion.18), channel_id=1, source_target_pairs={{0,16},{8,24},{16,0},{24,8},{1,17},{9,25},{17,1},{25,9},{2,18},{10... | collective-permute-start | bytes 3145736 | tf_op jit(solution)/shard_map/ppermute | solution.py:61
  853.8 26.8 %collective-permute-start.81 = (bf16[4,2,128,640]{2,1,3,0:T(2,128)(2,1)}, bf16[4,2,128,640]{2,1,3,0:T(2,128)(2,1)}, u32[]{:S(2)}, u32[]{:S(2)}) collective-permute-start(bf16[4,2,128,640]{2,1,3,0:T(2,128)(2,1)} %dynamic-slice_bitcast_fusion.1), channel_id=1, source_target_pairs={{0,1},{1,0},{2,3},{3,2},{4,5},{5,4},{6,7},{7,6},{8,9},{9,8},{10,11... | collective-permute-start | bytes 3932168 | tf_op jit(solution)/shard_map/ppermute | solution.py:61
  910.8 42.7 %collective-permute-start.99 = (bf16[4,40,1024]{2,1,0:T(8,128)(2,1)}, bf16[4,40,1024]{2,1,0:T(8,128)(2,1)}, u32[]{:S(2)}, u32[]{:S(2)}) collective-permute-start(bf16[4,40,1024]{2,1,0:T(8,128)(2,1)} %dynamic-slice_bitcast_fusion.9), channel_id=1, source_target_pairs={{0,1},{1,0},{2,3},{3,2},{4,5},{5,4},{6,7},{7,6},{8,9},{9,8},{10,11... | collective-permute-start | bytes 983048 | tf_op jit(solution)/shard_map/ppermute | solution.py:61
  915.7 40.8 %collective-permute-start.105 = (bf16[4,40,1024]{2,1,0:T(8,128)(2,1)}, bf16[4,40,1024]{2,1,0:T(8,128)(2,1)}, u32[]{:S(2)}, u32[]{:S(2)}) collective-permute-start(bf16[4,40,1024]{2,1,0:T(8,128)(2,1)} %dynamic-slice_bitcast_fusion.8), channel_id=1, source_target_pairs={{0,16},{8,24},{16,0},{24,8},{1,17},{9,25},{17,1},{25,9},{2,18},{10... | collective-permute-start | bytes 983048 | tf_op jit(solution)/shard_map/ppermute | solution.py:61
  948.0 29.0 %collective-permute-start.91 = (bf16[2,4,2,64,896]{4,3,1,0,2:T(8,128)(2,1)S(1)}, bf16[2,4,2,64,896]{4,3,1,0,2:T(8,128)(2,1)S(1)}, u32[]{:S(2)}, u32[]{:S(2)}) collective-permute-start(bf16[2,4,2,64,896]{4,3,1,0,2:T(8,128)(2,1)S(1)} %fusion.81), channel_id=1, source_target_pairs={{0,8},{8,0},{16,24},{24,16},{1,9},{9,1},{17,25},{25,17},{2,10},{10... | collective-permute-start | bytes 5505032 | tf_op jit(solution)/shard_map/ppermute | solution.py:61
  951.1 28.5 %collective-permute-start.85 = (bf16[2,4,2,64,1024]{4,3,1,2,0:T(8,128)(2,1)S(1)}, bf16[2,4,2,64,1024]{4,3,1,2,0:T(8,128)(2,1)S(1)}, u32[]{:S(2)}, u32[]{:S(2)}) collective-permute-start(bf16[2,4,2,64,1024]{4,3,1,2,0:T(8,128)(2,1)S(1)} %fusion.63), channel_id=1, source_target_pairs={{0,8},{8,0},{16,24},{24,16},{1,9},{9,1},{17,25},{25,17},{2,10},{10... | collective-permute-start | bytes 6291464 | tf_op jit(solution)/shard_map/ppermute | solution.py:61
  (242 other events, 2409.7 us)

commit v2 on v0

v2 whole, which is shorter than its diff:
```python
import functools

import jax
import jax.numpy as jnp
from jax import lax
from jax.experimental import pallas as pl
from jax.experimental.pallas import tpu as pltpu
from jax.sharding import Mesh
from jax.sharding import PartitionSpec as P

norm_eps = 1e-06
masked_score = -1e30


def head_sums(values, head_dim):
    width = values.shape[1]
    row = lax.broadcasted_iota(jnp.int32, (width, width), 0) // head_dim
    column = lax.broadcasted_iota(jnp.int32, (width, width), 1) // head_dim
    ones = jnp.where(row == column, 1.0, 0.0).astype(jnp.bfloat16)
    total = None
    for _ in range(3):
        part = values.astype(jnp.bfloat16)
        values = values - part.astype(jnp.float32)
        term = jnp.dot(part, ones, preferred_element_type=jnp.float32)
        total = term if total is None else total + term
    return total


def half_turn(values, head_dim):
    half = head_dim // 2
    width = values.shape[1]
    lane = lax.broadcasted_iota(jnp.int32, values.shape, 1) % head_dim
    ahead = pltpu.roll(values, width - half, 1)
    behind = pltpu.roll(values, half, 1)
    return jnp.where(lane < half, ahead, behind)


def signed(sine, head_dim):
    lane = lax.broadcasted_iota(jnp.int32, sine.shape, 1) % head_dim
    return jnp.where(lane < head_dim // 2, -sine, sine)


def head_norm_rotate(values, gain, cosine, sine, head_dim):
    scale = lax.rsqrt(head_sums(values * values, head_dim) / head_dim + norm_eps)
    normed = values * scale * gain
    return normed * cosine + half_turn(normed, head_dim) * signed(sine, head_dim)


def head_norm_rotate_back(grad, values, gain, cosine, sine, head_dim):
    grad = grad * cosine - half_turn(grad * sine, head_dim) * signed(
        jnp.ones_like(sine), head_dim
    )
    scale = lax.rsqrt(head_sums(values * values, head_dim) / head_dim + norm_eps)
    weighted = grad * gain
    inner = head_sums(weighted * values, head_dim)
    back = scale * weighted - values * (scale * scale * scale) * inner / head_dim
    return back, grad * values * scale


def wide(table, count):
    return jnp.concatenate([table] * count, axis=1)


def fill_mask(pieces, row, base_ref, segq_ref, segk_ref, mask_ref):
    size = segq_ref.shape[1]
    seg_query = segq_ref[pl.ds(row, 1), :]
    query_at = base_ref[0] + lax.broadcasted_iota(jnp.int32, (size, size), 1)
    for piece in range(pieces):
        count = segk_ref.shape[0] // segq_ref.shape[0]
        line = segk_ref[pl.ds(row * count + base_ref[1 + piece] // size, 1), :]
        seg_key = jnp.broadcast_to(line, (size, size)).astype(jnp.float32).T
        key_at = base_ref[1 + piece] + lax.broadcasted_iota(jnp.int32, (size, size), 0)
        allowed = (key_at <= query_at) & (
            seg_key == jnp.broadcast_to(seg_query, (size, size)).astype(jnp.float32)
        )
        mask_ref[piece * size : (piece + 1) * size, :] = jnp.where(allowed, 0.0, masked_score)


def attend_kernel(pieces, heads_kv, grouping, base_ref, q_ref, segq_ref, segk_ref, *refs):
    kv_refs = refs[:pieces]
    out_ref, log_ref, q_heads, k_heads, v_heads, mask_ref = refs[pieces:]
    row, group = pl.program_id(0), pl.program_id(1)
    size, head_dim = segq_ref.shape[1], k_heads.shape[2]

    @pl.when(group == 0)
    def _():
        for head in range(heads_kv):
            for j in range(grouping):
                at = (head * grouping + j) * head_dim
                q_heads[head, j * size : (j + 1) * size, :] = q_ref[:, at : at + head_dim]
            for piece in range(pieces):
                rows = slice(piece * size, (piece + 1) * size)
                at = head * head_dim
                k_heads[head, rows, :] = kv_refs[piece][:, at : at + head_dim]
                at += heads_kv * head_dim
                v_heads[head, rows, :] = kv_refs[piece][:, at : at + head_dim]
        fill_mask(pieces, row, base_ref, segq_ref, segk_ref, mask_ref)

    together = grouping if pieces <= 8 else 1
    turned = []
    for first in range(0, grouping, together):
        rows = slice(first * size, (first + together) * size)
        scores = lax.dot_general(
            k_heads[group], q_heads[group, rows, :], NT, preferred_element_type=jnp.float32
        ) + wide(mask_ref[...], together)
        top = jnp.max(scores, axis=0, keepdims=True)
        probs = jnp.exp(scores - top)
        total = jnp.sum(probs, axis=0, keepdims=True)
        probs_b = (probs * (1.0 / total)).astype(jnp.bfloat16)
        mixed = lax.dot_general(
            v_heads[group], probs_b, (((0,), (0,)), ((), ())), preferred_element_type=jnp.float32
        )
        turned += [mixed[:, j * size : (j + 1) * size].T for j in range(together)]
        log_ref[:, rows] = top + jnp.log(total)
    out_ref[...] = jnp.concatenate(turned, axis=1).astype(jnp.bfloat16)


def attend_call(heads_kv, grouping, bases, query_b, seg_here, seg_all, kv_pieces):
    pieces = len(kv_pieces)
    rows, size = seg_here.shape
    head_dim = kv_pieces[0].shape[1] // (2 * heads_kv)
    block = grouping * head_dim
    width = heads_kv * block
    keys = pieces * size
    row_block = lambda w: pl.BlockSpec((size, w), lambda r, g: (r, 0))
    whole = lambda a: pl.BlockSpec(a.shape, lambda r, g: (0,) * a.ndim)
    low, full = jnp.bfloat16, jnp.float32
    return pl.pallas_call(
        functools.partial(attend_kernel, pieces, heads_kv, grouping),
        grid=(rows, heads_kv),
        out_shape=[
            jax.ShapeDtypeStruct((rows * size, width), low),
            jax.ShapeDtypeStruct((rows, heads_kv, 1, grouping * size), full),
        ],
        in_specs=[
            pl.BlockSpec(memory_space=pltpu.SMEM),
            row_block(width),
            whole(seg_here),
            whole(seg_all),
        ]
        + [row_block(2 * heads_kv * head_dim)] * pieces,
        out_specs=[
            pl.BlockSpec((size, block), lambda r, g: (r, g)),
            pl.BlockSpec((None, None, 1, grouping * size), lambda r, g: (r, g, 0, 0)),
        ],
        scratch_shapes=[
            pltpu.VMEM((heads_kv, grouping * size, head_dim), low),
            pltpu.VMEM((heads_kv, keys, head_dim), low),
            pltpu.VMEM((heads_kv, keys, head_dim), low),
            pltpu.VMEM((keys, size), full),
        ],
        compiler_params=pltpu.CompilerParams(vmem_limit_bytes=60 * 1024 * 1024),
        cost_estimate=pl.CostEstimate(
            flops=4 * rows * size * keys * width * 4,
            bytes_accessed=4 * rows * size * width + 4 * rows * keys * heads_kv * head_dim,
            transcendentals=rows * heads_kv * grouping * size * keys,
        ),
    )(bases, query_b, seg_here, seg_all, *kv_pieces)


def attend_back_kernel(
    pieces,
    heads_kv,
    grouping,
    base_ref,
    q_ref,
    do_ref,
    segq_ref,
    segk_ref,
    log_ref,
    pre_ref,
    gain_ref,
    cos_ref,
    sin_ref,
    *refs,
):
    kv_refs = refs[:pieces]
    dq_ref, gain_rows_ref = refs[pieces : pieces + 2]
    dkv_refs = refs[pieces + 2 : 2 * pieces + 2]
    q_heads, do_heads, k_heads, v_heads, dk_heads, dv_heads, mask_ref = refs[2 * pieces + 2 :]
    row, group = pl.program_id(0), pl.program_id(1)
    size, head_dim = segq_ref.shape[1], k_heads.shape[2]

    @pl.when(group == 0)
    def _():
        for head in range(heads_kv):
            for j in range(grouping):
                at = (head * grouping + j) * head_dim
                q_heads[head, j * size : (j + 1) * size, :] = q_ref[:, at : at + head_dim]
                do_heads[head, j * size : (j + 1) * size, :] = do_ref[:, at : at + head_dim]
            for piece in range(pieces):
                rows = slice(piece * size, (piece + 1) * size)
                at = head * head_dim
                k_heads[head, rows, :] = kv_refs[piece][:, at : at + head_dim]
                at += heads_kv * head_dim
                v_heads[head, rows, :] = kv_refs[piece][:, at : at + head_dim]
        fill_mask(pieces, row, base_ref, segq_ref, segk_ref, mask_ref)

    together = grouping if pieces <= 8 else 1
    turned = []
    for first in range(0, grouping, together):
        rows = slice(first * size, (first + together) * size)
        queries, grads = q_heads[group, rows, :], do_heads[group, rows, :]
        scores = lax.dot_general(
            k_heads[group], queries, NT, preferred_element_type=jnp.float32
        ) + wide(mask_ref[...], together)
        probs = jnp.exp(scores - log_ref[:, rows])
        grad_probs = lax.dot_general(
            v_heads[group], grads, NT, preferred_element_type=jnp.float32
        )
        grad_values = jnp.dot(
            probs.astype(jnp.bfloat16), grads, preferred_element_type=jnp.float32
        )
        delta = jnp.sum(probs * grad_probs, axis=0, keepdims=True)
        grad_scores = (probs * (grad_probs - delta)).astype(jnp.bfloat16)
        grad_keys = jnp.dot(grad_scores, queries, preferred_element_type=jnp.float32)
        if first:
            grad_values = grad_values + dv_heads[group].astype(jnp.float32)
            grad_keys = grad_keys + dk_heads[group].astype(jnp.float32)
        dv_heads[group] = grad_values.astype(dv_heads.dtype)
        dk_heads[group] = grad_keys.astype(dk_heads.dtype)
        mixed = lax.dot_general(
            k_heads[group], grad_scores, (((0,), (0,)), ((), ())), preferred_element_type=jnp.float32
        ) * (head_dim**-0.5)
        turned += [mixed[:, j * size : (j + 1) * size].T for j in range(together)]
    grad_query = jnp.concatenate(turned, axis=1)
    copies = grad_query.shape[1] // cos_ref.shape[1]
    back, gain_rows = head_norm_rotate_back(
        grad_query,
        pre_ref[...],
        gain_ref[...],
        wide(cos_ref[...], copies),
        wide(sin_ref[...], copies),
        head_dim,
    )
    dq_ref[...] = back.astype(jnp.bfloat16)
    gain_rows_ref[...] = jnp.sum(gain_rows, axis=0, keepdims=True)

    @pl.when(group == heads_kv - 1)
    def _():
        for piece in range(pieces):
            rows = slice(piece * size, (piece + 1) * size)
            dkv_refs[piece][...] = jnp.concatenate(
                [dk_heads[head, rows, :] for head in range(heads_kv)]
                + [dv_heads[head, rows, :] for head in range(heads_kv)],
                axis=1,
            )


def attend_back_call(
    heads_kv, grouping, bases, query_b, grad_att, seg_here, seg_all, logs, query_pre, gain, cosine, sine, kv_pieces
):
    pieces = len(kv_pieces)
    rows, size = seg_here.shape
    head_dim = kv_pieces[0].shape[1] // (2 * heads_kv)
    block = grouping * head_dim
    width = heads_kv * block
    keys = pieces * size
    kv_width = 2 * heads_kv * head_dim
    row_block = lambda w: pl.BlockSpec((size, w), lambda r, g: (r, 0))
    column_block = pl.BlockSpec((size, block), lambda r, g: (r, g))
    whole = lambda a: pl.BlockSpec(a.shape, lambda r, g: (0,) * a.ndim)
    low, full = jnp.bfloat16, jnp.float32
    heads = lambda n, t: pltpu.VMEM((heads_kv, n, head_dim), t)
    return pl.pallas_call(
        functools.partial(attend_back_kernel, pieces, heads_kv, grouping),
        grid=(rows, heads_kv),
        out_shape=[
            jax.ShapeDtypeStruct((rows * size, width), low),
            jax.ShapeDtypeStruct((rows, heads_kv, 1, block), full),
        ]
        + [jax.ShapeDtypeStruct((rows * size, kv_width), low)] * pieces,
        in_specs=[
            pl.BlockSpec(memory_space=pltpu.SMEM),
            row_block(width),
            row_block(width),
            whole(seg_here),
            whole(seg_all),
            pl.BlockSpec((None, None, 1, grouping * size), lambda r, g: (r, g, 0, 0)),
            column_block,
            whole(gain),
            row_block(cosine.shape[1]),
            row_block(sine.shape[1]),
        ]
        + [row_block(kv_width)] * pieces,
        out_specs=[
            column_block,
            pl.BlockSpec((None, None, 1, block), lambda r, g: (r, g, 0, 0)),
        ]
        + [row_block(kv_width)] * pieces,
        scratch_shapes=[
            heads(grouping * size, low),
            heads(grouping * size, low),
            heads(keys, low),
            heads(keys, low),
            heads(keys, low),
            heads(keys, low),
            pltpu.VMEM((keys, size), full),
        ],
        compiler_params=pltpu.CompilerParams(vmem_limit_bytes=60 * 1024 * 1024),
        cost_estimate=pl.CostEstimate(
            flops=10 * rows * size * keys * width * 4,
            bytes_accessed=8 * rows * size * width + 8 * rows * keys * heads_kv * head_dim,
            transcendentals=rows * heads_kv * grouping * size * keys,
        ),
    )(bases, query_b, grad_att, seg_here, seg_all, logs, query_pre, gain, cosine, sine, *kv_pieces)


def place_copies(spots, pieces, place_ref, w_ref, sems):
    x_at, core_at, z_at, y_at = [place_ref[i] for i in range(4)]
    copies = []
    for index, (dx, dy, dc, column) in enumerate(spots):
        piece = pieces[index]
        planes, size, width = piece.shape
        for t in range(planes):
            row = (x_at + dx - 2 * x_at * dx) * 2 + (core_at + dc - 2 * core_at * dc)
            row = (row * planes + lax.rem(z_at + t, planes)) * 2 + (y_at + dy - 2 * y_at * dy)
            start = pl.multiple_of(row * size, size)
            copies.append(
                pltpu.make_async_copy(
                    piece.at[t],
                    w_ref.at[pl.ds(start, size), column : column + width],
                    sems.at[index, t],
                )
            )
    return copies


def project_kernel(width_q, head_dim, spots, place_ref, x_ref, gain_ref, gq_ref, gk_ref, cos_ref, sin_ref, *refs):
    pieces, outs, (w_ref, sems) = refs[: len(spots)], refs[len(spots) : -2], refs[-2:]
    copies_in = place_copies(spots, pieces, place_ref, w_ref, sems)
    for copy in copies_in:
        copy.start()
    normed_ref, pre_ref, kpre_ref, q_ref, kv_ref = outs
    values = x_ref[...].astype(jnp.float32)
    scale = lax.rsqrt(jnp.mean(values * values, axis=1, keepdims=True) + norm_eps)
    normed_ref[...] = (values * scale * gain_ref[...]).astype(jnp.bfloat16)
    block = 256
    cosine, sine = cos_ref[...], sin_ref[...]
    for copy in copies_in:
        copy.wait()
    total = w_ref.shape[1]
    for first in range(0, width_q, block):
        pre = jnp.dot(
            normed_ref[...], w_ref[:, first : first + block], preferred_element_type=jnp.float32
        )
        pre_ref[:, first : first + block] = pre
        copies = block // cosine.shape[1]
        rotated = head_norm_rotate(
            pre, gq_ref[...], wide(cosine, copies), wide(sine, copies), head_dim
        )
        q_ref[:, first : first + block] = (rotated * (head_dim**-0.5)).astype(jnp.bfloat16)
    pre = jnp.dot(normed_ref[...], w_ref[:, width_q:], preferred_element_type=jnp.float32)
    kpre_ref[...] = pre
    copies = pre.shape[1] // cosine.shape[1]
    rotated = head_norm_rotate(pre, gk_ref[...], wide(cosine, copies), wide(sine, copies), head_dim)
    lane = lax.broadcasted_iota(jnp.int32, pre.shape, 1)
    kv_ref[...] = jnp.where(lane < pre.shape[1] // 2, rotated, pre).astype(jnp.bfloat16)


def project_call(width_q, head_dim, total, place, x, gain, gain_q, gain_k, cosine, sine, spots, pieces):
    tokens, features = x.shape
    kv = total - width_q
    low, full = jnp.bfloat16, jnp.float32
    vm = pl.BlockSpec(memory_space=pltpu.VMEM)
    return pl.pallas_call(
        functools.partial(project_kernel, width_q, head_dim, spots),
        out_shape=[
            jax.ShapeDtypeStruct((tokens, features), low),
            jax.ShapeDtypeStruct((tokens, width_q), full),
            jax.ShapeDtypeStruct((tokens, kv), full),
            jax.ShapeDtypeStruct((tokens, width_q), low),
            jax.ShapeDtypeStruct((tokens, kv), low),
        ],
        in_specs=[pl.BlockSpec(memory_space=pltpu.SMEM)]
        + [vm] * 6
        + [pl.BlockSpec(memory_space=pl.ANY)] * len(pieces),
        out_specs=[vm] * 5,
        scratch_shapes=[
            pltpu.VMEM((features, total), low),
            pltpu.SemaphoreType.DMA((len(pieces), pieces[0].shape[0])),
        ],
        compiler_params=pltpu.CompilerParams(vmem_limit_bytes=60 * 1024 * 1024),
        cost_estimate=pl.CostEstimate(
            flops=2 * tokens * features * total,
            bytes_accessed=2 * features * total + 10 * tokens * features,
            transcendentals=tokens,
        ),
    )(place, x, gain, gain_q, gain_k, cosine, sine, *pieces)


def keys_back_kernel(head_dim, grad_ref, kpre_ref, gk_ref, cos_ref, sin_ref, out_ref, gain_rows_ref):
    grad = grad_ref[...]
    copies = grad.shape[1] // cos_ref.shape[1]
    back, gain_rows = head_norm_rotate_back(
        grad,
        kpre_ref[...],
        gk_ref[...],
        wide(cos_ref[...], copies),
        wide(sin_ref[...], copies),
        head_dim,
    )
    lane = lax.broadcasted_iota(jnp.int32, grad.shape, 1)
    out_ref[...] = jnp.where(lane < grad.shape[1] // 2, back, grad).astype(jnp.bfloat16)
    gain_rows_ref[...] = jnp.sum(gain_rows, axis=0, keepdims=True)


def keys_back_call(head_dim, grad, kpre, gain_k, cosine, sine):
    vm = pl.BlockSpec(memory_space=pltpu.VMEM)
    return pl.pallas_call(
        functools.partial(keys_back_kernel, head_dim),
        out_shape=[
            jax.ShapeDtypeStruct(grad.shape, jnp.bfloat16),
            jax.ShapeDtypeStruct((1, grad.shape[1]), jnp.float32),
        ],
        in_specs=[vm] * 5,
        out_specs=[vm] * 2,
        compiler_params=pltpu.CompilerParams(vmem_limit_bytes=60 * 1024 * 1024),
    )(grad, kpre, gain_k, cosine, sine)


def input_kernel(spots, place_ref, g_ref, x_ref, gain_ref, mid_ref, *refs):
    pieces = refs[: len(spots)]
    out_ref, gain_rows_ref, w_ref, sems = refs[len(spots) :]
    copies = place_copies(spots, pieces, place_ref, w_ref, sems)
    for copy in copies:
        copy.start()
    values = x_ref[...].astype(jnp.float32)
    scale = lax.rsqrt(jnp.mean(values * values, axis=1, keepdims=True) + norm_eps)
    for copy in copies:
        copy.wait()
    grad = lax.dot_general(
        g_ref[...], w_ref[...], (((1,), (1,)), ((), ())), preferred_element_type=jnp.float32
    )
    weighted = grad * gain_ref[...]
    inner = jnp.sum(weighted * values, axis=1, keepdims=True)
    back = scale * weighted - values * (scale * scale * scale) * inner / values.shape[1]
    out_ref[...] = mid_ref[...] + back
    gain_rows_ref[...] = jnp.sum(grad * values * scale, axis=0, keepdims=True)


def input_call(place, grad_qkv, x, gain, grad_middle, spots, pieces):
    tokens, features = x.shape
    total = grad_qkv.shape[1]
    vm = pl.BlockSpec(memory_space=pltpu.VMEM)
    return pl.pallas_call(
        functools.partial(input_kernel, spots),
        out_shape=[
            jax.ShapeDtypeStruct((tokens, features), jnp.float32),
            jax.ShapeDtypeStruct((1, features), jnp.float32),
        ],
        in_specs=[pl.BlockSpec(memory_space=pltpu.SMEM)]
        + [vm] * 4
        + [pl.BlockSpec(memory_space=pl.ANY)] * len(pieces),
        out_specs=[vm] * 2,
        scratch_shapes=[
            pltpu.VMEM((features, total), jnp.bfloat16),
            pltpu.SemaphoreType.DMA((len(pieces), pieces[0].shape[0])),
        ],
        compiler_params=pltpu.CompilerParams(vmem_limit_bytes=60 * 1024 * 1024),
        cost_estimate=pl.CostEstimate(
            flops=2 * tokens * features * total,
            bytes_accessed=2 * features * total + 10 * tokens * features,
            transcendentals=tokens,
        ),
    )(place, grad_qkv, x, gain, grad_middle, *pieces)

ANY = pl.BlockSpec(memory_space=pl.ANY)
VMEM = pl.BlockSpec(memory_space=pltpu.VMEM)
SMEM = pl.BlockSpec(memory_space=pltpu.SMEM)
NT = (((1,), (1,)), ((), ()))


def params():
    return pltpu.CompilerParams(vmem_limit_bytes=60 * 1024 * 1024)


def cuts(total, step):
    edges = list(range(0, total - step // 2, step)) + [total]
    return list(zip(edges[:-1], edges[1:]))


def weight_copies(planes, gathered, which, target, sems):
    size = gathered.shape[2]
    return [
        pltpu.make_async_copy(
            gathered.at[core * planes + z, which],
            target.at[pl.ds((2 * z + core) * size, size)],
            sems.at[core * planes + z],
        )
        for core in range(2)
        for z in range(planes)
    ]


def ffn_kernel(planes, blocks, chained, place_ref, *refs):
    refs = list(refs)
    take = lambda n: [refs.pop(0) for _ in range(n)]
    x_refs, c_refs = take(blocks), take(blocks)
    before = take(blocks) if chained else None
    (gathered,) = take(1)
    outs = take(4 * blocks)
    weights, sems = refs
    copies = [
        weight_copies(planes, gathered, which, weights.at[which], sems.at[which])
        for which in range(3)
    ]
    for group in copies:
        for copy in group:
            copy.start()
    waiting = list(copies)

    def arrive():
        if waiting:
            for copy in waiting.pop(0):
                copy.wait()

    features, units = weights.shape[1:]
    for block in range(blocks):
        hidden_ref, dgate_ref, dup_ref, dx_ref = outs[4 * block : 4 * block + 4]
        for first, last in cuts(units, 512):
            arrive()
            gate = jnp.dot(
                x_refs[block][...], weights[0, :, first:last], preferred_element_type=jnp.float32
            )
            arrive()
            up = jnp.dot(
                x_refs[block][...], weights[1, :, first:last], preferred_element_type=jnp.float32
            )
            arrive()
            dh = jnp.dot(
                c_refs[block][...], weights[2, :, first:last], preferred_element_type=jnp.float32
            )
            sigma = 1.0 / (1.0 + jnp.exp(-gate))
            silu = gate * sigma
            hidden_ref[:, first:last] = (silu * up).astype(jnp.bfloat16)
            dup_ref[:, first:last] = (dh * silu).astype(jnp.bfloat16)
            dgate_ref[:, first:last] = (dh * up * (sigma + silu * (1.0 - sigma))).astype(
                jnp.bfloat16
            )
        for first, last in cuts(features, 512):
            dx = lax.dot_general(
                dgate_ref[...], weights[0, first:last], NT, preferred_element_type=jnp.float32
            ) + lax.dot_general(
                dup_ref[...], weights[1, first:last], NT, preferred_element_type=jnp.float32
            )
            if chained:
                dx = dx + before[block][:, first:last].astype(jnp.float32)
            dx_ref[:, first:last] = dx.astype(jnp.bfloat16)


def ffn_call(planes, place, xs, cs, gathered, before=None):
    blocks = len(xs)
    tokens, features = xs[0].shape
    units = gathered.shape[3]
    low = jnp.bfloat16
    one = [jax.ShapeDtypeStruct((tokens, units), low)] * 3 + [
        jax.ShapeDtypeStruct((tokens, features), low)
    ]
    chained = before is not None
    operands = [*xs, *cs, *(before or [])]
    return pl.pallas_call(
        functools.partial(ffn_kernel, planes, blocks, chained),
        out_shape=one * blocks,
        in_specs=[SMEM] + [VMEM] * len(operands) + [ANY],
        out_specs=[VMEM] * (4 * blocks),
        scratch_shapes=[
            pltpu.VMEM((3, features, units), low),
            pltpu.SemaphoreType.DMA((3, 2 * planes)),
        ],
        compiler_params=params(),
        cost_estimate=pl.CostEstimate(
            flops=10 * blocks * tokens * features * units,
            bytes_accessed=6 * features * units + 8 * blocks * tokens * features,
            transcendentals=blocks * tokens * units,
        ),
    )(place, *operands, gathered)


def weight_grad_kernel(blocks, place_ref, *refs):
    a_refs = [refs[:blocks], refs[blocks : 2 * blocks]]
    b_refs = [refs[(2 + i) * blocks : (3 + i) * blocks] for i in range(3)]
    own_ref, other_ref, turned = refs[5 * blocks :]
    size, units = own_ref.shape[1:]
    tokens = a_refs[0][0].shape[0]
    core_at = place_ref[1]
    for kind in range(2):
        for block in range(blocks):
            turned[kind, :, block * tokens : (block + 1) * tokens] = a_refs[kind][block][...].T
    for out_ref, half in ((other_ref, 1 - core_at), (own_ref, core_at)):
        rows = pl.ds(pl.multiple_of(half * size, size), size)
        for which in range(3):
            for first, last in cuts(units, 512):
                total = None
                for block in range(blocks):
                    part = jnp.dot(
                        turned[which // 2, rows, block * tokens : (block + 1) * tokens],
                        b_refs[which][block][:, first:last],
                        preferred_element_type=jnp.float32,
                    )
                    total = part if total is None else total + part
                out_ref[which, :, first:last] = total.astype(jnp.bfloat16)


def weight_grad_call(planes, place, xs, cs, dgates, dups, hiddens):
    blocks = len(xs)
    tokens, features = xs[0].shape
    units = dgates[0].shape[1]
    size = features // (2 * planes)
    out = jax.ShapeDtypeStruct((planes, 3, size, units), jnp.bfloat16)
    column = pl.BlockSpec((tokens, 2 * size), lambda t, place: (0, t))
    return pl.pallas_call(
        functools.partial(weight_grad_kernel, blocks),
        out_shape=[out, out],
        grid_spec=pltpu.PrefetchScalarGridSpec(
            num_scalar_prefetch=1,
            grid=(planes,),
            in_specs=[column] * (2 * blocks)
            + [pl.BlockSpec((tokens, units), lambda t, place: (0, 0))] * (3 * blocks),
            out_specs=[pl.BlockSpec((None, 3, size, units), lambda t, place: (t, 0, 0, 0))] * 2,
            scratch_shapes=[pltpu.VMEM((2, 2 * size, blocks * tokens), jnp.bfloat16)],
        ),
        compiler_params=params(),
        cost_estimate=pl.CostEstimate(
            flops=6 * blocks * tokens * features * units,
            bytes_accessed=6 * blocks * tokens * units + 6 * features * units,
            transcendentals=0,
        ),
    )(place, *xs, *cs, *dgates, *dups, *hiddens)


def down_kernel(planes, blocks, parts, place_ref, *refs):
    refs = list(refs)
    take = lambda n: [refs.pop(0) for _ in range(n)]
    h_refs = [take(blocks) for _ in range(parts)]
    gathered = take(parts)
    outs = take(blocks)
    weights = take(parts)
    (sems,) = refs
    copies = []
    for part in range(parts):
        copies += weight_copies(planes, gathered[part], 2, weights[part], sems.at[part])
    for copy in copies:
        copy.start()
    for copy in copies:
        copy.wait()
    for block in range(blocks):
        for first, last in cuts(weights[0].shape[0], 512):
            total = None
            for part in range(parts):
                term = lax.dot_general(
                    h_refs[part][block][...],
                    weights[part][first:last],
                    NT,
                    preferred_element_type=jnp.float32,
                )
                total = term if total is None else total + term
            outs[block][:, first:last] = total.astype(jnp.bfloat16)


def down_call(planes, place, hidden_parts, gathered_parts):
    parts, blocks = len(hidden_parts), len(hidden_parts[0])
    tokens = hidden_parts[0][0].shape[0]
    size = gathered_parts[0].shape[2]
    features = 2 * planes * size
    units = [h[0].shape[1] for h in hidden_parts]
    return pl.pallas_call(
        functools.partial(down_kernel, planes, blocks, parts),
        out_shape=[jax.ShapeDtypeStruct((tokens, features), jnp.bfloat16)] * blocks,
        in_specs=[SMEM] + [VMEM] * (parts * blocks) + [ANY] * parts,
        out_specs=[VMEM] * blocks,
        scratch_shapes=[pltpu.VMEM((features, n), jnp.bfloat16) for n in units]
        + [pltpu.SemaphoreType.DMA((parts, 2 * planes))],
        compiler_params=params(),
        cost_estimate=pl.CostEstimate(
            flops=2 * blocks * tokens * features * sum(units),
            bytes_accessed=2 * features * sum(units) + 8 * blocks * tokens * features,
            transcendentals=0,
        ),
    )(
        place,
        *[h for part in hidden_parts for h in part],
        *gathered_parts,
    )


def rms_apply(values, gain_vec):
    row_scale = lax.rsqrt(jnp.mean(values * values, axis=-1, keepdims=True) + norm_eps)
    return values * row_scale * gain_vec


def rms_back(values, gain_vec, grad_in):
    row_scale = lax.rsqrt(jnp.mean(values * values, axis=-1, keepdims=True) + norm_eps)
    weighted = grad_in * gain_vec
    inner_sum = jnp.sum(weighted * values, axis=-1, keepdims=True)
    grad_values = (
        row_scale * weighted
        - values * (row_scale * row_scale * row_scale) * inner_sum / values.shape[-1]
    )
    return (grad_values, grad_in * values * row_scale)


def rotary_tables(positions, head_dim):
    half_dim = head_dim // 2
    frequencies = 10000.0 ** (-2.0 * jnp.arange(half_dim).astype(jnp.float32) / head_dim)
    angles = positions.astype(jnp.float32)[..., None] * frequencies
    angles = jnp.concatenate([angles, angles], axis=-1)
    return (jnp.cos(angles), jnp.sin(angles))


def times_transposed(left, right):
    return lax.dot_general(
        left, right, (((1,), (1,)), ((), ())), preferred_element_type=jnp.float32
    )


def transposed_times(left, right):
    return lax.dot_general(
        left, right, (((0,), (0,)), ((), ())), preferred_element_type=jnp.float32
    )


def swap(values, axis_name, bit):
    count = lax.axis_size(axis_name)
    return lax.ppermute(values, axis_name, [(i, i ^ bit) for i in range(count)])


def ring(values, shift):
    count = lax.axis_size("z")
    return lax.ppermute(values, "z", [(i, (i + shift) % count) for i in range(count)])


def core_swap(values):
    return swap(values, "core", 1)


def x_swap(values):
    return swap(values, "x", 1)


def y_swap(values):
    return swap(values, "y", 1)


def sum_over(values, names):
    for axis_name in names:
        bit = 1
        while bit < lax.axis_size(axis_name):
            values = values + swap(values, axis_name, bit)
            bit *= 2
    return values


def places():
    return tuple(lax.axis_index(name) for name in ("x", "core", "z", "y"))


def in_order(first, other, bit, axis):
    return jnp.where(
        bit == 0, jnp.stack([first, other], axis=axis), jnp.stack([other, first], axis=axis)
    )


def corner(values):
    moved = lax.ppermute(values, ("core", "y"), [(1, 2), (2, 1)])
    return jnp.where(lax.axis_index("core") == lax.axis_index("y"), values, moved)


def chain(values, shift):
    count = lax.axis_size("z")
    moves = [(i, i + shift) for i in range(count) if 0 <= i + shift < count]
    return lax.ppermute(values, "z", moves)


def hold(values, *others):
    return lax.optimization_barrier((values, *others))[0]


def together(*values):
    return lax.optimization_barrier(values)


def ring_gather(values):
    pieces = [values]
    for _ in range(lax.axis_size("z") - 1):
        pieces.append(ring(pieces[-1], -1))
    return pieces


def direct_gather(values):
    return [values] + [ring(values, -t) for t in range(1, lax.axis_size("z"))]


def ring_scatter(pieces):
    count = len(pieces)
    moving = None
    for step in range(1, count):
        block = pieces[count - step]
        if moving is not None:
            block = (block.astype(jnp.float32) + moving.astype(jnp.float32)).astype(jnp.bfloat16)
        moving = ring(block, 1)
    return pieces[0].astype(jnp.float32) + moving.astype(jnp.float32)


def turn(values, start):
    count = values.shape[0]
    return lax.dynamic_slice_in_dim(jnp.concatenate([values, values], axis=0), start, count, 0)


def turn_columns(values, start, width):
    return lax.dynamic_slice_in_dim(
        jnp.concatenate([values, values], axis=1), start * width, values.shape[1], 1
    )


def pick(values, bit, axis):
    return (
        lax.dynamic_index_in_dim(values, bit, axis, keepdims=False),
        lax.dynamic_index_in_dim(values, 1 - bit, axis, keepdims=False),
    )


def add_low(left, right):
    return (left.astype(jnp.float32) + right.astype(jnp.float32)).astype(jnp.bfloat16)


def gather_tokens(values):
    half = values.shape[1] // 2
    from_x = x_swap(values)
    from_y = y_swap(values)
    from_xy = jnp.concatenate([y_swap(from_x[:, :half]), x_swap(from_y[:, half:])], axis=1)
    return [values, from_x, from_y, from_xy]


def scatter_tokens(blocks):
    own, to_x, to_y, to_xy = blocks
    half = own.shape[1] // 2
    via_x = x_swap(to_xy[:, :half])
    via_y = y_swap(to_xy[:, half:])
    to_y = jnp.concatenate([add_low(to_y[:, :half], via_x), to_y[:, half:]], axis=1)
    to_x = jnp.concatenate([to_x[:, :half], add_low(to_x[:, half:], via_y)], axis=1)
    return (
        own.astype(jnp.float32)
        + x_swap(to_x).astype(jnp.float32)
        + y_swap(to_y).astype(jnp.float32)
    )


def local(
    inputs,
    cotangent,
    positions,
    segment_ids,
    w_query,
    w_key,
    w_value,
    w_out,
    w_gate,
    w_up,
    w_down,
    gain_attn,
    gain_query,
    gain_key,
    gain_ffn,
):
    rows_here, seg_tok, feature_count = inputs.shape
    tokens_here = rows_here * seg_tok
    head_dim = gain_query.shape[0]
    heads_query = w_query.shape[1] // head_dim
    heads_kv = w_key.shape[1] // head_dim
    grouping = heads_query // heads_kv
    planes = lax.axis_size("z")
    rows_count, seq_count = 4, 2 * planes
    row_len = seg_tok * seq_count
    x_at, core_at, z_at, y_at = places()
    seq_place = 2 * z_at + y_at
    row_place = 2 * x_at + core_at
    device = row_place * seq_count + seq_place
    place = jnp.stack([x_at, core_at, z_at, y_at]).astype(jnp.int32)
    gain_size = gain_attn.shape[0]
    width_q, width_k = w_query.shape[1], w_key.shape[1]
    low = jnp.bfloat16

    shared = jnp.zeros((2 * feature_count + rows_count * rows_here * row_len,), jnp.float32)

    def put(shared, values, start):
        return lax.dynamic_update_slice_in_dim(shared, values.astype(jnp.float32), start, 0)

    shared = put(shared, gain_attn, device * gain_size)
    shared = put(shared, gain_ffn, feature_count + device * gain_size)
    for row in range(rows_here):
        start = ((row_place * rows_here + row) * seq_count + seq_place) * seg_tok
        shared = put(shared, segment_ids[row], 2 * feature_count + start)
    shared = shared.reshape(-1, 128)
    shared = shared + x_swap(shared)
    shared = shared + y_swap(shared)
    cotangent_here = cotangent.reshape(tokens_here, feature_count)
    cot_own = hold(cotangent_here, shared)
    cot_x, cot_y = x_swap(cot_own), y_swap(cot_own)
    shared = sum_over(shared, ("core", "z"))
    qkv_here = jnp.concatenate([w_query, w_key, w_value], axis=1)
    qkv_own, shared = together(jnp.stack(direct_gather(qkv_here)), shared)
    shared = shared.reshape(-1)
    attn_gain = shared[:feature_count].reshape(1, -1)
    ffn_gain = shared[feature_count : 2 * feature_count].reshape(1, -1)
    seg_all = shared[2 * feature_count :].reshape(rows_count, rows_here * seq_count, seg_tok)
    seg_all = lax.dynamic_index_in_dim(seg_all, row_place, 0, keepdims=False)
    seg_here = segment_ids.astype(jnp.float32)

    qkv_width = qkv_own.shape[2]
    cut = 1024
    out_own = turn(jnp.stack(direct_gather(w_out)), (planes - z_at) % planes)
    qkv_x, qkv_y, out_own, cot_x, cot_y = together(
        x_swap(qkv_own), y_swap(qkv_own), out_own, cot_x, cot_y
    )
    down_turned = w_down.T
    ffn_width = w_gate.shape[1]
    ffn_cut = (ffn_width // 256 + 1) * 128
    stacks = [
        jnp.stack([w[:, first:last] for w in (w_gate, w_up, down_turned)])
        for first, last in ((0, ffn_cut), (ffn_cut, ffn_width))
    ]
    qkv_a, qkv_b, out_x, first_stack = together(
        y_swap(qkv_x[..., :cut]),
        x_swap(qkv_y[..., cut:]),
        x_swap(out_own),
        corner(hold(stacks[0], qkv_x)),
    )
    out_block = in_order(out_own, out_x, x_at, 0)
    qkv_pieces = [qkv_own, qkv_x, qkv_y, qkv_a, qkv_b]
    qkv_pieces += [core_swap(piece) for piece in qkv_pieces]
    spots = [(0, 0, 0, 0), (1, 0, 0, 0), (0, 1, 0, 0), (1, 1, 0, 0), (1, 1, 0, cut)]
    spots = tuple(spots + [(dx, dy, 1, column) for dx, dy, _, column in spots])
    gathered_first = lax.all_gather(first_stack, ("core", "z"), axis=0)

    inputs_here = inputs.reshape(tokens_here, feature_count)
    cosine, sine = rotary_tables(positions.reshape(tokens_here), head_dim)
    cosine = jnp.concatenate([cosine, cosine], axis=1)
    sine = jnp.concatenate([sine, sine], axis=1)
    gain_q = jnp.tile(gain_query.astype(jnp.float32), grouping).reshape(1, -1)
    gain_k = jnp.tile(gain_key.astype(jnp.float32), 2 * heads_kv).reshape(1, -1)
    normed, query_pre, kv_pre, query_b, kv_here = project_call(
        width_q, head_dim, qkv_width, place, inputs_here, attn_gain, gain_q, gain_k, cosine, sine,
        spots, qkv_pieces,
    )

    half = feature_count // 2
    near = y_swap(kv_here)
    *kv_far, out_y, cot_a, cot_b, second_stack = together(
        *[chain(kv_here, t) for t in range(1, planes)],
        y_swap(hold(out_block, kv_here)),
        y_swap(hold(cot_x[:, :half], kv_here)),
        x_swap(hold(cot_y[:, half:], kv_here)),
        corner(hold(stacks[1], kv_here)),
    )
    parts = [gathered_first, lax.all_gather(second_stack, ("core", "z"), axis=0)]
    out_block = in_order(out_block, out_y, y_at, 2)
    kv_own = [kv_here] + list(kv_far)
    *kv_other, out_core = together(
        near, *[y_swap(piece) for piece in kv_far], core_swap(out_block)
    )
    out_full = in_order(out_block, out_core, core_at, 1).reshape(-1, feature_count)
    cot_blocks = [cotangent_here, cot_x, cot_y, jnp.concatenate([cot_a, cot_b], axis=1)]
    kv_pieces, bases = [], [seq_place * seg_tok]
    for t in range(planes):
        for dy, piece in enumerate((kv_own[t], kv_other[t])):
            kv_pieces.append(piece)
            bases.append(((z_at - t + planes) % planes * 2 + (y_at + dy) % 2) * seg_tok)
    bases = jnp.stack(bases).astype(jnp.int32)
    attended_b, logs = attend_call(
        heads_kv, grouping, bases, query_b, seg_here, seg_all, kv_pieces
    )
    residual = inputs_here.astype(jnp.float32)
    middle = residual + jnp.dot(attended_b, out_full, preferred_element_type=jnp.float32)
    ffn_in = rms_apply(middle, ffn_gain).astype(low)
    ffn_blocks = gather_tokens(ffn_in)

    before, where = None, place
    hidden_parts, home, sums = [], [], []
    for gathered in parts:
        result = ffn_call(
            planes, where, ffn_blocks, cot_blocks, gathered, before
        )
        hiddens, dgates, dups, before = [result[i::4] for i in range(4)]
        hidden_parts.append(hiddens)
        own, other = weight_grad_call(
            planes, place, ffn_blocks, cot_blocks, dgates, dups, hiddens
        )
        both = add_low(own, core_swap(other))
        where = hold(place, both) if not sums else place
        sums.append(lax.psum_scatter(both, "z", scatter_dimension=0))
    home = [corner(mine).astype(jnp.float32) for mine in sums]
    grad_ffn_in = scatter_tokens(before)
    down_blocks = down_call(planes, hold(place, own), hidden_parts, parts)
    down_blocks = hold(tuple(down_blocks), grad_ffn_in)
    down_mine = scatter_tokens(down_blocks)
    home = jnp.concatenate(home, axis=2)
    output_b = (middle + down_mine).astype(low).reshape(inputs.shape)
    grad_ffn_in = hold(grad_ffn_in, both)
    grad_mid_ffn, gain_ffn_rows = rms_back(middle, ffn_gain, grad_ffn_in)
    grad_middle = cotangent_here.astype(jnp.float32) + grad_mid_ffn
    grad_gain_ffn = jnp.sum(gain_ffn_rows, axis=0)
    grad_branch = grad_middle.astype(low)
    grad_attended = times_transposed(grad_branch, out_full).astype(low)

    def over_core(grad):
        keep, send = pick(grad.reshape(2, 2, planes, 2, -1, grad.shape[1]), core_at, 1)
        return add_low(keep, core_swap(send))

    def over_x(block):
        keep, send = pick(block, x_at, 0)
        return add_low(keep, x_swap(send))

    def over_y(block, axis):
        keep, send = pick(block, y_at, axis)
        return add_low(keep, y_swap(send))

    def over_z(block):
        block = turn(block, z_at)
        total = block[0].astype(jnp.float32)
        for t in range(1, planes):
            total = total + ring(block[t], t).astype(jnp.float32)
        return total

    out_core = over_core(transposed_times(attended_b, grad_branch).astype(low))
    result = attend_back_call(
        heads_kv, grouping, hold(bases, out_core, sums[0], *down_blocks), query_b, grad_attended,
        seg_here, seg_all, logs, query_pre, gain_q, cosine, sine, kv_pieces,
    )
    grad_query_b, gain_q_rows, dkv = result[0], result[1], result[2:]
    query_core = over_core(transposed_times(normed, grad_query_b).astype(low))
    *pairs, query_core, out_x = together(
        *[add_low(dkv[2 * t], y_swap(dkv[2 * t + 1])) for t in range(planes)],
        query_core,
        over_x(hold(out_core, down_mine)),
    )
    *far, query_x, out_y = together(
        *[chain(pairs[t], -t) for t in range(1, planes)], over_x(query_core), over_y(out_x, 1)
    )
    moving = pairs[0].astype(jnp.float32)
    for piece in far:
        moving = moving + piece.astype(jnp.float32)
    moving = hold(moving, sums[1])
    grad_kv_b, gain_k_rows = keys_back_call(head_dim, moving, kv_pre, gain_k, cosine, sine)
    kv_core, query_y, grad_out_mine = together(
        over_core(transposed_times(normed, grad_kv_b).astype(low)),
        over_y(query_x, 1),
        over_z(out_y),
    )
    grad_qkv_b = jnp.concatenate([grad_query_b, grad_kv_b], axis=1)
    grad_inputs, grad_gain_attn = input_call(
        hold(place, kv_core), grad_qkv_b, inputs_here, attn_gain, grad_middle, spots,
        qkv_pieces,
    )
    kv_y, grad_query_mine = together(over_y(kv_core, 2), over_z(query_y))
    grad_kv_mine = over_z(over_x(kv_y))
    gain_q_rows = jnp.sum(gain_q_rows.reshape(-1, head_dim), axis=0)
    gain_k_rows = jnp.sum(gain_k_rows.reshape(-1, head_dim)[:heads_kv], axis=0)
    small = jnp.concatenate([grad_gain_attn.reshape(-1), grad_gain_ffn, gain_q_rows, gain_k_rows])
    small = sum_over(small.reshape(-1, 128), ("x", "y", "core", "z")).reshape(-1)
    return (
        output_b,
        grad_inputs.reshape(inputs.shape),
        grad_query_mine,
        grad_kv_mine[:, :width_k],
        grad_kv_mine[:, width_k:],
        grad_out_mine,
        home[0],
        home[1],
        home[2].T,
        lax.dynamic_slice_in_dim(small, device * gain_size, gain_size),
        small[2 * feature_count : 2 * feature_count + head_dim],
        small[2 * feature_count + head_dim :],
        lax.dynamic_slice_in_dim(small, feature_count + device * gain_size, gain_size),
    )


def solution(mesh):
    rows, seq = mesh.devices.shape
    grid = Mesh(mesh.devices.reshape(2, rows // 2, seq // 2, 2), ("x", "core", "z", "y"))
    return jax.shard_map(
        local,
        mesh=grid,
        in_specs=(
            P(("x", "core"), ("z", "y"), None),
            P(("x", "core"), ("z", "y"), None),
            P(("x", "core"), ("z", "y")),
            P(("x", "core"), ("z", "y")),
            P(("x", "core", "z", "y"), None),
            P(("x", "core", "z", "y"), None),
            P(("x", "core", "z", "y"), None),
            P(("x", "core", "z", "y"), None),
            P(("z", "y"), ("x", "core")),
            P(("z", "y"), ("x", "core")),
            P(("x", "core"), ("z", "y")),
            P(("x", "core", "z", "y")),
            P(),
            P(),
            P(("x", "core", "z", "y")),
        ),
        out_specs=(
            P(("x", "core"), ("z", "y"), None),
            P(("x", "core"), ("z", "y"), None),
            P(("x", "core", "z", "y"), None),
            P(("x", "core", "z", "y"), None),
            P(("x", "core", "z", "y"), None),
            P(("x", "core", "z", "y"), None),
            P(("z", "y"), ("x", "core")),
            P(("z", "y"), ("x", "core")),
            P(("x", "core"), ("z", "y")),
            P(("x", "core", "z", "y")),
            P(),
            P(),
            P(("x", "core", "z", "y")),
        ),
        check_vma=False,
    )
```

time: 2160 us -> 797 us (0.37)
  waiting for transfers between devices: 1680 us -> 336 us
  matrix products: 226 us -> 12.8 us
  Pallas kernels: 0 us -> 196 us
  blocking collectives: 104 us -> 0 us
  starting transfers between devices: 0.89 us -> 97 us
  other arithmetic: 44.3 us -> 82.3 us
  local copies, waits for them, and re-layouts: 83.1 us -> 52.7 us
    reduce_scatter x9 -> x2, waiting for transfers between devices: 1040 us -> 1.67 us  [local(): sums.append(lax.psum_scatter(both, 'z', scatter_dimension=0))]
    all_gather x11 -> x2, waiting for transfers between devices: 558 us -> 0.02 us  [the longest x1 0.02 us: local(): lax.all_gather(second_stack, ('core', 'z'), axis=0)]
    ppermute x0 -> x82, waiting for transfers between devices: none -> 335 us  [the longest x57 264 us: swap(): return lax.ppermute(values, axis_name, [(i, i ^ bit) for i in range(count)])]
    pallas_call x0 -> x10, Pallas kernels: none -> 196 us  [the longest x2 66.5 us: ffn_call(): pl.pallas_call(functools.partial(ffn_kernel, planes, blocks, chained), ou...]
    dot_general x24 -> x0, matrix products: 118 us -> none  [the longest x6 21.5 us: block_scores(): jnp.einsum('rqhgd,rkhd->rhgqk', query_b, keys_blk, preferred_element_type...]
    ppermute x0 -> x82, starting transfers between devices: none -> 96.4 us  [the longest x57 47.2 us: swap(): return lax.ppermute(values, axis_name, [(i, i ^ bit) for i in range(count)])]
    unnamed x2 -> x0, blocking collectives: 85 us -> none
    unnamed x24 -> x4, waiting for transfers between devices: 79.8 us -> 0.07 us
  transfers between devices with their start and end apart: 22 -> 86, of which waited for: 22 -> 46; matrix products, arithmetic and copies ran while one was open for 10% -> 18% of each run, Pallas kernels for 0% -> 23%
where the time goes in v2:
time: 797 us; the launch traced here: 792 us
  waiting for transfers between devices  336 us (42%)
  Pallas kernels  196 us (25%)
  starting transfers between devices  97 us (12%)
  other arithmetic  82.3 us (10%)
  local copies, waits for them, and re-layouts  52.7 us (7%)
  between operations  15 us (2%)
  matrix products  12.8 us (2%)
    ppermute x57, waiting for transfers between devices, swap(): return lax.ppermute(values, axis_name, [(i, i ^ bit) for i in range(count)])  264 us
    pallas_call x2, Pallas kernels, ffn_call(): pl.pallas_call(functools.partial(ffn_kernel, planes, blocks, chained), ou...  66.5 us
    ppermute x6, waiting for transfers between devices, chain(): return lax.ppermute(values, 'z', moves)  60.4 us
    ppermute x57, starting transfers between devices, swap(): return lax.ppermute(values, axis_name, [(i, i ^ bit) for i in range(count)])  47.2 us
    pallas_call x2, Pallas kernels, weight_grad_call(): pl.pallas_call(functools.partial(weight_grad_kernel, blocks), out_shape=[...  40.2 us
    convert_element_type x19, other arithmetic, add_low(): (left.astype(jnp.float32) + right.astype(jnp.float32)).astype(jnp.bfloat16)  31.3 us
    pallas_call x1, Pallas kernels, attend_back_call(): pl.pallas_call(functools.partial(attend_back_kernel, pieces, heads_kv, gr...  30.9 us
    ppermute x15, starting transfers between devices, ring(): lax.ppermute(values, 'z', [(i, (i + shift) % count) for i in range(count)])  24.9 us
  transfers between devices with their start and end apart: 86, of which 46 were waited for; matrix products, arithmetic and copies ran while one was open for 18% of the time, Pallas kernels for 23%

profile of v2, /device:TPU:0, one launch (start us, length us, event | category | flops | bytes accessed | tf_op | source)
XLA Modules:
  0.0 792.2 jit_solution(1901105881791840281)
XLA Ops:
  7.2 5.1 collective-permute-start.10
  38.5 7.3 collective-permute-done.6
  46.4 4.7 collective-permute-start.7
  55.8 4.7 collective-permute-done.14.refs_6_
  60.5 11.6 %collective-permute-done.13.refs_5_ = bf16[256,2048]{1,0:T(8,128)(2,1)S(1)} collective-permute-done((bf16[256,2048]{1,0:T(8,128)(2,1)}, bf16[256,2048]{1,0:T(8,128)(2,1)S(1)}, u32[]{:S(2)}, u32[]{:S(2)}) %collective-permute-start.13) | collective-permute-done | bytes 1048608 | tf_op jit(solution)/shard_map/ppermute | solution.py:725
  72.1 8.4 %collective-permute-done.9.refs_2_ = bf16[4,64,1920]{2,1,0:T(8,128)(2,1)S(1)} collective-permute-done((bf16[4,64,1920]{2,1,0:T(8,128)(2,1)S(1)}, bf16[4,64,1920]{2,1,0:T(8,128)(2,1)S(1)}, u32[]{:S(2)}, u32[]{:S(2)}) %collective-permute-start.9) | collective-permute-done | bytes 983072 | tf_op jit(solution)/shard_map/ppermute | solution.py:725
  80.6 11.3 %collective-permute-done.8.refs_1_ = bf16[4,64,1920]{2,1,0:T(8,128)(2,1)S(1)} collective-permute-done((bf16[4,64,1920]{2,1,0:T(8,128)(2,1)S(1)}, bf16[4,64,1920]{2,1,0:T(8,128)(2,1)S(1)}, u32[]{:S(2)}, u32[]{:S(2)}) %collective-permute-start.8) | collective-permute-done | bytes 983072 | tf_op jit(solution)/shard_map/ppermute | solution.py:725
  101.7 18.7 %collective-permute-done.16.refs_4_ = bf16[4,64,896]{2,1,0:T(8,128)(2,1)} collective-permute-done((bf16[4,64,896]{2,1,0:T(8,128)(2,1)}, bf16[4,64,896]{2,1,0:T(8,128)(2,1)}, u32[]{:S(2)}, u32[]{:S(2)}) %collective-permute-start.16) | collective-permute-done | bytes 458784 | tf_op jit(solution)/shard_map/ppermute | solution.py:725
  135.5 12.5 %shard_map.246 = (bf16[256,2048]{1,0:T(8,128)(2,1)}, f32[256,1280]{1,0:T(8,128)}, f32[256,640]{1,0:T(8,128)}, bf16[256,1280]{1,0:T(8,128)(2,1)}, bf16[256,640]{1,0:T(8,128)(2,1)}) custom-call(s32[4]{0:T(128)} %pad_add_fusion.place_ref, bf16[256,2048]{1,0:T(8,128)(2,1)} %bitcast.228, f32[1,2048]{1,0:T(1,128)} %bitcast.240, ...), custom_call_target="tpu_custom_call" | custom-call | flops 2013265920 | bytes 13107200 | tf_op jit(solution)/shard_map/pallas_call | solution.py:366
  158.5 11.8 %collective-permute-done.27.refs_6_ = bf16[256,640]{1,0:T(8,128)(2,1)} collective-permute-done((bf16[256,640]{1,0:T(8,128)(2,1)}, bf16[256,640]{1,0:T(8,128)(2,1)}, u32[]{:S(2)}, u32[]{:S(2)}) %collective-permute-start.27) | collective-permute-done | bytes 327712 | tf_op jit(solution)/shard_map/ppermute | solution.py:772
  172.3 8.4 %collective-permute-start.25 = (bf16[256,640]{1,0:T(8,128)(2,1)}, bf16[256,640]{1,0:T(8,128)(2,1)}, u32[]{:S(2)}, u32[]{:S(2)}) collective-permute-start(bf16[256,640]{1,0:T(8,128)(2,1)} %get-tuple-element.140.refs_0_), channel_id=1, source_target_pairs={{0,2},{2,4},{4,6},{1,3},{3,5},{5,7},{8,10},{10,12},{12,14},{9,11},... | collective-permute-start | bytes 983048 | tf_op jit(solution)/shard_map/ppermute | solution.py:772
  186.9 13.2 %collective-permute-done.25.refs_2_ = bf16[256,640]{1,0:T(8,128)(2,1)} collective-permute-done((bf16[256,640]{1,0:T(8,128)(2,1)}, bf16[256,640]{1,0:T(8,128)(2,1)}, u32[]{:S(2)}, u32[]{:S(2)}) %collective-permute-start.25) | collective-permute-done | bytes 327712 | tf_op jit(solution)/shard_map/ppermute | solution.py:772
  200.2 5.8 collective-permute-done.29
  215.5 6.0 collective-permute-done.24.refs_1_
  221.5 7.0 collective-permute-done.32.refs_3_
  228.6 7.0 collective-permute-done.33.refs_5_
  235.6 6.6 collective-permute-done.34.refs_7_
  242.2 18.2 %shard_map.247 = (bf16[256,1280]{1,0:T(8,128)(2,1)}, f32[2,5,1,512]{3,2,1,0:T(1,128)}) custom-call(s32[9]{0:T(128)} %stack.160.base_ref, bf16[256,1280]{1,0:T(8,128)(2,1)} %get-tuple-element.139.q_ref, f32[2,128]{1,0:T(2,128)} %convert_element_type.358.segq_ref, f32[16,128]{1,0:T(8,128)} %dynamic-slice_bitcast_fusion.6.segk_ref, ...), custom_call_target="tpu_custom_call" | custom-call | flops 5368709120 | bytes 3932160 | tf_op jit(solution)/shard_map/pallas_call | solution.py:128
  260.5 4.4 maximum_select_fusion
  268.5 24.1 %collective-permute-done.36.refs_1_ = bf16[256,2048]{1,0:T(8,128)(2,1)S(1)} collective-permute-done((bf16[256,2048]{1,0:T(8,128)(2,1)S(1)}, bf16[256,2048]{1,0:T(8,128)(2,1)S(1)}, u32[]{:S(2)}, u32[]{:S(2)}) %collective-permute-start.36) | collective-permute-done | bytes 1048608 | tf_op jit(solution)/shard_map/ppermute | solution.py:725
  295.6 10.1 %collective-permute-done.38 = bf16[256,1024]{1,0:T(8,128)(2,1)S(1)} collective-permute-done((bf16[256,1024]{1,0:T(8,128)(2,1)S(1)}, bf16[256,1024]{1,0:T(8,128)(2,1)S(1)}, u32[]{:S(2)}, u32[]{:S(2)}) %collective-permute-start.38) | collective-permute-done | bytes 524320 | tf_op jit(solution)/shard_map/ppermute | solution.py:725
  307.5 40.3 %shard_map.248 = (bf16[256,896]{1,0:T(8,128)(2,1)}, bf16[256,896]{1,0:T(8,128)(2,1)}, bf16[256,896]{1,0:T(8,128)(2,1)}, bf16[256,2048]{1,0:T(8,128)(2,1)}, bf16[...) custom-call(s32[4]{0:T(128)} %pad_add_fusion.place_ref, ...), custom_call_target="tpu_custom_call" | custom-call | flops 18790481920 | bytes 27787264 | tf_op jit(solution)/shard_map/pallas_call | solution.py:562
  347.9 21.6 %shard_map.249 = (bf16[4,3,256,896]{3,2,1,0:T(8,128)(2,1)}, bf16[4,3,256,896]{3,2,1,0:T(8,128)(2,1)}) custom-call(s32[4]{0:T(128)} %pad_add_fusion.place_ref, bf16[256,2048]{1,0:T(8,128)(2,1)} %copy-done.28, bf16[256,2048]{1,0:T(8,128)(2,1)} %copy-done.44, bf16[256,2048]{1,0:T(8,128)(2,1)} %copy-done.45, ...), custom_call_target="tpu_custom_call" | custom-call | flops 11274289152 | bytes 16515072 | tf_op jit(solution)/shard_map/pallas_call | solution.py:612
  369.6 9.2 %collective-permute-done.40 = bf16[4,3,256,896]{3,2,1,0:T(8,128)(2,1)S(1)} collective-permute-done((bf16[4,3,256,896]{3,2,1,0:T(8,128)(2,1)}, bf16[4,3,256,896]{3,2,1,0:T(8,128)(2,1)S(1)}, u32[]{:S(2)}, u32[]{:S(2)}) %collective-permute-start.40) | collective-permute-done | bytes 5505056 | tf_op jit(solution)/shard_map/ppermute | solution.py:725
  378.8 6.6 add_convert_fusion
  385.9 26.2 %shard_map.250 = (bf16[256,768]{1,0:T(8,128)(2,1)}, bf16[256,768]{1,0:T(8,128)(2,1)}, bf16[256,768]{1,0:T(8,128)(2,1)}, bf16[256,2048]{1,0:T(8,128)(2,1)}, bf16[...) custom-call(s32[4]{0:T(128)} %pad_add_fusion.place_ref, ...), custom_call_target="tpu_custom_call" | custom-call | flops 16106127360 | bytes 26214400 | tf_op jit(solution)/shard_map/pallas_call | solution.py:562
  414.7 18.5 %shard_map.251 = (bf16[4,3,256,768]{3,2,1,0:T(8,128)(2,1)}, bf16[4,3,256,768]{3,2,1,0:T(8,128)(2,1)}) custom-call(s32[4]{0:T(128)} %pad_add_fusion.place_ref, bf16[256,2048]{1,0:T(8,128)(2,1)} %copy-done.28, bf16[256,2048]{1,0:T(8,128)(2,1)} %copy-done.44, bf16[256,2048]{1,0:T(8,128)(2,1)} %copy-done.45, ...), custom_call_target="tpu_custom_call" | custom-call | flops 9663676416 | bytes 14155776 | tf_op jit(solution)/shard_map/pallas_call | solution.py:612
  439.0 9.2 %collective-permute-done.41 = bf16[256,1024]{1,0:T(8,128)(2,1)S(1)} collective-permute-done((bf16[256,1024]{1,0:T(8,128)(2,1)S(1)}, bf16[256,1024]{1,0:T(8,128)(2,1)S(1)}, u32[]{:S(2)}, u32[]{:S(2)}) %collective-permute-start.41) | collective-permute-done | bytes 524320 | tf_op jit(solution)/shard_map/ppermute | solution.py:725
  451.1 13.8 %shard_map.252 = (bf16[256,2048]{1,0:T(8,128)(2,1)}, bf16[256,2048]{1,0:T(8,128)(2,1)}, bf16[256,2048]{1,0:T(8,128)(2,1)}, bf16[256,2048]{1,0:T(8,128)(2,1)}) custom-call(s32[4]{0:T(128)} %pad_add_fusion.place_ref, bf16[256,896]{1,0:T(8,128)(2,1)} %get-tuple-element.169.refs_16_.refs_0_, bf16[256,896]{1,0:T(8,128)(2,1)} %get-tuple-element.170.refs_17_.refs_1_, ...), custom_call_target="tpu_custom_call" | custom-call | flops 6979321856 | bytes 23592960 | tf_op jit(solution)/shard_map/pallas_call | solution.py:667
  464.9 5.4 collective-permute-done.44
  481.0 9.2 %collective-permute-done.47 = bf16[256,1024]{1,0:T(8,128)(2,1)S(1)} collective-permute-done((bf16[256,1024]{1,0:T(8,128)(2,1)S(1)}, bf16[256,1024]{1,0:T(8,128)(2,1)S(1)}, u32[]{:S(2)}, u32[]{:S(2)}) %collective-permute-start.47) | collective-permute-done | bytes 524320 | tf_op jit(solution)/shard_map/ppermute | solution.py:725
  495.7 7.2 add_convert_fusion.1
  505.2 9.2 %collective-permute-done.48 = bf16[256,2048]{1,0:T(8,128)(2,1)} collective-permute-done((bf16[256,2048]{1,0:T(8,128)(2,1)}, bf16[256,2048]{1,0:T(8,128)(2,1)}, u32[]{:S(2)}, u32[]{:S(2)}) %collective-permute-start.48) | collective-permute-done | bytes 1048608 | tf_op jit(solution)/shard_map/ppermute | solution.py:725
  516.7 4.0 add_convert_fusion.2
  528.4 5.0 convolution_convert_fusion.3.do_ref
  539.0 30.9 %shard_map.253 = (bf16[256,1280]{1,0:T(8,128)(2,1)}, f32[2,5,1,256]{3,2,1,0:T(1,128)}, bf16[256,640]{1,0:T(8,128)(2,1)}, bf16[256,640]{1,0:T(8,128)(2,1)}, bf16[...) custom-call(s32[9]{0:T(128)} %stack.160.base_ref, ...), custom_call_target="tpu_custom_call" | custom-call | flops 13421772800 | bytes 7864320 | tf_op jit(solution)/shard_map/pallas_call | solution.py:265
  589.0 5.4 collective-permute-done.52
  595.2 24.0 %collective-permute-done.53 = bf16[256,640]{1,0:T(8,128)(2,1)S(1)} collective-permute-done((bf16[256,640]{1,0:T(8,128)(2,1)S(1)}, bf16[256,640]{1,0:T(8,128)(2,1)S(1)}, u32[]{:S(2)}, u32[]{:S(2)}) %collective-permute-start.53) | collective-permute-done | bytes 327712 | tf_op jit(solution)/shard_map/ppermute | solution.py:725
  636.8 7.6 collective-permute-done.61
  648.5 8.2 %collective-permute-done.60 = bf16[4,2,64,1280]{3,2,0,1:T(8,128)(2,1)} collective-permute-done((bf16[4,2,64,1280]{3,2,0,1:T(8,128)(2,1)}, bf16[4,2,64,1280]{3,2,0,1:T(8,128)(2,1)}, u32[]{:S(2)}, u32[]{:S(2)}) %collective-permute-start.60) | collective-permute-done | bytes 1310752 | tf_op jit(solution)/shard_map/ppermute | solution.py:725
  659.4 8.9 %collective-permute-done.57 = bf16[256,640]{1,0:T(8,128)(2,1)} collective-permute-done((bf16[256,640]{1,0:T(8,128)(2,1)}, bf16[256,640]{1,0:T(8,128)(2,1)}, u32[]{:S(2)}, u32[]{:S(2)}) %collective-permute-start.57) | collective-permute-done | bytes 327712 | tf_op jit(solution)/shard_map/ppermute | solution.py:772
  668.2 22.7 %collective-permute-done.58 = bf16[256,640]{1,0:T(8,128)(2,1)} collective-permute-done((bf16[256,640]{1,0:T(8,128)(2,1)}, bf16[256,640]{1,0:T(8,128)(2,1)}, u32[]{:S(2)}, u32[]{:S(2)}) %collective-permute-start.58) | collective-permute-done | bytes 327712 | tf_op jit(solution)/shard_map/ppermute | solution.py:772
  693.1 3.9 shard_map.254
  709.3 6.1 collective-permute-done.65
  718.4 7.5 collective-permute-done.63
  727.8 10.1 %shard_map.255 = (f32[256,2048]{1,0:T(8,128)}, f32[1,2048]{1,0:T(1,128)}) custom-call(s32[4]{0:T(128)} %pad_add_fusion.place_ref, bf16[256,1920]{1,0:T(8,128)(2,1)} %pad_maximum_fusion.10.g_ref, bf16[256,2048]{1,0:T(8,128)(2,1)} %bitcast.229, f32[1,2048]{1,0:T(1,128)} %bitcast.241, f32[256,2048]{1,0:T(8,128)} %copy-done.1, bf16[4,64,1920]{2,1,0:T(8,128)(2,1)} %copy-done.5, ...), custom_call_target="tpu_custom_call" | custom-call | flops 2013265920 | bytes 13107200 | tf_op jit(solution)/shard_map/pallas_call | solution.py:446
  752.4 9.1 %collective-permute-done.80 = f32[33,128]{1,0:T(8,128)S(1)} collective-permute-done((f32[33,128]{1,0:T(8,128)S(1)}, f32[33,128]{1,0:T(8,128)S(1)}, u32[]{:S(2)}, u32[]{:S(2)}) %collective-permute-start.80) | collective-permute-done | bytes 16928 | tf_op jit(solution)/shard_map/ppermute | solution.py:725
  763.9 4.1 collective-permute-done.67
  (392 shorter events, 236.1 us)
Async XLA Ops:
  7.2 300.3 %all-gather.5.cloned.1.call-start = ((), (), s32[]{:S(2)}) async-start(), calls=%async_computation.4 | async-start | bytes 12386304 | tf_op jit(solution)/shard_map/all_gather | solution.py:934
  7.2 23.9 %collective-permute-start.10 = (bf16[40,2048]{1,0:T(8,128)(2,1)}, bf16[40,2048]{1,0:T(8,128)(2,1)S(1)}, u32[]{:S(2)}, u32[]{:S(2)}) collective-permute-start(bf16[40,2048]{1,0:T(8,128)(2,1)} %param.22), channel_id=1, source_target_pairs={{0,6},{2,0},{4,2},{6,4},{1,7},{3,1},{5,3},{7,5},{8,14},{10,8},{12,... | collective-permute-start | bytes 491528 | tf_op jit(solution)/shard_map/ppermute | solution.py:730
  12.3 24.2 %collective-permute-start.12 = (bf16[40,2048]{1,0:T(8,128)(2,1)}, bf16[40,2048]{1,0:T(8,128)(2,1)S(1)}, u32[]{:S(2)}, u32[]{:S(2)}) collective-permute-start(bf16[40,2048]{1,0:T(8,128)(2,1)} %param.22), channel_id=1, source_target_pairs={{0,2},{2,4},{4,6},{6,0},{1,3},{3,5},{5,7},{7,1},{8,10},{10,12},{12... | collective-permute-start | bytes 491528 | tf_op jit(solution)/shard_map/ppermute | solution.py:730
  12.3 22.0 %collective-permute-start.11 = (bf16[40,2048]{1,0:T(8,128)(2,1)}, bf16[40,2048]{1,0:T(8,128)(2,1)S(1)}, u32[]{:S(2)}, u32[]{:S(2)}) collective-permute-start(bf16[40,2048]{1,0:T(8,128)(2,1)} %param.22), channel_id=1, source_target_pairs={{0,4},{2,6},{4,0},{6,2},{1,5},{3,7},{5,1},{7,3},{8,12},{10,14},{12... | collective-permute-start | bytes 491528 | tf_op jit(solution)/shard_map/ppermute | solution.py:730
  18.9 27.5 %collective-permute-start.2 = (bf16[64,1920]{1,0:T(8,128)(2,1)S(1)}, bf16[64,1920]{1,0:T(8,128)(2,1)}, u32[]{:S(2)}, u32[]{:S(2)}) collective-permute-start(bf16[64,1920]{1,0:T(8,128)(2,1)S(1)} %concatenate.101), channel_id=1, source_target_pairs={{0,2},{2,4},{4,6},{6,0},{1,3},{3,5},{5,7},{7,1},{8,10},{10,12},{12... | collective-permute-start | bytes 737288 | tf_op jit(solution)/shard_map/ppermute | solution.py:730
  31.1 20.0 %collective-permute-start.1 = (bf16[64,1920]{1,0:T(8,128)(2,1)S(1)}, bf16[64,1920]{1,0:T(8,128)(2,1)S(1)}, u32[]{:S(2)}, u32[]{:S(2)}) collective-permute-start(bf16[64,1920]{1,0:T(8,128)(2,1)S(1)} %concatenate.101), channel_id=1, source_target_pairs={{0,4},{2,6},{4,0},{6,2},{1,5},{3,7},{5,1},{7,3},{8,12},{10,14},{12... | collective-permute-start | bytes 737288 | tf_op jit(solution)/shard_map/ppermute | solution.py:730
  31.2 20.0 %collective-permute-start = (bf16[64,1920]{1,0:T(8,128)(2,1)S(1)}, bf16[64,1920]{1,0:T(8,128)(2,1)S(1)}, u32[]{:S(2)}, u32[]{:S(2)}) collective-permute-start(bf16[64,1920]{1,0:T(8,128)(2,1)S(1)} %concatenate.101), channel_id=1, source_target_pairs={{0,6},{2,0},{4,2},{6,4},{1,7},{3,1},{5,3},{7,5},{8,14},{10,8},{12,... | collective-permute-start | bytes 737288 | tf_op jit(solution)/shard_map/ppermute | solution.py:730
  34.3 26.2 %collective-permute-start.14 = (bf16[256,2048]{1,0:T(8,128)(2,1)}, bf16[256,2048]{1,0:T(8,128)(2,1)S(1)}, u32[]{:S(2)}, u32[]{:S(2)}) collective-permute-start(bf16[256,2048]{1,0:T(8,128)(2,1)} %bitcast.27.refs_4_), channel_id=1, source_target_pairs={{0,1},{1,0},{2,3},{3,2},{4,5},{5,4},{6,7},{7,6},{8,9},{9,8},{10,11... | collective-permute-start | bytes 3145736 | tf_op jit(solution)/shard_map/ppermute | solution.py:725
  45.9 26.3 %collective-permute-start.13 = (bf16[256,2048]{1,0:T(8,128)(2,1)}, bf16[256,2048]{1,0:T(8,128)(2,1)S(1)}, u32[]{:S(2)}, u32[]{:S(2)}) collective-permute-start(bf16[256,2048]{1,0:T(8,128)(2,1)} %bitcast.27.refs_4_), channel_id=1, source_target_pairs={{0,16},{16,0},{1,17},{17,1},{2,18},{18,2},{3,19},{19,3},{4,20},{20... | collective-permute-start | bytes 3145736 | tf_op jit(solution)/shard_map/ppermute | solution.py:725
  53.2 27.4 %collective-permute-start.9 = (bf16[4,64,1920]{2,1,0:T(8,128)(2,1)S(1)}, bf16[4,64,1920]{2,1,0:T(8,128)(2,1)S(1)}, u32[]{:S(2)}, u32[]{:S(2)}) collective-permute-start(bf16[4,64,1920]{2,1,0:T(8,128)(2,1)S(1)} %pad_maximum_fusion.9.refs_0_), channel_id=1, source_target_pairs={{0,1},{1,0},{2,3},{3,2},{4,5},{5,4},{6,7},{7,6},{8,9},{9,8},{10,11... | collective-permute-start | bytes 2949128 | tf_op jit(solution)/shard_map/ppermute | solution.py:725
  54.2 37.7 %collective-permute-start.8 = (bf16[4,64,1920]{2,1,0:T(8,128)(2,1)S(1)}, bf16[4,64,1920]{2,1,0:T(8,128)(2,1)S(1)}, u32[]{:S(2)}, u32[]{:S(2)}) collective-permute-start(bf16[4,64,1920]{2,1,0:T(8,128)(2,1)S(1)} %pad_maximum_fusion.9.refs_0_), channel_id=1, source_target_pairs={{0,16},{16,0},{1,17},{17,1},{2,18},{18,2},{3,19},{19,3},{4,20},{20... | collective-permute-start | bytes 2949128 | tf_op jit(solution)/shard_map/ppermute | solution.py:725
  93.7 29.5 %collective-permute-start.17 = (bf16[4,40,2048]{2,1,0:T(8,128)(2,1)S(1)}, bf16[4,40,2048]{2,1,0:T(8,128)(2,1)S(1)}, u32[]{:S(2)}, u32[]{:S(2)}) collective-permute-start(bf16[4,40,2048]{2,1,0:T(8,128)(2,1)S(1)} %constant_dynamic-slice_fusion.6), channel_id=1, source_target_pairs={{0,16},{16,0},{1,17},{17,1},{2,18},{18,2},{3,19},{19,3},{4,20},{20... | collective-permute-start | bytes 1966088 | tf_op jit(solution)/shard_map/ppermute | solution.py:725
  95.1 28.1 %collective-permute-start.15 = (bf16[4,64,1024]{2,1,0:T(8,128)(2,1)}, bf16[4,64,1024]{2,1,0:T(8,128)(2,1)}, u32[]{:S(2)}, u32[]{:S(2)}) collective-permute-start(bf16[4,64,1024]{2,1,0:T(8,128)(2,1)} %slice.156), channel_id=1, source_target_pairs={{0,1},{1,0},{2,3},{3,2},{4,5},{5,4},{6,7},{7,6},{8,9},{9,8},{10,11... | collective-permute-start | bytes 1572872 | tf_op jit(solution)/shard_map/ppermute | solution.py:725
  97.6 22.8 %collective-permute-start.16 = (bf16[4,64,896]{2,1,0:T(8,128)(2,1)}, bf16[4,64,896]{2,1,0:T(8,128)(2,1)}, u32[]{:S(2)}, u32[]{:S(2)}) collective-permute-start(bf16[4,64,896]{2,1,0:T(8,128)(2,1)} %slice.157), channel_id=1, source_target_pairs={{0,16},{16,0},{1,17},{17,1},{2,18},{18,2},{3,19},{19,3},{4,20},{20... | collective-permute-start | bytes 1376264 | tf_op jit(solution)/shard_map/ppermute | solution.py:725
  123.2 262.8 %all-gather.7.cloned.1.call-start = ((), (), s32[]{:S(2)}) async-start(), calls=%async_computation.5 | async-start | bytes 10616832 | tf_op jit(solution)/shard_map/all_gather | solution.py:956
  148.1 24.3 %collective-permute-start.31 = (bf16[3,256,768]{2,1,0:T(8,128)(2,1)}, bf16[3,256,768]{2,1,0:T(8,128)(2,1)}, u32[]{:S(2)}, u32[]{:S(2)}) collective-permute-start(bf16[3,256,768]{2,1,0:T(8,128)(2,1)} %pad_maximum_fusion.4), channel_id=1, source_target_pairs={{1,8},{8,1},{3,10},{10,3},{5,12},{12,5},{7,14},{14,7},{17,24},{24,... | collective-permute-start | bytes 3538952 | tf_op jit(solution)/shard_map/ppermute | solution.py:765
  151.1 54.8 %collective-permute-start.28 = (bf16[2,4,40,2048]{3,2,1,0:T(8,128)(2,1)}, bf16[2,4,40,2048]{3,2,1,0:T(8,128)(2,1)S(1)}, u32[]{:S(2)}, u32[]{:S(2)}) collective-permute-start(bf16[2,4,40,2048]{3,2,1,0:T(8,128)(2,1)} %maximum_select_fusion.2), channel_id=1, source_target_pairs={{0,1},{1,0},{2,3},{3,2},{4,5},{5,4},{6,7},{7,6},{8,9},{9,8},{10,11... | collective-permute-start | bytes 3932168 | tf_op jit(solution)/shard_map/ppermute | solution.py:725
  153.5 16.8 %collective-permute-start.27 = (bf16[256,640]{1,0:T(8,128)(2,1)}, bf16[256,640]{1,0:T(8,128)(2,1)}, u32[]{:S(2)}, u32[]{:S(2)}) collective-permute-start(bf16[256,640]{1,0:T(8,128)(2,1)} %get-tuple-element.140.refs_0_), channel_id=1, source_target_pairs={{0,6},{1,7},{8,14},{9,15},{16,22},{17,23},{24,30},{25,31}} | collective-permute-start | bytes 983048 | tf_op jit(solution)/shard_map/ppermute | solution.py:772
  157.9 48.0 %collective-permute-start.29 = (bf16[256,1024]{1,0:T(8,128)(2,1)}, bf16[256,1024]{1,0:T(8,128)(2,1)S(1)}, u32[]{:S(2)}, u32[]{:S(2)}) collective-permute-start(bf16[256,1024]{1,0:T(8,128)(2,1)} %slice.162), channel_id=1, source_target_pairs={{0,1},{1,0},{2,3},{3,2},{4,5},{5,4},{6,7},{7,6},{8,9},{9,8},{10,11... | collective-permute-start | bytes 1572872 | tf_op jit(solution)/shard_map/ppermute | solution.py:725
  157.9 48.0 %collective-permute-start.30 = (bf16[256,1024]{1,0:T(8,128)(2,1)}, bf16[256,1024]{1,0:T(8,128)(2,1)}, u32[]{:S(2)}, u32[]{:S(2)}) collective-permute-start(bf16[256,1024]{1,0:T(8,128)(2,1)} %slice.163), channel_id=1, source_target_pairs={{0,16},{16,0},{1,17},{17,1},{2,18},{18,2},{3,19},{19,3},{4,20},{20... | collective-permute-start | bytes 1572872 | tf_op jit(solution)/shard_map/ppermute | solution.py:725
  170.3 16.7 %collective-permute-start.26 = (bf16[256,640]{1,0:T(8,128)(2,1)}, bf16[256,640]{1,0:T(8,128)(2,1)}, u32[]{:S(2)}, u32[]{:S(2)}) collective-permute-start(bf16[256,640]{1,0:T(8,128)(2,1)} %get-tuple-element.140.refs_0_), channel_id=1, source_target_pairs={{0,4},{2,6},{1,5},{3,7},{8,12},{10,14},{9,13},{11,15},{16,20},{18,... | collective-permute-start | bytes 983048 | tf_op jit(solution)/shard_map/ppermute | solution.py:772
  172.3 27.9 %collective-permute-start.25 = (bf16[256,640]{1,0:T(8,128)(2,1)}, bf16[256,640]{1,0:T(8,128)(2,1)}, u32[]{:S(2)}, u32[]{:S(2)}) collective-permute-start(bf16[256,640]{1,0:T(8,128)(2,1)} %get-tuple-element.140.refs_0_), channel_id=1, source_target_pairs={{0,2},{2,4},{4,6},{1,3},{3,5},{5,7},{8,10},{10,12},{12,14},{9,11},... | collective-permute-start | bytes 983048 | tf_op jit(solution)/shard_map/ppermute | solution.py:772
  206.0 333.1 %reduce-scatter.3.cloned.1.call-start = ((), (), s32[]{:S(2)}) async-start(), calls=%async_computation.2 | async-start | bytes 6881280 | tf_op jit(solution)/shard_map/reduce_scatter | solution.py:991
  208.6 33.6 %collective-permute-start.35 = (bf16[2,4,2,40,2048]{4,3,2,1,0:T(8,128)(2,1)}, bf16[2,4,2,40,2048]{4,3,2,1,0:T(8,128)(2,1)}, u32[]{:S(2)}, u32[]{:S(2)}) collective-permute-start(bf16[2,4,2,40,2048]{4,3,2,1,0:T(8,128)(2,1)} %maximum_select_fusion.1), channel_id=1, source_target_pairs={{0,8},{8,0},{1,9},{9,1},{2,10},{10,2},{3,11},{11,3},{4,12},{12,4},... | collective-permute-start | bytes 7864328 | tf_op jit(solution)/shard_map/ppermute | solution.py:725
  211.5 17.0 %collective-permute-start.32 = (bf16[256,640]{1,0:T(8,128)(2,1)}, bf16[256,640]{1,0:T(8,128)(2,1)}, u32[]{:S(2)}, u32[]{:S(2)}) collective-permute-start(bf16[256,640]{1,0:T(8,128)(2,1)} %collective-permute-done.25.refs_2_), channel_id=1, source_target_pairs={{0,1},{1,0},{2,3},{3,2},{4,5},{5,4},{6,7},{7,6},{8,9},{9,8},{10,11... | collective-permute-start | bytes 983048 | tf_op jit(solution)/shard_map/ppermute | solution.py:725
  212.7 22.8 %collective-permute-start.33 = (bf16[256,640]{1,0:T(8,128)(2,1)}, bf16[256,640]{1,0:T(8,128)(2,1)}, u32[]{:S(2)}, u32[]{:S(2)}) collective-permute-start(bf16[256,640]{1,0:T(8,128)(2,1)} %collective-permute-done.26.refs_4_), channel_id=1, source_target_pairs={{0,1},{1,0},{2,3},{3,2},{4,5},{5,4},{6,7},{7,6},{8,9},{9,8},{10,11... | collective-permute-start | bytes 983048 | tf_op jit(solution)/shard_map/ppermute | solution.py:725
  213.6 28.6 %collective-permute-start.34 = (bf16[256,640]{1,0:T(8,128)(2,1)}, bf16[256,640]{1,0:T(8,128)(2,1)}, u32[]{:S(2)}, u32[]{:S(2)}) collective-permute-start(bf16[256,640]{1,0:T(8,128)(2,1)} %collective-permute-done.27.refs_6_), channel_id=1, source_target_pairs={{0,1},{1,0},{2,3},{3,2},{4,5},{5,4},{6,7},{7,6},{8,9},{9,8},{10,11... | collective-permute-start | bytes 983048 | tf_op jit(solution)/shard_map/ppermute | solution.py:725
  267.5 25.0 %collective-permute-start.36 = (bf16[256,2048]{1,0:T(8,128)(2,1)S(1)}, bf16[256,2048]{1,0:T(8,128)(2,1)S(1)}, u32[]{:S(2)}, u32[]{:S(2)}) collective-permute-start(bf16[256,2048]{1,0:T(8,128)(2,1)S(1)} %multiply_convert_fusion.refs_0_), channel_id=1, source_target_pairs={{0,16},{16,0},{1,17},{17,1},{2,18},{18,2},{3,19},{19,3},{4,20},{20... | collective-permute-start | bytes 3145736 | tf_op jit(solution)/shard_map/ppermute | solution.py:725
  268.3 25.3 %collective-permute-start.37 = (bf16[256,2048]{1,0:T(8,128)(2,1)S(1)}, bf16[256,2048]{1,0:T(8,128)(2,1)S(1)}, u32[]{:S(2)}, u32[]{:S(2)}) collective-permute-start(bf16[256,2048]{1,0:T(8,128)(2,1)S(1)} %multiply_convert_fusion.refs_0_), channel_id=1, source_target_pairs={{0,1},{1,0},{2,3},{3,2},{4,5},{5,4},{6,7},{7,6},{8,9},{9,8},{10,11... | collective-permute-start | bytes 3145736 | tf_op jit(solution)/shard_map/ppermute | solution.py:725
  385.5 251.3 %reduce-scatter.5.cloned.1.call-start = ((), (), s32[]{:S(2)}) async-start(), calls=%async_computation.3 | async-start | bytes 5898240 | tf_op jit(solution)/shard_map/reduce_scatter | solution.py:991
  414.2 22.6 %collective-permute-start.43 = (bf16[256,1024]{1,0:T(8,128)(2,1)}, bf16[256,1024]{1,0:T(8,128)(2,1)S(1)}, u32[]{:S(2)}, u32[]{:S(2)}) collective-permute-start(bf16[256,1024]{1,0:T(8,128)(2,1)} %get-tuple-element.305), channel_id=1, source_target_pairs={{0,16},{16,0},{1,17},{17,1},{2,18},{18,2},{3,19},{19,3},{4,20},{20... | collective-permute-start | bytes 1572872 | tf_op jit(solution)/shard_map/ppermute | solution.py:725
  433.3 62.4 %collective-permute-start.49 = (bf16[4,3,256,768]{3,2,1,0:T(8,128)(2,1)}, bf16[4,3,256,768]{3,2,1,0:T(8,128)(2,1)}, u32[]{:S(2)}, u32[]{:S(2)}) collective-permute-start(bf16[4,3,256,768]{3,2,1,0:T(8,128)(2,1)} %get-tuple-element.208), channel_id=1, source_target_pairs={{0,8},{8,0},{1,9},{9,1},{2,10},{10,2},{3,11},{11,3},{4,12},{12,4},... | collective-permute-start | bytes 14155784 | tf_op jit(solution)/shard_map/ppermute | solution.py:725
  438.1 32.2 %collective-permute-start.44 = (bf16[256,2048]{1,0:T(8,128)(2,1)}, bf16[256,2048]{1,0:T(8,128)(2,1)}, u32[]{:S(2)}, u32[]{:S(2)}) collective-permute-start(bf16[256,2048]{1,0:T(8,128)(2,1)} %pad_maximum_fusion.6), channel_id=1, source_target_pairs={{0,1},{1,0},{2,3},{3,2},{4,5},{5,4},{6,7},{7,6},{8,9},{9,8},{10,11... | collective-permute-start | bytes 3145736 | tf_op jit(solution)/shard_map/ppermute | solution.py:725
  449.4 24.7 %collective-permute-start.42 = (bf16[256,2048]{1,0:T(8,128)(2,1)}, bf16[256,2048]{1,0:T(8,128)(2,1)}, u32[]{:S(2)}, u32[]{:S(2)}) collective-permute-start(bf16[256,2048]{1,0:T(8,128)(2,1)} %pad_maximum_fusion.5), channel_id=1, source_target_pairs={{0,16},{16,0},{1,17},{17,1},{2,18},{18,2},{3,19},{19,3},{4,20},{20... | collective-permute-start | bytes 3145736 | tf_op jit(solution)/shard_map/ppermute | solution.py:725
  491.5 22.9 %collective-permute-start.48 = (bf16[256,2048]{1,0:T(8,128)(2,1)}, bf16[256,2048]{1,0:T(8,128)(2,1)}, u32[]{:S(2)}, u32[]{:S(2)}) collective-permute-start(bf16[256,2048]{1,0:T(8,128)(2,1)} %pad_maximum_fusion.8), channel_id=1, source_target_pairs={{0,1},{1,0},{2,3},{3,2},{4,5},{5,4},{6,7},{7,6},{8,9},{9,8},{10,11... | collective-permute-start | bytes 3145736 | tf_op jit(solution)/shard_map/ppermute | solution.py:725
  494.0 22.7 %collective-permute-start.46 = (bf16[256,2048]{1,0:T(8,128)(2,1)}, bf16[256,2048]{1,0:T(8,128)(2,1)}, u32[]{:S(2)}, u32[]{:S(2)}) collective-permute-start(bf16[256,2048]{1,0:T(8,128)(2,1)} %pad_maximum_fusion.7), channel_id=1, source_target_pairs={{0,16},{16,0},{1,17},{17,1},{2,18},{18,2},{3,19},{19,3},{4,20},{20... | collective-permute-start | bytes 3145736 | tf_op jit(solution)/shard_map/ppermute | solution.py:725
  537.4 41.3 %collective-permute-start.56 = (bf16[4,2,40,2048]{3,2,0,1:T(8,128)(2,1)}, bf16[4,2,40,2048]{3,2,0,1:T(8,128)(2,1)}, u32[]{:S(2)}, u32[]{:S(2)}) collective-permute-start(bf16[4,2,40,2048]{3,2,0,1:T(8,128)(2,1)} %dynamic-slice_bitcast_fusion.1), channel_id=1, source_target_pairs={{0,16},{16,0},{1,17},{17,1},{2,18},{18,2},{3,19},{19,3},{4,20},{20... | collective-permute-start | bytes 3932168 | tf_op jit(solution)/shard_map/ppermute | solution.py:725
  576.6 47.0 %collective-permute-start.55 = (bf16[2,4,2,64,1280]{4,3,1,2,0:T(8,128)(2,1)}, bf16[2,4,2,64,1280]{4,3,1,2,0:T(8,128)(2,1)}, u32[]{:S(2)}, u32[]{:S(2)}) collective-permute-start(bf16[2,4,2,64,1280]{4,3,1,2,0:T(8,128)(2,1)} %bitcast.209), channel_id=1, source_target_pairs={{0,8},{8,0},{1,9},{9,1},{2,10},{10,2},{3,11},{11,3},{4,12},{12,4},... | collective-permute-start | bytes 7864328 | tf_op jit(solution)/shard_map/ppermute | solution.py:725
  577.5 16.9 %collective-permute-start.52 = (bf16[256,640]{1,0:T(8,128)(2,1)}, bf16[256,640]{1,0:T(8,128)(2,1)S(1)}, u32[]{:S(2)}, u32[]{:S(2)}) collective-permute-start(bf16[256,640]{1,0:T(8,128)(2,1)} %get-tuple-element.216), channel_id=1, source_target_pairs={{0,1},{1,0},{2,3},{3,2},{4,5},{5,4},{6,7},{7,6},{8,9},{9,8},{10,11... | collective-permute-start | bytes 983048 | tf_op jit(solution)/shard_map/ppermute | solution.py:725
  580.5 48.2 %collective-permute-start.75 = (bf16[3,256,896]{2,1,0:T(8,128)(2,1)}, bf16[3,256,896]{2,1,0:T(8,128)(2,1)}, u32[]{:S(2)}, u32[]{:S(2)}) collective-permute-start(bf16[3,256,896]{2,1,0:T(8,128)(2,1)} %bitcast.57), channel_id=1, source_target_pairs={{1,8},{8,1},{3,10},{10,3},{5,12},{12,5},{7,14},{14,7},{17,24},{24,... | collective-permute-start | bytes 4128776 | tf_op jit(solution)/shard_map/ppermute | solution.py:765
  582.5 36.7 %collective-permute-start.53 = (bf16[256,640]{1,0:T(8,128)(2,1)S(1)}, bf16[256,640]{1,0:T(8,128)(2,1)S(1)}, u32[]{:S(2)}, u32[]{:S(2)}) collective-permute-start(bf16[256,640]{1,0:T(8,128)(2,1)S(1)} %copy-done.54), channel_id=1, source_target_pairs={{0,1},{1,0},{2,3},{3,2},{4,5},{5,4},{6,7},{7,6},{8,9},{9,8},{10,11... | collective-permute-start | bytes 983048 | tf_op jit(solution)/shard_map/ppermute | solution.py:725
  587.4 35.3 %collective-permute-start.54 = (bf16[256,640]{1,0:T(8,128)(2,1)S(1)}, bf16[256,640]{1,0:T(8,128)(2,1)S(1)}, u32[]{:S(2)}, u32[]{:S(2)}) collective-permute-start(bf16[256,640]{1,0:T(8,128)(2,1)S(1)} %copy-done.53), channel_id=1, source_target_pairs={{0,1},{1,0},{2,3},{3,2},{4,5},{5,4},{6,7},{7,6},{8,9},{9,8},{10,11... | collective-permute-start | bytes 983048 | tf_op jit(solution)/shard_map/ppermute | solution.py:725
  627.3 29.4 %collective-permute-start.60 = (bf16[4,2,64,1280]{3,2,0,1:T(8,128)(2,1)}, bf16[4,2,64,1280]{3,2,0,1:T(8,128)(2,1)}, u32[]{:S(2)}, u32[]{:S(2)}) collective-permute-start(bf16[4,2,64,1280]{3,2,0,1:T(8,128)(2,1)} %dynamic-slice_bitcast_fusion), channel_id=1, source_target_pairs={{0,16},{16,0},{1,17},{17,1},{2,18},{18,2},{3,19},{19,3},{4,20},{20... | collective-permute-start | bytes 3932168 | tf_op jit(solution)/shard_map/ppermute | solution.py:725
  631.3 37.0 %collective-permute-start.57 = (bf16[256,640]{1,0:T(8,128)(2,1)}, bf16[256,640]{1,0:T(8,128)(2,1)}, u32[]{:S(2)}, u32[]{:S(2)}) collective-permute-start(bf16[256,640]{1,0:T(8,128)(2,1)} %add_convert_fusion.9), channel_id=1, source_target_pairs={{2,0},{4,2},{6,4},{3,1},{5,3},{7,5},{10,8},{12,10},{14,12},{11,9},... | collective-permute-start | bytes 983048 | tf_op jit(solution)/shard_map/ppermute | solution.py:772
  632.6 58.4 %collective-permute-start.58 = (bf16[256,640]{1,0:T(8,128)(2,1)}, bf16[256,640]{1,0:T(8,128)(2,1)}, u32[]{:S(2)}, u32[]{:S(2)}) collective-permute-start(bf16[256,640]{1,0:T(8,128)(2,1)} %add_convert_fusion.8), channel_id=1, source_target_pairs={{4,0},{6,2},{5,1},{7,3},{12,8},{14,10},{13,9},{15,11},{20,16},{22,... | collective-permute-start | bytes 983048 | tf_op jit(solution)/shard_map/ppermute | solution.py:772
  633.9 57.1 %collective-permute-start.59 = (bf16[256,640]{1,0:T(8,128)(2,1)}, bf16[256,640]{1,0:T(8,128)(2,1)}, u32[]{:S(2)}, u32[]{:S(2)}) collective-permute-start(bf16[256,640]{1,0:T(8,128)(2,1)} %add_convert_fusion.7), channel_id=1, source_target_pairs={{6,0},{7,1},{14,8},{15,9},{22,16},{23,17},{30,24},{31,25}} | collective-permute-start | bytes 983048 | tf_op jit(solution)/shard_map/ppermute | solution.py:772
  645.3 71.9 %collective-permute-start.76 = (bf16[3,256,768]{2,1,0:T(8,128)(2,1)}, bf16[3,256,768]{2,1,0:T(8,128)(2,1)}, u32[]{:S(2)}, u32[]{:S(2)}) collective-permute-start(bf16[3,256,768]{2,1,0:T(8,128)(2,1)} %bitcast.233), channel_id=1, source_target_pairs={{1,8},{8,1},{3,10},{10,3},{5,12},{12,5},{7,14},{14,7},{17,24},{24,... | collective-permute-start | bytes 3538952 | tf_op jit(solution)/shard_map/ppermute | solution.py:765
  708.3 17.7 %collective-permute-start.62 = (bf16[2,4,2,64,640]{4,3,1,0,2:T(8,128)(2,1)}, bf16[2,4,2,64,640]{4,3,1,0,2:T(8,128)(2,1)}, u32[]{:S(2)}, u32[]{:S(2)}) collective-permute-start(bf16[2,4,2,64,640]{4,3,1,0,2:T(8,128)(2,1)} %bitcast.211), channel_id=1, source_target_pairs={{0,8},{8,0},{1,9},{9,1},{2,10},{10,2},{3,11},{11,3},{4,12},{12,4},... | collective-permute-start | bytes 3932168 | tf_op jit(solution)/shard_map/ppermute | solution.py:725
  (93 other events, 1236.4 us)
Sparse Core Ops, SparseCore 0:
  123.3 116.3 all-gather.4
  241.8 101.1 all-gather.6
  385.6 121.9 reduce-scatter.2
  527.0 109.8 reduce-scatter.4

commit v3 on v2

--- a/solution.py
+++ b/solution.py
@@ -159,6 +159,7 @@
 
 
 def attend_back_kernel(
+    row,
     pieces,
     heads_kv,
     grouping,
@@ -178,7 +179,7 @@
     dq_ref, gain_rows_ref = refs[pieces : pieces + 2]
     dkv_refs = refs[pieces + 2 : 2 * pieces + 2]
     q_heads, do_heads, k_heads, v_heads, dk_heads, dv_heads, mask_ref = refs[2 * pieces + 2 :]
-    row, group = pl.program_id(0), pl.program_id(1)
+    group = pl.program_id(0)
     size, head_dim = segq_ref.shape[1], k_heads.shape[2]
 
     @pl.when(group == 0)
@@ -248,7 +249,7 @@
 
 
 def attend_back_call(
-    heads_kv, grouping, bases, query_b, grad_att, seg_here, seg_all, logs, query_pre, gain, cosine, sine, kv_pieces
+    row, heads_kv, grouping, bases, query_b, grad_att, seg_here, seg_all, logs, query_pre, gain, cosine, sine, kv_pieces
 ):
     pieces = len(kv_pieces)
     rows, size = seg_here.shape
@@ -257,37 +258,36 @@
     width = heads_kv * block
     keys = pieces * size
     kv_width = 2 * heads_kv * head_dim
-    row_block = lambda w: pl.BlockSpec((size, w), lambda r, g: (r, 0))
-    column_block = pl.BlockSpec((size, block), lambda r, g: (r, g))
-    whole = lambda a: pl.BlockSpec(a.shape, lambda r, g: (0,) * a.ndim)
+    row_block = lambda w: pl.BlockSpec((size, w), lambda g: (row, 0))
+    whole = lambda a: pl.BlockSpec(a.shape, lambda g: (0,) * a.ndim)
     low, full = jnp.bfloat16, jnp.float32
     heads = lambda n, t: pltpu.VMEM((heads_kv, n, head_dim), t)
     return pl.pallas_call(
-        functools.partial(attend_back_kernel, pieces, heads_kv, grouping),
-        grid=(rows, heads_kv),
+        functools.partial(attend_back_kernel, row, pieces, heads_kv, grouping),
+        grid=(heads_kv,),
         out_shape=[
-            jax.ShapeDtypeStruct((rows * size, width), low),
-            jax.ShapeDtypeStruct((rows, heads_kv, 1, block), full),
+            jax.ShapeDtypeStruct((size, width), low),
+            jax.ShapeDtypeStruct((heads_kv, 1, block), full),
         ]
-        + [jax.ShapeDtypeStruct((rows * size, kv_width), low)] * pieces,
+        + [jax.ShapeDtypeStruct((size, kv_width), low)] * pieces,
         in_specs=[
             pl.BlockSpec(memory_space=pltpu.SMEM),
             row_block(width),
             row_block(width),
             whole(seg_here),
             whole(seg_all),
-            pl.BlockSpec((None, None, 1, grouping * size), lambda r, g: (r, g, 0, 0)),
-            column_block,
+            pl.BlockSpec((None, None, 1, grouping * size), lambda g: (row, g, 0, 0)),
+            pl.BlockSpec((size, block), lambda g: (row, g)),
             whole(gain),
             row_block(cosine.shape[1]),
             row_block(sine.shape[1]),
         ]
         + [row_block(kv_width)] * pieces,
         out_specs=[
-            column_block,
-            pl.BlockSpec((None, None, 1, block), lambda r, g: (r, g, 0, 0)),
+            pl.BlockSpec((size, block), lambda g: (0, g)),
+            pl.BlockSpec((None, 1, block), lambda g: (g, 0, 0)),
         ]
-        + [row_block(kv_width)] * pieces,
+        + [pl.BlockSpec((size, kv_width), lambda g: (0, 0))] * pieces,
         scratch_shapes=[
             heads(grouping * size, low),
             heads(grouping * size, low),
@@ -299,9 +299,9 @@
         ],
         compiler_params=pltpu.CompilerParams(vmem_limit_bytes=60 * 1024 * 1024),
         cost_estimate=pl.CostEstimate(
-            flops=10 * rows * size * keys * width * 4,
-            bytes_accessed=8 * rows * size * width + 8 * rows * keys * heads_kv * head_dim,
-            transcendentals=rows * heads_kv * grouping * size * keys,
+            flops=10 * size * keys * width * 4,
+            bytes_accessed=8 * size * width + 8 * keys * heads_kv * head_dim,
+            transcendentals=heads_kv * grouping * size * keys,
         ),
     )(bases, query_b, grad_att, seg_here, seg_all, logs, query_pre, gain, cosine, sine, *kv_pieces)
 
@@ -832,17 +832,22 @@
     return [values, from_x, from_y, from_xy]
 
 
-def scatter_tokens(blocks):
-    own, to_x, to_y, to_xy = blocks
-    half = own.shape[1] // 2
-    via_x = x_swap(to_xy[:, :half])
-    via_y = y_swap(to_xy[:, half:])
+def scatter_corner(blocks):
+    half = blocks[3].shape[1] // 2
+    return x_swap(blocks[3][:, :half]), y_swap(blocks[3][:, half:])
+
+
+def scatter_sides(blocks, via_x, via_y):
+    _, to_x, to_y, _ = blocks
+    half = to_x.shape[1] // 2
     to_y = jnp.concatenate([add_low(to_y[:, :half], via_x), to_y[:, half:]], axis=1)
     to_x = jnp.concatenate([to_x[:, :half], add_low(to_x[:, half:], via_y)], axis=1)
+    return x_swap(to_x), y_swap(to_y)
+
+
+def scatter_total(blocks, from_x, from_y):
     return (
-        own.astype(jnp.float32)
-        + x_swap(to_x).astype(jnp.float32)
-        + y_swap(to_y).astype(jnp.float32)
+        blocks[0].astype(jnp.float32) + from_x.astype(jnp.float32) + from_y.astype(jnp.float32)
     )
 
 
@@ -891,15 +896,12 @@
     for row in range(rows_here):
         start = ((row_place * rows_here + row) * seq_count + seq_place) * seg_tok
         shared = put(shared, segment_ids[row], 2 * feature_count + start)
-    shared = shared.reshape(-1, 128)
-    shared = shared + x_swap(shared)
-    shared = shared + y_swap(shared)
     cotangent_here = cotangent.reshape(tokens_here, feature_count)
-    cot_own = hold(cotangent_here, shared)
-    cot_x, cot_y = x_swap(cot_own), y_swap(cot_own)
-    shared = sum_over(shared, ("core", "z"))
+    shared = sum_over(shared.reshape(-1, 128), ("core", "z"))
     qkv_here = jnp.concatenate([w_query, w_key, w_value], axis=1)
-    qkv_own, shared = together(jnp.stack(direct_gather(qkv_here)), shared)
+    qkv_own, shared = together(
+        jnp.stack(direct_gather(qkv_here)), sum_over(shared, ("x", "y"))
+    )
     shared = shared.reshape(-1)
     attn_gain = shared[:feature_count].reshape(1, -1)
     ffn_gain = shared[feature_count : 2 * feature_count].reshape(1, -1)
@@ -908,11 +910,9 @@
     seg_here = segment_ids.astype(jnp.float32)
 
     qkv_width = qkv_own.shape[2]
-    cut = 1024
+    cut = 512
     out_own = turn(jnp.stack(direct_gather(w_out)), (planes - z_at) % planes)
-    qkv_x, qkv_y, out_own, cot_x, cot_y = together(
-        x_swap(qkv_own), y_swap(qkv_own), out_own, cot_x, cot_y
-    )
+    qkv_x, qkv_y, out_own = together(x_swap(qkv_own), y_swap(qkv_own), out_own)
     down_turned = w_down.T
     ffn_width = w_gate.shape[1]
     ffn_cut = (ffn_width // 256 + 1) * 128
@@ -920,13 +920,11 @@
         jnp.stack([w[:, first:last] for w in (w_gate, w_up, down_turned)])
         for first, last in ((0, ffn_cut), (ffn_cut, ffn_width))
     ]
-    qkv_a, qkv_b, out_x, first_stack = together(
+    qkv_a, qkv_b, first_stack = together(
         y_swap(qkv_x[..., :cut]),
         x_swap(qkv_y[..., cut:]),
-        x_swap(out_own),
         corner(hold(stacks[0], qkv_x)),
     )
-    out_block = in_order(out_own, out_x, x_at, 0)
     qkv_pieces = [qkv_own, qkv_x, qkv_y, qkv_a, qkv_b]
     qkv_pieces += [core_swap(piece) for piece in qkv_pieces]
     spots = [(0, 0, 0, 0), (1, 0, 0, 0), (0, 1, 0, 0), (1, 1, 0, 0), (1, 1, 0, cut)]
@@ -944,23 +942,26 @@
         spots, qkv_pieces,
     )
 
-    half = feature_count // 2
-    near = y_swap(kv_here)
-    *kv_far, out_y, cot_a, cot_b, second_stack = together(
+    cot_own = hold(cotangent_here, kv_here)
+    *kv_far, near, out_y, cot_x, cot_y = together(
         *[chain(kv_here, t) for t in range(1, planes)],
-        y_swap(hold(out_block, kv_here)),
-        y_swap(hold(cot_x[:, :half], kv_here)),
-        x_swap(hold(cot_y[:, half:], kv_here)),
-        corner(hold(stacks[1], kv_here)),
+        y_swap(kv_here),
+        y_swap(hold(out_own, kv_here)),
+        x_swap(cot_own),
+        y_swap(cot_own),
+    )
+    out_block = in_order(out_own, out_y, y_at, 1)
+    kv_own = [kv_here] + list(kv_far)
+    *kv_other, out_x, second_stack = together(
+        *[y_swap(piece) for piece in kv_far],
+        x_swap(out_block),
+        corner(hold(stacks[1], kv_far[-1])),
     )
     parts = [gathered_first, lax.all_gather(second_stack, ("core", "z"), axis=0)]
-    out_block = in_order(out_block, out_y, y_at, 2)
-    kv_own = [kv_here] + list(kv_far)
-    *kv_other, out_core = together(
-        near, *[y_swap(piece) for piece in kv_far], core_swap(out_block)
-    )
-    out_full = in_order(out_block, out_core, core_at, 1).reshape(-1, feature_count)
-    cot_blocks = [cotangent_here, cot_x, cot_y, jnp.concatenate([cot_a, cot_b], axis=1)]
+    cot_xy = x_swap(hold(cot_y, out_x))
+    kv_other = [near] + list(kv_other)
+    out_block = in_order(out_block, out_x, x_at, 0)
+    cot_blocks = [cotangent_here, cot_x, cot_y, cot_xy]
     kv_pieces, bases = [], [seq_place * seg_tok]
     for t in range(planes):
         for dy, piece in enumerate((kv_own[t], kv_other[t])):
@@ -970,10 +971,12 @@
     attended_b, logs = attend_call(
         heads_kv, grouping, bases, query_b, seg_here, seg_all, kv_pieces
     )
+    attended_b, out_core = together(attended_b, core_swap(out_block))
+    out_full = in_order(out_block, out_core, core_at, 1).reshape(-1, feature_count)
     residual = inputs_here.astype(jnp.float32)
     middle = residual + jnp.dot(attended_b, out_full, preferred_element_type=jnp.float32)
     ffn_in = rms_apply(middle, ffn_gain).astype(low)
-    ffn_blocks = gather_tokens(ffn_in)
+    ffn_blocks = gather_tokens(hold(ffn_in, cot_xy))
 
     before, where = None, place
     hidden_parts, home, sums = [], [], []
@@ -989,14 +992,13 @@
         both = add_low(own, core_swap(other))
         where = hold(place, both) if not sums else place
         sums.append(lax.psum_scatter(both, "z", scatter_dimension=0))
-    home = [corner(mine).astype(jnp.float32) for mine in sums]
-    grad_ffn_in = scatter_tokens(before)
-    down_blocks = down_call(planes, hold(place, own), hidden_parts, parts)
-    down_blocks = hold(tuple(down_blocks), grad_ffn_in)
-    down_mine = scatter_tokens(down_blocks)
-    home = jnp.concatenate(home, axis=2)
-    output_b = (middle + down_mine).astype(low).reshape(inputs.shape)
-    grad_ffn_in = hold(grad_ffn_in, both)
+    via_x, via_y, last_own = together(*scatter_corner(before), own)
+    from_x, from_y, both, *down_blocks = together(
+        *scatter_sides(before, via_x, via_y),
+        both,
+        *down_call(planes, hold(place, last_own), hidden_parts, parts),
+    )
+    grad_ffn_in = scatter_total(before, from_x, from_y)
     grad_mid_ffn, gain_ffn_rows = rms_back(middle, ffn_gain, grad_ffn_in)
     grad_middle = cotangent_here.astype(jnp.float32) + grad_mid_ffn
     grad_gain_ffn = jnp.sum(gain_ffn_rows, axis=0)
@@ -1022,38 +1024,79 @@
             total = total + ring(block[t], t).astype(jnp.float32)
         return total
 
-    out_core = over_core(transposed_times(attended_b, grad_branch).astype(low))
-    result = attend_back_call(
-        heads_kv, grouping, hold(bases, out_core, sums[0], *down_blocks), query_b, grad_attended,
-        seg_here, seg_all, logs, query_pre, gain_q, cosine, sine, kv_pieces,
-    )
-    grad_query_b, gain_q_rows, dkv = result[0], result[1], result[2:]
-    query_core = over_core(transposed_times(normed, grad_query_b).astype(low))
-    *pairs, query_core, out_x = together(
-        *[add_low(dkv[2 * t], y_swap(dkv[2 * t + 1])) for t in range(planes)],
-        query_core,
-        over_x(hold(out_core, down_mine)),
-    )
-    *far, query_x, out_y = together(
-        *[chain(pairs[t], -t) for t in range(1, planes)], over_x(query_core), over_y(out_x, 1)
-    )
-    moving = pairs[0].astype(jnp.float32)
-    for piece in far:
-        moving = moving + piece.astype(jnp.float32)
-    moving = hold(moving, sums[1])
+    def back(row, bases):
+        result = attend_back_call(
+            row, heads_kv, grouping, bases, query_b, grad_attended, seg_here, seg_all, logs,
+            query_pre, gain_q, cosine, sine, kv_pieces,
+        )
+        return result[0], result[1], result[2:]
+
+    def over_pairs(dkv):
+        return [add_low(dkv[2 * t], y_swap(dkv[2 * t + 1])) for t in range(planes)]
+
+    def over_planes(pairs):
+        return [pairs[0]] + [chain(pairs[t], -t) for t in range(1, planes)]
+
+    grad_rows, gain_rows, pairs = [], [], []
+    for row in range(rows_here):
+        start = bases if row == 0 else hold(bases, grad_rows[-1])
+        grad_row, gain_row, dkv = back(row, start)
+        if row == 0:
+            via_x, via_y, grad_row = together(*scatter_corner(down_blocks), grad_row)
+        if row == 1:
+            from_x, from_y, out_core, grad_row, *pairs[0] = together(
+                *scatter_sides(down_blocks, via_x, via_y),
+                over_core(
+                    transposed_times(hold(attended_b, grad_rows[0]), grad_branch).astype(low)
+                ),
+                grad_row,
+                *pairs[0],
+            )
+        grad_rows.append(grad_row)
+        gain_rows.append(gain_row)
+        pairs.append(over_pairs(dkv))
+    down_mine = scatter_total(down_blocks, from_x, from_y)
+    grad_query_b = jnp.concatenate(grad_rows, axis=0)
+    gain_q_rows = jnp.stack(gain_rows)
+    grad_query_w = transposed_times(normed, grad_query_b).astype(low)
+    middle_q = width_q // 2
+    *tied, query_a, query_b2, out_x, first_sum = together(
+        *[piece for group in pairs[:-1] for piece in over_planes(group)],
+        *pairs[-1],
+        over_core(grad_query_w[:, :middle_q]),
+        over_core(grad_query_w[:, middle_q:]),
+        over_x(out_core),
+        sums[0],
+    )
+    landed = [tied[i * planes : (i + 1) * planes] for i in range(rows_here)]
+    *last, query_a, query_b2, out_y = together(
+        *over_planes(landed[-1]), over_x(query_a), over_y(query_b2, 2), over_y(out_x, 1)
+    )
+    landed[-1] = last
+    moving = []
+    for pieces in landed:
+        total = pieces[0].astype(jnp.float32)
+        for piece in pieces[1:]:
+            total = total + piece.astype(jnp.float32)
+        moving.append(total)
+    moving = jnp.concatenate(moving, axis=0)
     grad_kv_b, gain_k_rows = keys_back_call(head_dim, moving, kv_pre, gain_k, cosine, sine)
-    kv_core, query_y, grad_out_mine = together(
+    kv_core, query_a, query_b2, grad_out_mine = together(
         over_core(transposed_times(normed, grad_kv_b).astype(low)),
-        over_y(query_x, 1),
+        over_y(query_a, 1),
+        over_x(query_b2),
         over_z(out_y),
     )
     grad_qkv_b = jnp.concatenate([grad_query_b, grad_kv_b], axis=1)
     grad_inputs, grad_gain_attn = input_call(
-        hold(place, kv_core), grad_qkv_b, inputs_here, attn_gain, grad_middle, spots,
-        qkv_pieces,
-    )
-    kv_y, grad_query_mine = together(over_y(kv_core, 2), over_z(query_y))
+        hold(place, kv_core), grad_qkv_b, inputs_here, attn_gain, grad_middle, spots, qkv_pieces
+    )
+    kv_y, last_sum = together(over_y(kv_core, 2), sums[1])
     grad_kv_mine = over_z(over_x(kv_y))
+    grad_query_mine = over_z(jnp.concatenate([query_a, query_b2], axis=2))
+    home = [corner(mine).astype(jnp.float32) for mine in (first_sum, last_sum)]
+    home = jnp.concatenate(home, axis=2)
+    output_b = (middle + down_mine).astype(low).reshape(inputs.shape)
     gain_q_rows = jnp.sum(gain_q_rows.reshape(-1, head_dim), axis=0)
     gain_k_rows = jnp.sum(gain_k_rows.reshape(-1, head_dim)[:heads_kv], axis=0)
     small = jnp.concatenate([grad_gain_attn.reshape(-1), grad_gain_ffn, gain_q_rows, gain_k_rows])

time: 797 us -> 764 us (0.959)
  waiting for transfers between devices: 336 us -> 289 us
  starting transfers between devices: 97 us -> 110 us
    ppermute x57 -> x63, waiting for transfers between devices: 264 us -> 199 us  [swap(): return lax.ppermute(values, axis_name, [(i, i ^ bit) for i in range(count)])]
    ppermute x15, waiting for transfers between devices: 10.1 us -> 21.8 us  [ring(): lax.ppermute(values, 'z', [(i, (i + shift) % count) for i in range(count)])]
    ppermute x6 -> x9, starting transfers between devices: 17 us -> 24.9 us  [chain(): return lax.ppermute(values, 'z', moves)]
    ppermute x6 -> x9, waiting for transfers between devices: 60.4 us -> 67.2 us  [chain(): return lax.ppermute(values, 'z', moves)]
    ppermute x57 -> x63, starting transfers between devices: 47.2 us -> 53.7 us  [swap(): return lax.ppermute(values, axis_name, [(i, i ^ bit) for i in range(count)])]
    convert_element_type x19 -> x26, other arithmetic: 31.3 us -> 36.7 us  [add_low(): (left.astype(jnp.float32) + right.astype(jnp.float32)).astype(jnp.bfloat16)]
    pallas_call x1 -> x2, Pallas kernels: 30.9 us -> 33.5 us  [attend_back_call(): pl.pallas_call(functools.partial(attend_back_kernel, row, pieces, heads_k...]
  transfers between devices with their start and end apart: 86 -> 95, of which waited for: 46 -> 39; matrix products, arithmetic and copies ran while one was open for 18% -> 18% of each run, Pallas kernels for 23% -> 26%
where the time goes in v3:
time: 764 us; the launch traced here: 752 us
  waiting for transfers between devices  289 us (38%)
  Pallas kernels  198 us (26%)
  starting transfers between devices  110 us (14%)
  other arithmetic  81.4 us (11%)
  local copies, waits for them, and re-layouts  48 us (6%)
  between operations  15.4 us (2%)
  matrix products  11.1 us (1%)
    ppermute x63, waiting for transfers between devices, swap(): return lax.ppermute(values, axis_name, [(i, i ^ bit) for i in range(count)])  199 us
    ppermute x9, waiting for transfers between devices, chain(): return lax.ppermute(values, 'z', moves)  67.2 us
    pallas_call x2, Pallas kernels, ffn_call(): pl.pallas_call(functools.partial(ffn_kernel, planes, blocks, chained), ou...  66.5 us
    ppermute x63, starting transfers between devices, swap(): return lax.ppermute(values, axis_name, [(i, i ^ bit) for i in range(count)])  53.7 us
    pallas_call x2, Pallas kernels, weight_grad_call(): pl.pallas_call(functools.partial(weight_grad_kernel, blocks), out_shape=[...  39.7 us
    convert_element_type x26, other arithmetic, add_low(): (left.astype(jnp.float32) + right.astype(jnp.float32)).astype(jnp.bfloat16)  36.7 us
    pallas_call x2, Pallas kernels, attend_back_call(): pl.pallas_call(functools.partial(attend_back_kernel, row, pieces, heads_k...  33.5 us
    ppermute x15, starting transfers between devices, ring(): lax.ppermute(values, 'z', [(i, (i + shift) % count) for i in range(count)])  25.1 us
  transfers between devices with their start and end apart: 95, of which 39 were waited for; matrix products, arithmetic and copies ran while one was open for 18% of the time, Pallas kernels for 26%

profile of v3, /device:TPU:0, one launch (start us, length us, event | category | flops | bytes accessed | tf_op | source)
XLA Modules:
  0.0 752.3 jit_solution(5715901321579422180)
XLA Ops:
  7.2 5.1 collective-permute-start.10
  23.7 8.9 %collective-permute-done.4 = f32[96,128]{1,0:T(8,128)S(1)} collective-permute-done((f32[96,128]{1,0:T(8,128)S(1)}, f32[96,128]{1,0:T(8,128)S(1)}, u32[]{:S(2)}, u32[]{:S(2)}) %collective-permute-start.4) | collective-permute-done | bytes 49184 | tf_op jit(solution)/shard_map/ppermute | solution.py:725
  33.9 3.8 collective-permute-done.5
  46.3 9.2 %collective-permute-done.1 = bf16[64,1920]{1,0:T(8,128)(2,1)S(1)} collective-permute-done((bf16[64,1920]{1,0:T(8,128)(2,1)S(1)}, bf16[64,1920]{1,0:T(8,128)(2,1)S(1)}, u32[]{:S(2)}, u32[]{:S(2)}) %collective-permute-start.1) | collective-permute-done | bytes 245792 | tf_op jit(solution)/shard_map/ppermute | solution.py:730
  61.6 18.7 %collective-permute-done.8.refs_1_ = bf16[4,64,1920]{2,1,0:T(8,128)(2,1)S(1)} collective-permute-done((bf16[4,64,1920]{2,1,0:T(8,128)(2,1)S(1)}, bf16[4,64,1920]{2,1,0:T(8,128)(2,1)S(1)}, u32[]{:S(2)}, u32[]{:S(2)}) %collective-permute-start.8) | collective-permute-done | bytes 983072 | tf_op jit(solution)/shard_map/ppermute | solution.py:725
  91.4 15.8 %collective-permute-done.13.refs_3_ = bf16[4,64,512]{2,1,0:T(8,128)(2,1)} collective-permute-done((bf16[4,64,512]{2,1,0:T(8,128)(2,1)}, bf16[4,64,512]{2,1,0:T(8,128)(2,1)}, u32[]{:S(2)}, u32[]{:S(2)}) %collective-permute-start.13) | collective-permute-done | bytes 262176 | tf_op jit(solution)/shard_map/ppermute | solution.py:725
  114.5 12.3 %shard_map.246 = (bf16[256,2048]{1,0:T(8,128)(2,1)}, f32[256,1280]{1,0:T(8,128)}, f32[256,640]{1,0:T(8,128)}, bf16[256,1280]{1,0:T(8,128)(2,1)}, bf16[256,640]{1,0:T(8,128)(2,1)}) custom-call(s32[4]{0:T(128)} %pad_add_fusion.place_ref, bf16[256,2048]{1,0:T(8,128)(2,1)} %bitcast.223, f32[1,2048]{1,0:T(1,128)} %bitcast.240, ...), custom_call_target="tpu_custom_call" | custom-call | flops 2013265920 | bytes 13107200 | tf_op jit(solution)/shard_map/pallas_call | solution.py:366
  131.9 4.3 collective-permute-start.22
  138.0 9.3 %collective-permute-done.21.refs_2_ = bf16[256,640]{1,0:T(8,128)(2,1)S(1)} collective-permute-done((bf16[256,640]{1,0:T(8,128)(2,1)}, bf16[256,640]{1,0:T(8,128)(2,1)S(1)}, u32[]{:S(2)}, u32[]{:S(2)}) %collective-permute-start.21) | collective-permute-done | bytes 327712 | tf_op jit(solution)/shard_map/ppermute | solution.py:772
  147.3 10.9 %collective-permute-start.23 = (bf16[256,640]{1,0:T(8,128)(2,1)}, bf16[256,640]{1,0:T(8,128)(2,1)S(1)}, u32[]{:S(2)}, u32[]{:S(2)}) collective-permute-start(bf16[256,640]{1,0:T(8,128)(2,1)} %get-tuple-element.168.refs_0_), channel_id=1, source_target_pairs={{0,6},{1,7},{8,14},{9,15},{16,22},{17,23},{24,30},{25,31}} | collective-permute-start | bytes 983048 | tf_op jit(solution)/shard_map/ppermute | solution.py:772
  158.2 3.1 collective-permute-done.22.refs_4_
  163.2 11.7 %collective-permute-done.23.refs_6_ = bf16[256,640]{1,0:T(8,128)(2,1)S(1)} collective-permute-done((bf16[256,640]{1,0:T(8,128)(2,1)}, bf16[256,640]{1,0:T(8,128)(2,1)S(1)}, u32[]{:S(2)}, u32[]{:S(2)}) %collective-permute-start.23) | collective-permute-done | bytes 327712 | tf_op jit(solution)/shard_map/ppermute | solution.py:772
  183.3 23.1 %collective-permute-done.28.refs_3_ = bf16[256,640]{1,0:T(8,128)(2,1)} collective-permute-done((bf16[256,640]{1,0:T(8,128)(2,1)}, bf16[256,640]{1,0:T(8,128)(2,1)}, u32[]{:S(2)}, u32[]{:S(2)}) %collective-permute-start.28) | collective-permute-done | bytes 327712 | tf_op jit(solution)/shard_map/ppermute | solution.py:725
  206.4 3.5 collective-permute-done.29.refs_5_
  209.9 3.5 collective-permute-done.30.refs_7_
  219.9 18.4 %shard_map.247 = (bf16[256,1280]{1,0:T(8,128)(2,1)}, f32[2,5,1,512]{3,2,1,0:T(1,128)}) custom-call(s32[9]{0:T(128)} %stack.169.base_ref, bf16[256,1280]{1,0:T(8,128)(2,1)} %get-tuple-element.167.q_ref, f32[2,128]{1,0:T(2,128)} %convert_element_type.442.segq_ref, f32[16,128]{1,0:T(8,128)} %fusion.27.segk_ref, bf16[256,640]{1,0:T(8,128)(2,1)} %get-tuple-element.168.refs_0_, ...), custom_call_target="tpu_custom_call" | custom-call | flops 5368709120 | bytes 3932160 | tf_op jit(solution)/shard_map/pallas_call | solution.py:128
  238.3 3.9 maximum_select_fusion
  247.6 22.6 %collective-permute-done.35.refs_1_ = bf16[256,2048]{1,0:T(8,128)(2,1)S(1)} collective-permute-done((bf16[256,2048]{1,0:T(8,128)(2,1)S(1)}, bf16[256,2048]{1,0:T(8,128)(2,1)S(1)}, u32[]{:S(2)}, u32[]{:S(2)}) %collective-permute-start.35) | collective-permute-done | bytes 1048608 | tf_op jit(solution)/shard_map/ppermute | solution.py:725
  272.8 10.9 %collective-permute-done.37 = bf16[256,1024]{1,0:T(8,128)(2,1)S(1)} collective-permute-done((bf16[256,1024]{1,0:T(8,128)(2,1)S(1)}, bf16[256,1024]{1,0:T(8,128)(2,1)S(1)}, u32[]{:S(2)}, u32[]{:S(2)}) %collective-permute-start.37) | collective-permute-done | bytes 524320 | tf_op jit(solution)/shard_map/ppermute | solution.py:725
  285.5 40.3 %shard_map.248 = (bf16[256,896]{1,0:T(8,128)(2,1)}, bf16[256,896]{1,0:T(8,128)(2,1)}, bf16[256,896]{1,0:T(8,128)(2,1)}, bf16[256,2048]{1,0:T(8,128)(2,1)}, bf16[...) custom-call(s32[4]{0:T(128)} %pad_add_fusion.place_ref, ...), custom_call_target="tpu_custom_call" | custom-call | flops 18790481920 | bytes 27787264 | tf_op jit(solution)/shard_map/pallas_call | solution.py:562
  325.9 21.7 %shard_map.249 = (bf16[4,3,256,896]{3,2,1,0:T(8,128)(2,1)}, bf16[4,3,256,896]{3,2,1,0:T(8,128)(2,1)}) custom-call(s32[4]{0:T(128)} %pad_add_fusion.place_ref, bf16[256,2048]{1,0:T(8,128)(2,1)} %copy-done.24, bf16[256,2048]{1,0:T(8,128)(2,1)} %copy-done.34, bf16[256,2048]{1,0:T(8,128)(2,1)} %copy-done.35, ...), custom_call_target="tpu_custom_call" | custom-call | flops 11274289152 | bytes 16515072 | tf_op jit(solution)/shard_map/pallas_call | solution.py:612
  347.6 9.2 %collective-permute-done.39 = bf16[4,3,256,896]{3,2,1,0:T(8,128)(2,1)S(1)} collective-permute-done((bf16[4,3,256,896]{3,2,1,0:T(8,128)(2,1)}, bf16[4,3,256,896]{3,2,1,0:T(8,128)(2,1)S(1)}, u32[]{:S(2)}, u32[]{:S(2)}) %collective-permute-start.39) | collective-permute-done | bytes 5505056 | tf_op jit(solution)/shard_map/ppermute | solution.py:725
  356.9 6.6 add_convert_fusion
  364.0 26.2 %shard_map.250 = (bf16[256,768]{1,0:T(8,128)(2,1)}, bf16[256,768]{1,0:T(8,128)(2,1)}, bf16[256,768]{1,0:T(8,128)(2,1)}, bf16[256,2048]{1,0:T(8,128)(2,1)}, bf16[...) custom-call(s32[4]{0:T(128)} %pad_add_fusion.place_ref, ...), custom_call_target="tpu_custom_call" | custom-call | flops 16106127360 | bytes 26214400 | tf_op jit(solution)/shard_map/pallas_call | solution.py:562
  390.2 18.1 %shard_map.251 = (bf16[4,3,256,768]{3,2,1,0:T(8,128)(2,1)}, bf16[4,3,256,768]{3,2,1,0:T(8,128)(2,1)}) custom-call(s32[4]{0:T(128)} %pad_add_fusion.place_ref, bf16[256,2048]{1,0:T(8,128)(2,1)} %copy-done.24, bf16[256,2048]{1,0:T(8,128)(2,1)} %copy-done.34, bf16[256,2048]{1,0:T(8,128)(2,1)} %copy-done.35, ...), custom_call_target="tpu_custom_call" | custom-call | flops 9663676416 | bytes 14155776 | tf_op jit(solution)/shard_map/pallas_call | solution.py:612
  414.3 10.9 %collective-permute-done.40 = bf16[256,1024]{1,0:T(8,128)(2,1)} collective-permute-done((bf16[256,1024]{1,0:T(8,128)(2,1)}, bf16[256,1024]{1,0:T(8,128)(2,1)}, u32[]{:S(2)}, u32[]{:S(2)}) %collective-permute-start.40) | collective-permute-done | bytes 524320 | tf_op jit(solution)/shard_map/ppermute | solution.py:725
  432.4 13.7 %shard_map.252 = (bf16[256,2048]{1,0:T(8,128)(2,1)}, bf16[256,2048]{1,0:T(8,128)(2,1)}, bf16[256,2048]{1,0:T(8,128)(2,1)}, bf16[256,2048]{1,0:T(8,128)(2,1)}) custom-call(s32[4]{0:T(128)} %pad_add_fusion.place_ref, bf16[256,896]{1,0:T(8,128)(2,1)} %get-tuple-element.198.refs_16_.refs_0_, bf16[256,896]{1,0:T(8,128)(2,1)} %get-tuple-element.199.refs_17_.refs_1_, ...), custom_call_target="tpu_custom_call" | custom-call | flops 6979321856 | bytes 23592960 | tf_op jit(solution)/shard_map/pallas_call | solution.py:667
  446.2 7.2 add_convert_fusion.1
  462.8 2.9 subtract_add_fusion.mid_ref
  468.2 16.8 %shard_map.253 = (bf16[128,1280]{1,0:T(8,128)(2,1)}, f32[5,1,256]{2,1,0:T(1,128)}, bf16[128,640]{1,0:T(8,128)(2,1)}, bf16[128,640]{1,0:T(8,128)(2,1)}, bf16[128,...) custom-call(s32[9]{0:T(128)} %stack.169.base_ref, ...), custom_call_target="tpu_custom_call" | custom-call | flops 6710886400 | bytes 3932160 | tf_op jit(solution)/shard_map/pallas_call | solution.py:265
  491.4 3.4 convolution_convert_fusion.1
  509.0 16.6 %shard_map.254 = (bf16[128,1280]{1,0:T(8,128)(2,1)}, f32[5,1,256]{2,1,0:T(1,128)}, bf16[128,640]{1,0:T(8,128)(2,1)}, bf16[128,640]{1,0:T(8,128)(2,1)}, bf16[128,...) custom-call(s32[9]{0:T(128)} %stack.169.base_ref, ...), custom_call_target="tpu_custom_call" | custom-call | flops 6710886400 | bytes 3932160 | tf_op jit(solution)/shard_map/pallas_call | solution.py:265
  530.0 3.8 fusion
  549.8 19.9 %collective-permute-done.63 = bf16[4,2,40,2048]{3,2,0,1:T(8,128)(2,1)S(1)} collective-permute-done((bf16[4,2,40,2048]{3,2,0,1:T(8,128)(2,1)S(1)}, bf16[4,2,40,2048]{3,2,0,1:T(8,128)(2,1)S(1)}, u32[]{:S(2)}, u32[]{:S(2)}) %collective-permute-start.63) | collective-permute-done | bytes 1310752 | tf_op jit(solution)/shard_map/ppermute | solution.py:725
  572.7 18.1 %collective-permute-done.54 = bf16[128,640]{1,0:T(8,128)(2,1)S(1)} collective-permute-done((bf16[128,640]{1,0:T(8,128)(2,1)S(1)}, bf16[128,640]{1,0:T(8,128)(2,1)S(1)}, u32[]{:S(2)}, u32[]{:S(2)}) %collective-permute-start.54) | collective-permute-done | bytes 163872 | tf_op jit(solution)/shard_map/ppermute | solution.py:772
  590.7 21.6 %collective-permute-done.55 = bf16[128,640]{1,0:T(8,128)(2,1)S(1)} collective-permute-done((bf16[128,640]{1,0:T(8,128)(2,1)S(1)}, bf16[128,640]{1,0:T(8,128)(2,1)S(1)}, u32[]{:S(2)}, u32[]{:S(2)}) %collective-permute-start.55) | collective-permute-done | bytes 163872 | tf_op jit(solution)/shard_map/ppermute | solution.py:772
  617.6 3.3 add_convert_fusion.2
  625.2 18.7 %collective-permute-done.68 = bf16[2,4,64,640]{3,2,1,0:T(8,128)(2,1)S(1)} collective-permute-done((bf16[2,4,64,640]{3,2,1,0:T(8,128)(2,1)S(1)}, bf16[2,4,64,640]{3,2,1,0:T(8,128)(2,1)S(1)}, u32[]{:S(2)}, u32[]{:S(2)}) %collective-permute-start.68) | collective-permute-done | bytes 655392 | tf_op jit(solution)/shard_map/ppermute | solution.py:725
  649.4 3.5 collective-permute-done.66
  653.9 3.9 shard_map.255
  663.4 3.0 collective-permute-start.74
  668.1 4.5 collective-permute-done.73
  673.7 4.9 collective-permute-done.74
  681.8 5.7 collective-permute-done.71
  689.3 10.2 %shard_map.256 = (f32[256,2048]{1,0:T(8,128)}, f32[1,2048]{1,0:T(1,128)}) custom-call(s32[4]{0:T(128)} %pad_add_fusion.place_ref, bf16[256,1920]{1,0:T(8,128)(2,1)} %pad_maximum_fusion.9.g_ref, bf16[256,2048]{1,0:T(8,128)(2,1)} %bitcast.224, f32[1,2048]{1,0:T(1,128)} %bitcast.241, f32[256,2048]{1,0:T(8,128)} %copy-done, bf16[4,64,1920]{2,1,0:T(8,128)(2,1)} %copy-done.2, ...), custom_call_target="tpu_custom_call" | custom-call | flops 2013265920 | bytes 13107200 | tf_op jit(solution)/shard_map/pallas_call | solution.py:446
  713.9 2.9 collective-permute-start.78
  721.2 8.7 %collective-permute-done.90 = f32[33,128]{1,0:T(8,128)S(1)} collective-permute-done((f32[33,128]{1,0:T(8,128)S(1)}, f32[33,128]{1,0:T(8,128)S(1)}, u32[]{:S(2)}, u32[]{:S(2)}) %collective-permute-start.90) | collective-permute-done | bytes 16928 | tf_op jit(solution)/shard_map/ppermute | solution.py:725
  731.7 3.0 collective-permute-start.82
  (444 shorter events, 208.6 us)
Async XLA Ops:
  7.2 278.3 %all-gather.5.cloned.1.call-start = ((), (), s32[]{:S(2)}) async-start(), calls=%async_computation.4 | async-start | bytes 12386304 | tf_op jit(solution)/shard_map/all_gather | solution.py:932
  7.2 30.5 %collective-permute-start.10 = (bf16[40,2048]{1,0:T(8,128)(2,1)}, bf16[40,2048]{1,0:T(8,128)(2,1)S(1)}, u32[]{:S(2)}, u32[]{:S(2)}) collective-permute-start(bf16[40,2048]{1,0:T(8,128)(2,1)} %param.22), channel_id=1, source_target_pairs={{0,6},{2,0},{4,2},{6,4},{1,7},{3,1},{5,3},{7,5},{8,14},{10,8},{12,... | collective-permute-start | bytes 491528 | tf_op jit(solution)/shard_map/ppermute | solution.py:730
  12.3 28.1 %collective-permute-start.11 = (bf16[40,2048]{1,0:T(8,128)(2,1)}, bf16[40,2048]{1,0:T(8,128)(2,1)S(1)}, u32[]{:S(2)}, u32[]{:S(2)}) collective-permute-start(bf16[40,2048]{1,0:T(8,128)(2,1)} %param.22), channel_id=1, source_target_pairs={{0,4},{2,6},{4,0},{6,2},{1,5},{3,7},{5,1},{7,3},{8,12},{10,14},{12... | collective-permute-start | bytes 491528 | tf_op jit(solution)/shard_map/ppermute | solution.py:730
  12.3 30.3 %collective-permute-start.12 = (bf16[40,2048]{1,0:T(8,128)(2,1)}, bf16[40,2048]{1,0:T(8,128)(2,1)S(1)}, u32[]{:S(2)}, u32[]{:S(2)}) collective-permute-start(bf16[40,2048]{1,0:T(8,128)(2,1)} %param.22), channel_id=1, source_target_pairs={{0,2},{2,4},{4,6},{6,0},{1,3},{3,5},{5,7},{7,1},{8,10},{10,12},{12... | collective-permute-start | bytes 491528 | tf_op jit(solution)/shard_map/ppermute | solution.py:730
  17.4 28.8 %collective-permute-start = (bf16[64,1920]{1,0:T(8,128)(2,1)S(1)}, bf16[64,1920]{1,0:T(8,128)(2,1)}, u32[]{:S(2)}, u32[]{:S(2)}) collective-permute-start(bf16[64,1920]{1,0:T(8,128)(2,1)S(1)} %concatenate.107), channel_id=1, source_target_pairs={{0,6},{2,0},{4,2},{6,4},{1,7},{3,1},{5,3},{7,5},{8,14},{10,8},{12,... | collective-permute-start | bytes 737288 | tf_op jit(solution)/shard_map/ppermute | solution.py:730
  56.6 23.7 %collective-permute-start.8 = (bf16[4,64,1920]{2,1,0:T(8,128)(2,1)S(1)}, bf16[4,64,1920]{2,1,0:T(8,128)(2,1)S(1)}, u32[]{:S(2)}, u32[]{:S(2)}) collective-permute-start(bf16[4,64,1920]{2,1,0:T(8,128)(2,1)S(1)} %pad_maximum_fusion.8.refs_0_), channel_id=1, source_target_pairs={{0,16},{16,0},{1,17},{17,1},{2,18},{18,2},{3,19},{19,3},{4,20},{20... | collective-permute-start | bytes 2949128 | tf_op jit(solution)/shard_map/ppermute | solution.py:725
  58.2 23.4 %collective-permute-start.9 = (bf16[4,64,1920]{2,1,0:T(8,128)(2,1)S(1)}, bf16[4,64,1920]{2,1,0:T(8,128)(2,1)S(1)}, u32[]{:S(2)}, u32[]{:S(2)}) collective-permute-start(bf16[4,64,1920]{2,1,0:T(8,128)(2,1)S(1)} %pad_maximum_fusion.8.refs_0_), channel_id=1, source_target_pairs={{0,1},{1,0},{2,3},{3,2},{4,5},{5,4},{6,7},{7,6},{8,9},{9,8},{10,11... | collective-permute-start | bytes 2949128 | tf_op jit(solution)/shard_map/ppermute | solution.py:725
  84.2 23.0 %collective-permute-start.14 = (bf16[4,64,1408]{2,1,0:T(8,128)(2,1)}, bf16[4,64,1408]{2,1,0:T(8,128)(2,1)}, u32[]{:S(2)}, u32[]{:S(2)}) collective-permute-start(bf16[4,64,1408]{2,1,0:T(8,128)(2,1)} %slice.157), channel_id=1, source_target_pairs={{0,16},{16,0},{1,17},{17,1},{2,18},{18,2},{3,19},{19,3},{4,20},{20... | collective-permute-start | bytes 2162696 | tf_op jit(solution)/shard_map/ppermute | solution.py:725
  87.1 20.1 %collective-permute-start.13 = (bf16[4,64,512]{2,1,0:T(8,128)(2,1)}, bf16[4,64,512]{2,1,0:T(8,128)(2,1)}, u32[]{:S(2)}, u32[]{:S(2)}) collective-permute-start(bf16[4,64,512]{2,1,0:T(8,128)(2,1)} %slice.156), channel_id=1, source_target_pairs={{0,1},{1,0},{2,3},{3,2},{4,5},{5,4},{6,7},{7,6},{8,9},{9,8},{10,11... | collective-permute-start | bytes 786440 | tf_op jit(solution)/shard_map/ppermute | solution.py:725
  107.2 256.7 %all-gather.7.cloned.1.call-start = ((), (), s32[]{:S(2)}) async-start(), calls=%async_computation.5 | async-start | bytes 10616832 | tf_op jit(solution)/shard_map/all_gather | solution.py:960
  126.8 48.1 %collective-permute-start.26 = (bf16[256,2048]{1,0:T(8,128)(2,1)}, bf16[256,2048]{1,0:T(8,128)(2,1)}, u32[]{:S(2)}, u32[]{:S(2)}) collective-permute-start(bf16[256,2048]{1,0:T(8,128)(2,1)} %bitcast.33.refs_4_), channel_id=1, source_target_pairs={{0,16},{16,0},{1,17},{17,1},{2,18},{18,2},{3,19},{19,3},{4,20},{20... | collective-permute-start | bytes 3145736 | tf_op jit(solution)/shard_map/ppermute | solution.py:725
  128.5 46.4 %collective-permute-start.27 = (bf16[256,2048]{1,0:T(8,128)(2,1)}, bf16[256,2048]{1,0:T(8,128)(2,1)}, u32[]{:S(2)}, u32[]{:S(2)}) collective-permute-start(bf16[256,2048]{1,0:T(8,128)(2,1)} %bitcast.33.refs_4_), channel_id=1, source_target_pairs={{0,1},{1,0},{2,3},{3,2},{4,5},{5,4},{6,7},{7,6},{8,9},{9,8},{10,11... | collective-permute-start | bytes 3145736 | tf_op jit(solution)/shard_map/ppermute | solution.py:725
  131.9 29.4 %collective-permute-start.22 = (bf16[256,640]{1,0:T(8,128)(2,1)}, bf16[256,640]{1,0:T(8,128)(2,1)}, u32[]{:S(2)}, u32[]{:S(2)}) collective-permute-start(bf16[256,640]{1,0:T(8,128)(2,1)} %get-tuple-element.168.refs_0_), channel_id=1, source_target_pairs={{0,4},{2,6},{1,5},{3,7},{8,12},{10,14},{9,13},{11,15},{16,20},{18,... | collective-permute-start | bytes 983048 | tf_op jit(solution)/shard_map/ppermute | solution.py:772
  136.2 38.7 %collective-permute-start.25 = (bf16[4,40,2048]{2,1,0:T(8,128)(2,1)S(1)}, bf16[4,40,2048]{2,1,0:T(8,128)(2,1)S(1)}, u32[]{:S(2)}, u32[]{:S(2)}) collective-permute-start(bf16[4,40,2048]{2,1,0:T(8,128)(2,1)S(1)} %constant_dynamic-slice_fusion.9), channel_id=1, source_target_pairs={{0,1},{1,0},{2,3},{3,2},{4,5},{5,4},{6,7},{7,6},{8,9},{9,8},{10,11... | collective-permute-start | bytes 1966088 | tf_op jit(solution)/shard_map/ppermute | solution.py:725
  147.3 27.6 %collective-permute-start.23 = (bf16[256,640]{1,0:T(8,128)(2,1)}, bf16[256,640]{1,0:T(8,128)(2,1)S(1)}, u32[]{:S(2)}, u32[]{:S(2)}) collective-permute-start(bf16[256,640]{1,0:T(8,128)(2,1)} %get-tuple-element.168.refs_0_), channel_id=1, source_target_pairs={{0,6},{1,7},{8,14},{9,15},{16,22},{17,23},{24,30},{25,31}} | collective-permute-start | bytes 983048 | tf_op jit(solution)/shard_map/ppermute | solution.py:772
  177.1 36.3 %collective-permute-start.31 = (bf16[4,2,40,2048]{3,2,1,0:T(8,128)(2,1)}, bf16[4,2,40,2048]{3,2,1,0:T(8,128)(2,1)S(1)}, u32[]{:S(2)}, u32[]{:S(2)}) collective-permute-start(bf16[4,2,40,2048]{3,2,1,0:T(8,128)(2,1)} %maximum_select_fusion.3), channel_id=1, source_target_pairs={{0,16},{16,0},{1,17},{17,1},{2,18},{18,2},{3,19},{19,3},{4,20},{20... | collective-permute-start | bytes 3932168 | tf_op jit(solution)/shard_map/ppermute | solution.py:725
  177.9 28.5 %collective-permute-start.28 = (bf16[256,640]{1,0:T(8,128)(2,1)}, bf16[256,640]{1,0:T(8,128)(2,1)}, u32[]{:S(2)}, u32[]{:S(2)}) collective-permute-start(bf16[256,640]{1,0:T(8,128)(2,1)} %copy-done.60), channel_id=1, source_target_pairs={{0,1},{1,0},{2,3},{3,2},{4,5},{5,4},{6,7},{7,6},{8,9},{9,8},{10,11... | collective-permute-start | bytes 983048 | tf_op jit(solution)/shard_map/ppermute | solution.py:725
  180.2 29.8 %collective-permute-start.29 = (bf16[256,640]{1,0:T(8,128)(2,1)}, bf16[256,640]{1,0:T(8,128)(2,1)}, u32[]{:S(2)}, u32[]{:S(2)}) collective-permute-start(bf16[256,640]{1,0:T(8,128)(2,1)} %collective-permute-done.22.refs_4_), channel_id=1, source_target_pairs={{0,1},{1,0},{2,3},{3,2},{4,5},{5,4},{6,7},{7,6},{8,9},{9,8},{10,11... | collective-permute-start | bytes 983048 | tf_op jit(solution)/shard_map/ppermute | solution.py:725
  180.2 33.2 %collective-permute-start.30 = (bf16[256,640]{1,0:T(8,128)(2,1)S(1)}, bf16[256,640]{1,0:T(8,128)(2,1)}, u32[]{:S(2)}, u32[]{:S(2)}) collective-permute-start(bf16[256,640]{1,0:T(8,128)(2,1)S(1)} %collective-permute-done.23.refs_6_), channel_id=1, source_target_pairs={{0,1},{1,0},{2,3},{3,2},{4,5},{5,4},{6,7},{7,6},{8,9},{9,8},{10,11... | collective-permute-start | bytes 983048 | tf_op jit(solution)/shard_map/ppermute | solution.py:725
  213.5 399.5 %reduce-scatter.3.cloned.1.call-start = ((), (), s32[]{:S(2)}) async-start(), calls=%async_computation.2 | async-start | bytes 6881280 | tf_op jit(solution)/shard_map/reduce_scatter | solution.py:994
  215.6 22.7 %collective-permute-start.33 = (bf16[2,4,2,40,2048]{4,3,2,1,0:T(8,128)(2,1)}, bf16[2,4,2,40,2048]{4,3,2,1,0:T(8,128)(2,1)}, u32[]{:S(2)}, u32[]{:S(2)}) collective-permute-start(bf16[2,4,2,40,2048]{4,3,2,1,0:T(8,128)(2,1)} %maximum_select_fusion.1), channel_id=1, source_target_pairs={{0,8},{8,0},{1,9},{9,1},{2,10},{10,2},{3,11},{11,3},{4,12},{12,4},... | collective-permute-start | bytes 7864328 | tf_op jit(solution)/shard_map/ppermute | solution.py:725
  217.5 27.4 %collective-permute-start.34 = (bf16[256,2048]{1,0:T(8,128)(2,1)}, bf16[256,2048]{1,0:T(8,128)(2,1)}, u32[]{:S(2)}, u32[]{:S(2)}) collective-permute-start(bf16[256,2048]{1,0:T(8,128)(2,1)} %collective-permute-done.27.refs_6_), channel_id=1, source_target_pairs={{0,16},{16,0},{1,17},{17,1},{2,18},{18,2},{3,19},{19,3},{4,20},{20... | collective-permute-start | bytes 3145736 | tf_op jit(solution)/shard_map/ppermute | solution.py:725
  244.9 25.4 %collective-permute-start.35 = (bf16[256,2048]{1,0:T(8,128)(2,1)S(1)}, bf16[256,2048]{1,0:T(8,128)(2,1)S(1)}, u32[]{:S(2)}, u32[]{:S(2)}) collective-permute-start(bf16[256,2048]{1,0:T(8,128)(2,1)S(1)} %multiply_convert_fusion.refs_0_), channel_id=1, source_target_pairs={{0,16},{16,0},{1,17},{17,1},{2,18},{18,2},{3,19},{19,3},{4,20},{20... | collective-permute-start | bytes 3145736 | tf_op jit(solution)/shard_map/ppermute | solution.py:725
  246.3 25.0 %collective-permute-start.36 = (bf16[256,2048]{1,0:T(8,128)(2,1)S(1)}, bf16[256,2048]{1,0:T(8,128)(2,1)S(1)}, u32[]{:S(2)}, u32[]{:S(2)}) collective-permute-start(bf16[256,2048]{1,0:T(8,128)(2,1)S(1)} %multiply_convert_fusion.refs_0_), channel_id=1, source_target_pairs={{0,1},{1,0},{2,3},{3,2},{4,5},{5,4},{6,7},{7,6},{8,9},{9,8},{10,11... | collective-permute-start | bytes 3145736 | tf_op jit(solution)/shard_map/ppermute | solution.py:725
  363.5 356.3 %reduce-scatter.5.cloned.1.call-start = ((), (), s32[]{:S(2)}) async-start(), calls=%async_computation.3 | async-start | bytes 5898240 | tf_op jit(solution)/shard_map/reduce_scatter | solution.py:994
  408.2 37.9 %collective-permute-start.44 = (bf16[4,3,256,768]{3,2,1,0:T(8,128)(2,1)}, bf16[4,3,256,768]{3,2,1,0:T(8,128)(2,1)}, u32[]{:S(2)}, u32[]{:S(2)}) collective-permute-start(bf16[4,3,256,768]{3,2,1,0:T(8,128)(2,1)} %get-tuple-element.228), channel_id=1, source_target_pairs={{0,8},{8,0},{1,9},{9,1},{2,10},{10,2},{3,11},{11,3},{4,12},{12,4},... | collective-permute-start | bytes 14155784 | tf_op jit(solution)/shard_map/ppermute | solution.py:725
  428.8 24.6 %collective-permute-start.43 = (bf16[256,2048]{1,0:T(8,128)(2,1)}, bf16[256,2048]{1,0:T(8,128)(2,1)}, u32[]{:S(2)}, u32[]{:S(2)}) collective-permute-start(bf16[256,2048]{1,0:T(8,128)(2,1)} %pad_maximum_fusion.5), channel_id=1, source_target_pairs={{0,1},{1,0},{2,3},{3,2},{4,5},{5,4},{6,7},{7,6},{8,9},{9,8},{10,11... | collective-permute-start | bytes 3145736 | tf_op jit(solution)/shard_map/ppermute | solution.py:725
  431.9 24.2 %collective-permute-start.42 = (bf16[256,2048]{1,0:T(8,128)(2,1)}, bf16[256,2048]{1,0:T(8,128)(2,1)}, u32[]{:S(2)}, u32[]{:S(2)}) collective-permute-start(bf16[256,2048]{1,0:T(8,128)(2,1)} %pad_maximum_fusion.4), channel_id=1, source_target_pairs={{0,16},{16,0},{1,17},{17,1},{2,18},{18,2},{3,19},{19,3},{4,20},{20... | collective-permute-start | bytes 3145736 | tf_op jit(solution)/shard_map/ppermute | solution.py:725
  458.3 31.7 %collective-permute-start.45 = (bf16[256,1024]{1,0:T(8,128)(2,1)}, bf16[256,1024]{1,0:T(8,128)(2,1)}, u32[]{:S(2)}, u32[]{:S(2)}) collective-permute-start(bf16[256,1024]{1,0:T(8,128)(2,1)} %get-tuple-element.364), channel_id=1, source_target_pairs={{0,16},{16,0},{1,17},{17,1},{2,18},{18,2},{3,19},{19,3},{4,20},{20... | collective-permute-start | bytes 1572872 | tf_op jit(solution)/shard_map/ppermute | solution.py:725
  458.9 32.5 %collective-permute-start.46 = (bf16[256,1024]{1,0:T(8,128)(2,1)}, bf16[256,1024]{1,0:T(8,128)(2,1)}, u32[]{:S(2)}, u32[]{:S(2)}) collective-permute-start(bf16[256,1024]{1,0:T(8,128)(2,1)} %get-tuple-element.363), channel_id=1, source_target_pairs={{0,1},{1,0},{2,3},{3,2},{4,5},{5,4},{6,7},{7,6},{8,9},{9,8},{10,11... | collective-permute-start | bytes 1572872 | tf_op jit(solution)/shard_map/ppermute | solution.py:725
  499.0 29.6 %collective-permute-start.49 = (bf16[2,4,2,40,2048]{4,3,1,2,0:T(8,128)(2,1)}, bf16[2,4,2,40,2048]{4,3,1,2,0:T(8,128)(2,1)}, u32[]{:S(2)}, u32[]{:S(2)}) collective-permute-start(bf16[2,4,2,40,2048]{4,3,1,2,0:T(8,128)(2,1)} %bitcast.206), channel_id=1, source_target_pairs={{0,8},{8,0},{1,9},{9,1},{2,10},{10,2},{3,11},{11,3},{4,12},{12,4},... | collective-permute-start | bytes 7864328 | tf_op jit(solution)/shard_map/ppermute | solution.py:725
  504.6 29.2 %collective-permute-start.48 = (bf16[256,2048]{1,0:T(8,128)(2,1)}, bf16[256,2048]{1,0:T(8,128)(2,1)}, u32[]{:S(2)}, u32[]{:S(2)}) collective-permute-start(bf16[256,2048]{1,0:T(8,128)(2,1)} %pad_maximum_fusion.7), channel_id=1, source_target_pairs={{0,1},{1,0},{2,3},{3,2},{4,5},{5,4},{6,7},{7,6},{8,9},{9,8},{10,11... | collective-permute-start | bytes 3145736 | tf_op jit(solution)/shard_map/ppermute | solution.py:725
  507.6 27.2 %collective-permute-start.47 = (bf16[256,2048]{1,0:T(8,128)(2,1)}, bf16[256,2048]{1,0:T(8,128)(2,1)}, u32[]{:S(2)}, u32[]{:S(2)}) collective-permute-start(bf16[256,2048]{1,0:T(8,128)(2,1)} %pad_maximum_fusion.6), channel_id=1, source_target_pairs={{0,16},{16,0},{1,17},{17,1},{2,18},{18,2},{3,19},{19,3},{4,20},{20... | collective-permute-start | bytes 3145736 | tf_op jit(solution)/shard_map/ppermute | solution.py:725
  538.4 31.2 %collective-permute-start.63 = (bf16[4,2,40,2048]{3,2,0,1:T(8,128)(2,1)S(1)}, bf16[4,2,40,2048]{3,2,0,1:T(8,128)(2,1)S(1)}, u32[]{:S(2)}, u32[]{:S(2)}) collective-permute-start(bf16[4,2,40,2048]{3,2,0,1:T(8,128)(2,1)S(1)} %dynamic-slice_bitcast_fusion), channel_id=1, source_target_pairs={{0,16},{16,0},{1,17},{17,1},{2,18},{18,2},{3,19},{19,3},{4,20},{20... | collective-permute-start | bytes 3932168 | tf_op jit(solution)/shard_map/ppermute | solution.py:725
  541.5 29.7 %collective-permute-start.61 = (bf16[2,4,2,64,640]{4,3,1,2,0:T(8,128)(2,1)S(1)}, bf16[2,4,2,64,640]{4,3,1,2,0:T(8,128)(2,1)S(1)}, u32[]{:S(2)}, u32[]{:S(2)}) collective-permute-start(bf16[2,4,2,64,640]{4,3,1,2,0:T(8,128)(2,1)S(1)} %bitcast.231), channel_id=1, source_target_pairs={{0,8},{8,0},{1,9},{9,1},{2,10},{10,2},{3,11},{11,3},{4,12},{12,4},... | collective-permute-start | bytes 3932168 | tf_op jit(solution)/shard_map/ppermute | solution.py:725
  544.4 46.3 %collective-permute-start.54 = (bf16[128,640]{1,0:T(8,128)(2,1)S(1)}, bf16[128,640]{1,0:T(8,128)(2,1)S(1)}, u32[]{:S(2)}, u32[]{:S(2)}) collective-permute-start(bf16[128,640]{1,0:T(8,128)(2,1)S(1)} %copy-done.38), channel_id=1, source_target_pairs={{2,0},{4,2},{6,4},{3,1},{5,3},{7,5},{10,8},{12,10},{14,12},{11,9},... | collective-permute-start | bytes 491528 | tf_op jit(solution)/shard_map/ppermute | solution.py:772
  545.7 66.6 %collective-permute-start.55 = (bf16[128,640]{1,0:T(8,128)(2,1)S(1)}, bf16[128,640]{1,0:T(8,128)(2,1)S(1)}, u32[]{:S(2)}, u32[]{:S(2)}) collective-permute-start(bf16[128,640]{1,0:T(8,128)(2,1)S(1)} %copy-done.37), channel_id=1, source_target_pairs={{4,0},{6,2},{5,1},{7,3},{12,8},{14,10},{13,9},{15,11},{20,16},{22,... | collective-permute-start | bytes 491528 | tf_op jit(solution)/shard_map/ppermute | solution.py:772
  547.0 65.9 %collective-permute-start.56 = (bf16[128,640]{1,0:T(8,128)(2,1)S(1)}, bf16[128,640]{1,0:T(8,128)(2,1)}, u32[]{:S(2)}, u32[]{:S(2)}) collective-permute-start(bf16[128,640]{1,0:T(8,128)(2,1)S(1)} %copy-done.36), channel_id=1, source_target_pairs={{6,0},{7,1},{14,8},{15,9},{22,16},{23,17},{30,24},{31,25}} | collective-permute-start | bytes 491528 | tf_op jit(solution)/shard_map/ppermute | solution.py:772
  614.2 31.2 %collective-permute-start.69 = (bf16[4,40,2048]{2,1,0:T(8,128)(2,1)S(1)}, bf16[4,40,2048]{2,1,0:T(8,128)(2,1)S(1)}, u32[]{:S(2)}, u32[]{:S(2)}) collective-permute-start(bf16[4,40,2048]{2,1,0:T(8,128)(2,1)S(1)} %dynamic-slice_bitcast_fusion.2), channel_id=1, source_target_pairs={{0,1},{1,0},{2,3},{3,2},{4,5},{5,4},{6,7},{7,6},{8,9},{9,8},{10,11... | collective-permute-start | bytes 1966088 | tf_op jit(solution)/shard_map/ppermute | solution.py:725
  616.1 27.9 %collective-permute-start.68 = (bf16[2,4,64,640]{3,2,1,0:T(8,128)(2,1)S(1)}, bf16[2,4,64,640]{3,2,1,0:T(8,128)(2,1)S(1)}, u32[]{:S(2)}, u32[]{:S(2)}) collective-permute-start(bf16[2,4,64,640]{3,2,1,0:T(8,128)(2,1)S(1)} %dynamic-slice_bitcast_fusion.3), channel_id=1, source_target_pairs={{0,1},{1,0},{2,3},{3,2},{4,5},{5,4},{6,7},{7,6},{8,9},{9,8},{10,11... | collective-permute-start | bytes 1966088 | tf_op jit(solution)/shard_map/ppermute | solution.py:725
  621.0 27.5 %collective-permute-start.67 = (bf16[4,2,64,640]{3,2,0,1:T(8,128)(2,1)S(1)}, bf16[4,2,64,640]{3,2,0,1:T(8,128)(2,1)S(1)}, u32[]{:S(2)}, u32[]{:S(2)}) collective-permute-start(bf16[4,2,64,640]{3,2,0,1:T(8,128)(2,1)S(1)} %dynamic-slice_bitcast_fusion.4), channel_id=1, source_target_pairs={{0,16},{16,0},{1,17},{17,1},{2,18},{18,2},{3,19},{19,3},{4,20},{20... | collective-permute-start | bytes 1966088 | tf_op jit(solution)/shard_map/ppermute | solution.py:725
  621.6 27.8 %collective-permute-start.64 = (bf16[128,640]{1,0:T(8,128)(2,1)S(1)}, bf16[128,640]{1,0:T(8,128)(2,1)S(1)}, u32[]{:S(2)}, u32[]{:S(2)}) collective-permute-start(bf16[128,640]{1,0:T(8,128)(2,1)S(1)} %copy-done.41), channel_id=1, source_target_pairs={{2,0},{4,2},{6,4},{3,1},{5,3},{7,5},{10,8},{12,10},{14,12},{11,9},... | collective-permute-start | bytes 491528 | tf_op jit(solution)/shard_map/ppermute | solution.py:772
  622.9 26.5 %collective-permute-start.65 = (bf16[128,640]{1,0:T(8,128)(2,1)S(1)}, bf16[128,640]{1,0:T(8,128)(2,1)S(1)}, u32[]{:S(2)}, u32[]{:S(2)}) collective-permute-start(bf16[128,640]{1,0:T(8,128)(2,1)S(1)} %copy-done.40), channel_id=1, source_target_pairs={{4,0},{6,2},{5,1},{7,3},{12,8},{14,10},{13,9},{15,11},{20,16},{22,... | collective-permute-start | bytes 491528 | tf_op jit(solution)/shard_map/ppermute | solution.py:772
  645.4 56.0 %collective-permute-start.84 = (bf16[3,256,896]{2,1,0:T(8,128)(2,1)}, bf16[3,256,896]{2,1,0:T(8,128)(2,1)}, u32[]{:S(2)}, u32[]{:S(2)}) collective-permute-start(bf16[3,256,896]{2,1,0:T(8,128)(2,1)} %bitcast.61), channel_id=1, source_target_pairs={{1,8},{8,1},{3,10},{10,3},{5,12},{12,5},{7,14},{14,7},{17,24},{24,... | collective-permute-start | bytes 4128776 | tf_op jit(solution)/shard_map/ppermute | solution.py:765
  661.3 26.3 %collective-permute-start.70 = (bf16[2,4,2,64,640]{4,3,1,0,2:T(8,128)(2,1)}, bf16[2,4,2,64,640]{4,3,1,0,2:T(8,128)(2,1)}, u32[]{:S(2)}, u32[]{:S(2)}) collective-permute-start(bf16[2,4,2,64,640]{4,3,1,0,2:T(8,128)(2,1)} %bitcast.207), channel_id=1, source_target_pairs={{0,8},{8,0},{1,9},{9,1},{2,10},{10,2},{3,11},{11,3},{4,12},{12,4},... | collective-permute-start | bytes 3932168 | tf_op jit(solution)/shard_map/ppermute | solution.py:725
  710.5 21.1 %collective-permute-start.76 = (bf16[64,1280]{1,0:T(8,128)(2,1)}, bf16[64,1280]{1,0:T(8,128)(2,1)S(1)}, u32[]{:S(2)}, u32[]{:S(2)}) collective-permute-start(bf16[64,1280]{1,0:T(8,128)(2,1)} %get-tuple-element.367), channel_id=1, source_target_pairs={{0,2},{2,4},{4,6},{6,0},{1,3},{3,5},{5,7},{7,1},{8,10},{10,12},{12... | collective-permute-start | bytes 491528 | tf_op jit(solution)/shard_map/ppermute | solution.py:730
  712.1 22.5 %collective-permute-start.77 = (bf16[64,1280]{1,0:T(8,128)(2,1)}, bf16[64,1280]{1,0:T(8,128)(2,1)}, u32[]{:S(2)}, u32[]{:S(2)}) collective-permute-start(bf16[64,1280]{1,0:T(8,128)(2,1)} %get-tuple-element.368), channel_id=1, source_target_pairs={{0,4},{2,6},{4,0},{6,2},{1,5},{3,7},{5,1},{7,3},{8,12},{10,14},{12... | collective-permute-start | bytes 491528 | tf_op jit(solution)/shard_map/ppermute | solution.py:730
  713.9 21.6 %collective-permute-start.78 = (bf16[64,1280]{1,0:T(8,128)(2,1)}, bf16[64,1280]{1,0:T(8,128)(2,1)}, u32[]{:S(2)}, u32[]{:S(2)}) collective-permute-start(bf16[64,1280]{1,0:T(8,128)(2,1)} %get-tuple-element.369), channel_id=1, source_target_pairs={{0,6},{2,0},{4,2},{6,4},{1,7},{3,1},{5,3},{7,5},{8,14},{10,8},{12,... | collective-permute-start | bytes 491528 | tf_op jit(solution)/shard_map/ppermute | solution.py:730
  (113 other events, 1147.8 us)
Sparse Core Ops, SparseCore 0:
  107.3 117.7 all-gather.4
  227.4 108.2 all-gather.6
  363.6 129.1 reduce-scatter.2
  495.0 123.5 reduce-scatter.4

commit v4 on v3

--- a/solution.py
+++ b/solution.py
@@ -911,8 +911,8 @@
 
     qkv_width = qkv_own.shape[2]
     cut = 512
-    out_own = turn(jnp.stack(direct_gather(w_out)), (planes - z_at) % planes)
-    qkv_x, qkv_y, out_own = together(x_swap(qkv_own), y_swap(qkv_own), out_own)
+    out_own = turn(jnp.stack(direct_gather(hold(w_out, qkv_own))), (planes - z_at) % planes)
+    qkv_x, qkv_y = together(x_swap(qkv_own), y_swap(qkv_own))
     down_turned = w_down.T
     ffn_width = w_gate.shape[1]
     ffn_cut = (ffn_width // 256 + 1) * 128
@@ -920,9 +920,10 @@
         jnp.stack([w[:, first:last] for w in (w_gate, w_up, down_turned)])
         for first, last in ((0, ffn_cut), (ffn_cut, ffn_width))
     ]
-    qkv_a, qkv_b, first_stack = together(
+    qkv_a, qkv_b, out_own, first_stack = together(
         y_swap(qkv_x[..., :cut]),
         x_swap(qkv_y[..., cut:]),
+        out_own,
         corner(hold(stacks[0], qkv_x)),
     )
     qkv_pieces = [qkv_own, qkv_x, qkv_y, qkv_a, qkv_b]
@@ -952,16 +953,10 @@
     )
     out_block = in_order(out_own, out_y, y_at, 1)
     kv_own = [kv_here] + list(kv_far)
-    *kv_other, out_x, second_stack = together(
-        *[y_swap(piece) for piece in kv_far],
-        x_swap(out_block),
-        corner(hold(stacks[1], kv_far[-1])),
-    )
-    parts = [gathered_first, lax.all_gather(second_stack, ("core", "z"), axis=0)]
+    *kv_other, out_x = together(*[y_swap(piece) for piece in kv_far], x_swap(out_block))
     cot_xy = x_swap(hold(cot_y, out_x))
     kv_other = [near] + list(kv_other)
     out_block = in_order(out_block, out_x, x_at, 0)
-    cot_blocks = [cotangent_here, cot_x, cot_y, cot_xy]
     kv_pieces, bases = [], [seq_place * seg_tok]
     for t in range(planes):
         for dy, piece in enumerate((kv_own[t], kv_other[t])):
@@ -971,12 +966,16 @@
     attended_b, logs = attend_call(
         heads_kv, grouping, bases, query_b, seg_here, seg_all, kv_pieces
     )
-    attended_b, out_core = together(attended_b, core_swap(out_block))
+    attended_b, out_core, second_stack, cot_xy = together(
+        attended_b, core_swap(out_block), corner(hold(stacks[1], kv_other[-1])), cot_xy
+    )
+    cot_blocks = [cotangent_here, cot_x, cot_y, cot_xy]
+    parts = [gathered_first, lax.all_gather(second_stack, ("core", "z"), axis=0)]
     out_full = in_order(out_block, out_core, core_at, 1).reshape(-1, feature_count)
     residual = inputs_here.astype(jnp.float32)
     middle = residual + jnp.dot(attended_b, out_full, preferred_element_type=jnp.float32)
     ffn_in = rms_apply(middle, ffn_gain).astype(low)
-    ffn_blocks = gather_tokens(hold(ffn_in, cot_xy))
+    ffn_blocks = gather_tokens(ffn_in)
 
     before, where = None, place
     hidden_parts, home, sums = [], [], []

time: 764 us -> 753 us (0.986)
  waiting for transfers between devices: 289 us -> 278 us
    ppermute x63, waiting for transfers between devices: 199 us -> 189 us  [swap(): return lax.ppermute(values, axis_name, [(i, i ^ bit) for i in range(count)])]
  transfers between devices with their start and end apart: 95 -> 95, of which waited for: 39 -> 44; matrix products, arithmetic and copies ran while one was open for 18% -> 17% of each run, Pallas kernels for 26% -> 27%
where the time goes in v4:
time: 753 us; the launch traced here: 743 us
  waiting for transfers between devices  278 us (37%)
  Pallas kernels  199 us (26%)
  starting transfers between devices  116 us (15%)
  other arithmetic  82.1 us (11%)
  local copies, waits for them, and re-layouts  41.1 us (5%)
  between operations  15.4 us (2%)
  matrix products  11.2 us (1%)
    ppermute x63, waiting for transfers between devices, swap(): return lax.ppermute(values, axis_name, [(i, i ^ bit) for i in range(count)])  189 us
    pallas_call x2, Pallas kernels, ffn_call(): pl.pallas_call(functools.partial(ffn_kernel, planes, blocks, chained), ou...  66.5 us
    ppermute x9, waiting for transfers between devices, chain(): return lax.ppermute(values, 'z', moves)  65.5 us
    ppermute x63, starting transfers between devices, swap(): return lax.ppermute(values, axis_name, [(i, i ^ bit) for i in range(count)])  53.9 us
    pallas_call x2, Pallas kernels, weight_grad_call(): pl.pallas_call(functools.partial(weight_grad_kernel, blocks), out_shape=[...  39.9 us
    convert_element_type x26, other arithmetic, add_low(): (left.astype(jnp.float32) + right.astype(jnp.float32)).astype(jnp.bfloat16)  36.8 us
    pallas_call x2, Pallas kernels, attend_back_call(): pl.pallas_call(functools.partial(attend_back_kernel, row, pieces, heads_k...  33.5 us
    ppermute x9, starting transfers between devices, chain(): return lax.ppermute(values, 'z', moves)  30.9 us
  transfers between devices with their start and end apart: 95, of which 44 were waited for; matrix products, arithmetic and copies ran while one was open for 17% of the time, Pallas kernels for 27%

profile of v4, /device:TPU:0, one launch (start us, length us, event | category | flops | bytes accessed | tf_op | source)
XLA Modules:
  0.0 742.6 jit_solution(4650002610743634036)
XLA Ops:
  11.9 4.7 collective-permute-start
  21.8 12.3 %collective-permute-done.4 = f32[96,128]{1,0:T(8,128)S(1)} collective-permute-done((f32[96,128]{1,0:T(8,128)S(1)}, f32[96,128]{1,0:T(8,128)S(1)}, u32[]{:S(2)}, u32[]{:S(2)}) %collective-permute-start.4) | collective-permute-done | bytes 49184 | tf_op jit(solution)/shard_map/ppermute | solution.py:725
  35.9 3.4 collective-permute-done.5
  50.6 5.1 collective-permute-start.12
  56.4 3.2 collective-permute-done.12
  59.6 6.9 collective-permute-done.13
  78.1 17.3 %collective-permute-done.10.refs_3_ = bf16[4,64,512]{2,1,0:T(8,128)(2,1)} collective-permute-done((bf16[4,64,512]{2,1,0:T(8,128)(2,1)}, bf16[4,64,512]{2,1,0:T(8,128)(2,1)}, u32[]{:S(2)}, u32[]{:S(2)}) %collective-permute-start.10) | collective-permute-done | bytes 262176 | tf_op jit(solution)/shard_map/ppermute | solution.py:725
  102.6 13.3 %shard_map.246 = (bf16[256,2048]{1,0:T(8,128)(2,1)}, f32[256,1280]{1,0:T(8,128)}, f32[256,640]{1,0:T(8,128)}, bf16[256,1280]{1,0:T(8,128)(2,1)}, bf16[256,640]{1,0:T(8,128)(2,1)}) custom-call(s32[4]{0:T(128)} %pad_add_fusion.place_ref, bf16[256,2048]{1,0:T(8,128)(2,1)} %bitcast.223, f32[1,2048]{1,0:T(1,128)} %bitcast.246, ...), custom_call_target="tpu_custom_call" | custom-call | flops 2013265920 | bytes 13107200 | tf_op jit(solution)/shard_map/pallas_call | solution.py:366
  117.2 5.4 collective-permute-start.21
  122.6 4.8 collective-permute-start.22
  128.3 8.9 %collective-permute-done.21.refs_2_ = bf16[256,640]{1,0:T(8,128)(2,1)} collective-permute-done((bf16[256,640]{1,0:T(8,128)(2,1)}, bf16[256,640]{1,0:T(8,128)(2,1)}, u32[]{:S(2)}, u32[]{:S(2)}) %collective-permute-start.21) | collective-permute-done | bytes 327712 | tf_op jit(solution)/shard_map/ppermute | solution.py:772
  137.2 13.0 %collective-permute-start.23 = (bf16[256,640]{1,0:T(8,128)(2,1)}, bf16[256,640]{1,0:T(8,128)(2,1)}, u32[]{:S(2)}, u32[]{:S(2)}) collective-permute-start(bf16[256,640]{1,0:T(8,128)(2,1)} %get-tuple-element.170.refs_0_), channel_id=1, source_target_pairs={{0,6},{1,7},{8,14},{9,15},{16,22},{17,23},{24,30},{25,31}} | collective-permute-start | bytes 983048 | tf_op jit(solution)/shard_map/ppermute | solution.py:772
  152.3 12.6 %collective-permute-done.23.refs_6_ = bf16[256,640]{1,0:T(8,128)(2,1)} collective-permute-done((bf16[256,640]{1,0:T(8,128)(2,1)}, bf16[256,640]{1,0:T(8,128)(2,1)}, u32[]{:S(2)}, u32[]{:S(2)}) %collective-permute-start.23) | collective-permute-done | bytes 327712 | tf_op jit(solution)/shard_map/ppermute | solution.py:772
  170.4 7.5 %collective-permute-done.28.refs_3_ = bf16[256,640]{1,0:T(8,128)(2,1)S(1)} collective-permute-done((bf16[256,640]{1,0:T(8,128)(2,1)}, bf16[256,640]{1,0:T(8,128)(2,1)S(1)}, u32[]{:S(2)}, u32[]{:S(2)}) %collective-permute-start.28) | collective-permute-done | bytes 327712 | tf_op jit(solution)/shard_map/ppermute | solution.py:725
  177.9 7.0 collective-permute-done.29.refs_5_
  185.0 4.6 collective-permute-done.30.refs_7_
  189.6 6.4 collective-permute-done.31
  205.5 18.2 %shard_map.247 = (bf16[256,1280]{1,0:T(8,128)(2,1)}, f32[2,5,1,512]{3,2,1,0:T(1,128)}) custom-call(s32[9]{0:T(128)} %stack.169.base_ref, bf16[256,1280]{1,0:T(8,128)(2,1)} %get-tuple-element.169.q_ref, f32[2,128]{1,0:T(2,128)} %convert_element_type.442.segq_ref, f32[16,128]{1,0:T(8,128)} %fusion.27.segk_ref, bf16[256,640]{1,0:T(8,128)(2,1)} %get-tuple-element.170.refs_0_, ...), custom_call_target="tpu_custom_call" | custom-call | flops 5368709120 | bytes 3932160 | tf_op jit(solution)/shard_map/pallas_call | solution.py:128
  229.5 4.0 maximum_select_fusion
  237.4 23.9 %collective-permute-done.35.refs_1_ = bf16[256,2048]{1,0:T(8,128)(2,1)S(1)} collective-permute-done((bf16[256,2048]{1,0:T(8,128)(2,1)S(1)}, bf16[256,2048]{1,0:T(8,128)(2,1)S(1)}, u32[]{:S(2)}, u32[]{:S(2)}) %collective-permute-start.35) | collective-permute-done | bytes 1048608 | tf_op jit(solution)/shard_map/ppermute | solution.py:725
  263.3 11.3 %collective-permute-done.37 = bf16[256,1024]{1,0:T(8,128)(2,1)S(1)} collective-permute-done((bf16[256,1024]{1,0:T(8,128)(2,1)S(1)}, bf16[256,1024]{1,0:T(8,128)(2,1)S(1)}, u32[]{:S(2)}, u32[]{:S(2)}) %collective-permute-start.37) | collective-permute-done | bytes 524320 | tf_op jit(solution)/shard_map/ppermute | solution.py:725
  276.4 40.3 %shard_map.248 = (bf16[256,896]{1,0:T(8,128)(2,1)}, bf16[256,896]{1,0:T(8,128)(2,1)}, bf16[256,896]{1,0:T(8,128)(2,1)}, bf16[256,2048]{1,0:T(8,128)(2,1)}, bf16[...) custom-call(s32[4]{0:T(128)} %pad_add_fusion.place_ref, ...), custom_call_target="tpu_custom_call" | custom-call | flops 18790481920 | bytes 27787264 | tf_op jit(solution)/shard_map/pallas_call | solution.py:562
  316.6 21.8 %shard_map.249 = (bf16[4,3,256,896]{3,2,1,0:T(8,128)(2,1)}, bf16[4,3,256,896]{3,2,1,0:T(8,128)(2,1)}) custom-call(s32[4]{0:T(128)} %pad_add_fusion.place_ref, bf16[256,2048]{1,0:T(8,128)(2,1)} %copy-done.23, bf16[256,2048]{1,0:T(8,128)(2,1)} %copy-done.32, bf16[256,2048]{1,0:T(8,128)(2,1)} %copy-done.33, ...), custom_call_target="tpu_custom_call" | custom-call | flops 11274289152 | bytes 16515072 | tf_op jit(solution)/shard_map/pallas_call | solution.py:612
  338.5 9.2 %collective-permute-done.39 = bf16[4,3,256,896]{3,2,1,0:T(8,128)(2,1)S(1)} collective-permute-done((bf16[4,3,256,896]{3,2,1,0:T(8,128)(2,1)}, bf16[4,3,256,896]{3,2,1,0:T(8,128)(2,1)S(1)}, u32[]{:S(2)}, u32[]{:S(2)}) %collective-permute-start.39) | collective-permute-done | bytes 5505056 | tf_op jit(solution)/shard_map/ppermute | solution.py:725
  347.8 6.7 add_convert_fusion
  354.9 26.2 %shard_map.250 = (bf16[256,768]{1,0:T(8,128)(2,1)}, bf16[256,768]{1,0:T(8,128)(2,1)}, bf16[256,768]{1,0:T(8,128)(2,1)}, bf16[256,2048]{1,0:T(8,128)(2,1)}, bf16[...) custom-call(s32[4]{0:T(128)} %pad_add_fusion.place_ref, ...), custom_call_target="tpu_custom_call" | custom-call | flops 16106127360 | bytes 26214400 | tf_op jit(solution)/shard_map/pallas_call | solution.py:562
  381.1 18.0 %shard_map.251 = (bf16[4,3,256,768]{3,2,1,0:T(8,128)(2,1)}, bf16[4,3,256,768]{3,2,1,0:T(8,128)(2,1)}) custom-call(s32[4]{0:T(128)} %pad_add_fusion.place_ref, bf16[256,2048]{1,0:T(8,128)(2,1)} %copy-done.23, bf16[256,2048]{1,0:T(8,128)(2,1)} %copy-done.32, bf16[256,2048]{1,0:T(8,128)(2,1)} %copy-done.33, ...), custom_call_target="tpu_custom_call" | custom-call | flops 9663676416 | bytes 14155776 | tf_op jit(solution)/shard_map/pallas_call | solution.py:612
  405.0 11.2 %collective-permute-done.40 = bf16[256,1024]{1,0:T(8,128)(2,1)} collective-permute-done((bf16[256,1024]{1,0:T(8,128)(2,1)}, bf16[256,1024]{1,0:T(8,128)(2,1)}, u32[]{:S(2)}, u32[]{:S(2)}) %collective-permute-start.40) | collective-permute-done | bytes 524320 | tf_op jit(solution)/shard_map/ppermute | solution.py:725
  423.4 13.7 %shard_map.252 = (bf16[256,2048]{1,0:T(8,128)(2,1)}, bf16[256,2048]{1,0:T(8,128)(2,1)}, bf16[256,2048]{1,0:T(8,128)(2,1)}, bf16[256,2048]{1,0:T(8,128)(2,1)}) custom-call(s32[4]{0:T(128)} %pad_add_fusion.place_ref, bf16[256,896]{1,0:T(8,128)(2,1)} %get-tuple-element.200.refs_16_.refs_0_, bf16[256,896]{1,0:T(8,128)(2,1)} %get-tuple-element.201.refs_17_.refs_1_, ...), custom_call_target="tpu_custom_call" | custom-call | flops 6979321856 | bytes 23592960 | tf_op jit(solution)/shard_map/pallas_call | solution.py:667
  437.1 7.2 add_convert_fusion.1
  458.8 16.9 %shard_map.253 = (bf16[128,1280]{1,0:T(8,128)(2,1)}, f32[5,1,256]{2,1,0:T(1,128)}, bf16[128,640]{1,0:T(8,128)(2,1)}, bf16[128,640]{1,0:T(8,128)(2,1)}, bf16[128,...) custom-call(s32[9]{0:T(128)} %stack.169.base_ref, ...), custom_call_target="tpu_custom_call" | custom-call | flops 6710886400 | bytes 3932160 | tf_op jit(solution)/shard_map/pallas_call | solution.py:265
  482.0 3.5 convolution_convert_fusion.1
  499.4 16.6 %shard_map.254 = (bf16[128,1280]{1,0:T(8,128)(2,1)}, f32[5,1,256]{2,1,0:T(1,128)}, bf16[128,640]{1,0:T(8,128)(2,1)}, bf16[128,640]{1,0:T(8,128)(2,1)}, bf16[128,...) custom-call(s32[9]{0:T(128)} %stack.169.base_ref, ...), custom_call_target="tpu_custom_call" | custom-call | flops 6710886400 | bytes 3932160 | tf_op jit(solution)/shard_map/pallas_call | solution.py:265
  520.1 3.8 fusion
  540.4 19.5 %collective-permute-done.63 = bf16[4,2,40,2048]{3,2,0,1:T(8,128)(2,1)S(1)} collective-permute-done((bf16[4,2,40,2048]{3,2,0,1:T(8,128)(2,1)S(1)}, bf16[4,2,40,2048]{3,2,0,1:T(8,128)(2,1)S(1)}, u32[]{:S(2)}, u32[]{:S(2)}) %collective-permute-start.63) | collective-permute-done | bytes 1310752 | tf_op jit(solution)/shard_map/ppermute | solution.py:725
  562.9 17.9 %collective-permute-done.54 = bf16[128,640]{1,0:T(8,128)(2,1)S(1)} collective-permute-done((bf16[128,640]{1,0:T(8,128)(2,1)S(1)}, bf16[128,640]{1,0:T(8,128)(2,1)S(1)}, u32[]{:S(2)}, u32[]{:S(2)}) %collective-permute-start.54) | collective-permute-done | bytes 163872 | tf_op jit(solution)/shard_map/ppermute | solution.py:772
  580.9 21.6 %collective-permute-done.55 = bf16[128,640]{1,0:T(8,128)(2,1)S(1)} collective-permute-done((bf16[128,640]{1,0:T(8,128)(2,1)S(1)}, bf16[128,640]{1,0:T(8,128)(2,1)S(1)}, u32[]{:S(2)}, u32[]{:S(2)}) %collective-permute-start.55) | collective-permute-done | bytes 163872 | tf_op jit(solution)/shard_map/ppermute | solution.py:772
  607.8 3.3 add_convert_fusion.2
  615.4 18.8 %collective-permute-done.68 = bf16[2,4,64,640]{3,2,1,0:T(8,128)(2,1)S(1)} collective-permute-done((bf16[2,4,64,640]{3,2,1,0:T(8,128)(2,1)S(1)}, bf16[2,4,64,640]{3,2,1,0:T(8,128)(2,1)S(1)}, u32[]{:S(2)}, u32[]{:S(2)}) %collective-permute-start.68) | collective-permute-done | bytes 655392 | tf_op jit(solution)/shard_map/ppermute | solution.py:725
  639.6 3.5 collective-permute-done.66
  644.1 3.9 shard_map.255
  658.2 4.5 collective-permute-done.73
  663.8 5.0 collective-permute-done.74
  672.0 5.8 collective-permute-done.71
  679.5 10.2 %shard_map.256 = (f32[256,2048]{1,0:T(8,128)}, f32[1,2048]{1,0:T(1,128)}) custom-call(s32[4]{0:T(128)} %pad_add_fusion.place_ref, bf16[256,1920]{1,0:T(8,128)(2,1)} %pad_maximum_fusion.9.g_ref, bf16[256,2048]{1,0:T(8,128)(2,1)} %bitcast.224, f32[1,2048]{1,0:T(1,128)} %bitcast.247, f32[256,2048]{1,0:T(8,128)} %copy-done, bf16[4,64,1920]{2,1,0:T(8,128)(2,1)} %copy-done.1, ...), custom_call_target="tpu_custom_call" | custom-call | flops 2013265920 | bytes 13107200 | tf_op jit(solution)/shard_map/pallas_call | solution.py:446
  704.1 2.9 collective-permute-start.78
  711.3 8.8 %collective-permute-done.90 = f32[33,128]{1,0:T(8,128)S(1)} collective-permute-done((f32[33,128]{1,0:T(8,128)S(1)}, f32[33,128]{1,0:T(8,128)S(1)}, u32[]{:S(2)}, u32[]{:S(2)}) %collective-permute-start.90) | collective-permute-done | bytes 16928 | tf_op jit(solution)/shard_map/ppermute | solution.py:725
  721.8 3.0 collective-permute-start.82
  (440 shorter events, 209.7 us)
Async XLA Ops:
  7.2 269.2 %all-gather.5.cloned.1.call-start = ((), (), s32[]{:S(2)}) async-start(), calls=%async_computation.4 | async-start | bytes 12386304 | tf_op jit(solution)/shard_map/all_gather | solution.py:933
  11.9 33.0 %collective-permute-start = (bf16[64,1920]{1,0:T(8,128)(2,1)S(1)}, bf16[64,1920]{1,0:T(8,128)(2,1)S(1)}, u32[]{:S(2)}, u32[]{:S(2)}) collective-permute-start(bf16[64,1920]{1,0:T(8,128)(2,1)S(1)} %concatenate.107), channel_id=1, source_target_pairs={{0,6},{2,0},{4,2},{6,4},{1,7},{3,1},{5,3},{7,5},{8,14},{10,8},{12,... | collective-permute-start | bytes 737288 | tf_op jit(solution)/shard_map/ppermute | solution.py:730
  16.7 28.3 %collective-permute-start.1 = (bf16[64,1920]{1,0:T(8,128)(2,1)S(1)}, bf16[64,1920]{1,0:T(8,128)(2,1)S(1)}, u32[]{:S(2)}, u32[]{:S(2)}) collective-permute-start(bf16[64,1920]{1,0:T(8,128)(2,1)S(1)} %concatenate.107), channel_id=1, source_target_pairs={{0,4},{2,6},{4,0},{6,2},{1,5},{3,7},{5,1},{7,3},{8,12},{10,14},{12... | collective-permute-start | bytes 737288 | tf_op jit(solution)/shard_map/ppermute | solution.py:730
  16.7 28.3 %collective-permute-start.2 = (bf16[64,1920]{1,0:T(8,128)(2,1)S(1)}, bf16[64,1920]{1,0:T(8,128)(2,1)}, u32[]{:S(2)}, u32[]{:S(2)}) collective-permute-start(bf16[64,1920]{1,0:T(8,128)(2,1)S(1)} %concatenate.107), channel_id=1, source_target_pairs={{0,2},{2,4},{4,6},{6,0},{1,3},{3,5},{5,7},{7,1},{8,10},{10,12},{12... | collective-permute-start | bytes 737288 | tf_op jit(solution)/shard_map/ppermute | solution.py:730
  47.5 20.9 %collective-permute-start.8 = (bf16[4,64,1920]{2,1,0:T(8,128)(2,1)S(1)}, bf16[4,64,1920]{2,1,0:T(8,128)(2,1)S(1)}, u32[]{:S(2)}, u32[]{:S(2)}) collective-permute-start(bf16[4,64,1920]{2,1,0:T(8,128)(2,1)S(1)} %pad_maximum_fusion.8.refs_0_), channel_id=1, source_target_pairs={{0,16},{16,0},{1,17},{17,1},{2,18},{18,2},{3,19},{19,3},{4,20},{20... | collective-permute-start | bytes 2949128 | tf_op jit(solution)/shard_map/ppermute | solution.py:725
  49.1 20.6 %collective-permute-start.9 = (bf16[4,64,1920]{2,1,0:T(8,128)(2,1)S(1)}, bf16[4,64,1920]{2,1,0:T(8,128)(2,1)S(1)}, u32[]{:S(2)}, u32[]{:S(2)}) collective-permute-start(bf16[4,64,1920]{2,1,0:T(8,128)(2,1)S(1)} %pad_maximum_fusion.8.refs_0_), channel_id=1, source_target_pairs={{0,1},{1,0},{2,3},{3,2},{4,5},{5,4},{6,7},{7,6},{8,9},{9,8},{10,11... | collective-permute-start | bytes 2949128 | tf_op jit(solution)/shard_map/ppermute | solution.py:725
  71.4 23.9 %collective-permute-start.11 = (bf16[4,64,1408]{2,1,0:T(8,128)(2,1)}, bf16[4,64,1408]{2,1,0:T(8,128)(2,1)}, u32[]{:S(2)}, u32[]{:S(2)}) collective-permute-start(bf16[4,64,1408]{2,1,0:T(8,128)(2,1)} %slice.157), channel_id=1, source_target_pairs={{0,16},{16,0},{1,17},{17,1},{2,18},{18,2},{3,19},{19,3},{4,20},{20... | collective-permute-start | bytes 2162696 | tf_op jit(solution)/shard_map/ppermute | solution.py:725
  72.7 22.6 %collective-permute-start.10 = (bf16[4,64,512]{2,1,0:T(8,128)(2,1)}, bf16[4,64,512]{2,1,0:T(8,128)(2,1)}, u32[]{:S(2)}, u32[]{:S(2)}) collective-permute-start(bf16[4,64,512]{2,1,0:T(8,128)(2,1)} %slice.156), channel_id=1, source_target_pairs={{0,1},{1,0},{2,3},{3,2},{4,5},{5,4},{6,7},{7,6},{8,9},{9,8},{10,11... | collective-permute-start | bytes 786440 | tf_op jit(solution)/shard_map/ppermute | solution.py:725
  95.4 259.6 %all-gather.7.cloned.1.call-start = ((), (), s32[]{:S(2)}) async-start(), calls=%async_computation.5 | async-start | bytes 10616832 | tf_op jit(solution)/shard_map/all_gather | solution.py:973
  115.9 49.0 %collective-permute-start.26 = (bf16[256,2048]{1,0:T(8,128)(2,1)S(1)}, bf16[256,2048]{1,0:T(8,128)(2,1)}, u32[]{:S(2)}, u32[]{:S(2)}) collective-permute-start(bf16[256,2048]{1,0:T(8,128)(2,1)S(1)} %bitcast.239), channel_id=1, source_target_pairs={{0,16},{16,0},{1,17},{17,1},{2,18},{18,2},{3,19},{19,3},{4,20},{20... | collective-permute-start | bytes 3145736 | tf_op jit(solution)/shard_map/ppermute | solution.py:725
  116.5 48.4 %collective-permute-start.27 = (bf16[256,2048]{1,0:T(8,128)(2,1)S(1)}, bf16[256,2048]{1,0:T(8,128)(2,1)}, u32[]{:S(2)}, u32[]{:S(2)}) collective-permute-start(bf16[256,2048]{1,0:T(8,128)(2,1)S(1)} %bitcast.240), channel_id=1, source_target_pairs={{0,1},{1,0},{2,3},{3,2},{4,5},{5,4},{6,7},{7,6},{8,9},{9,8},{10,11... | collective-permute-start | bytes 3145736 | tf_op jit(solution)/shard_map/ppermute | solution.py:725
  117.2 20.0 %collective-permute-start.21 = (bf16[256,640]{1,0:T(8,128)(2,1)}, bf16[256,640]{1,0:T(8,128)(2,1)}, u32[]{:S(2)}, u32[]{:S(2)}) collective-permute-start(bf16[256,640]{1,0:T(8,128)(2,1)} %get-tuple-element.170.refs_0_), channel_id=1, source_target_pairs={{0,2},{2,4},{4,6},{1,3},{3,5},{5,7},{8,10},{10,12},{12,14},{9,11},... | collective-permute-start | bytes 983048 | tf_op jit(solution)/shard_map/ppermute | solution.py:772
  122.6 28.7 %collective-permute-start.22 = (bf16[256,640]{1,0:T(8,128)(2,1)}, bf16[256,640]{1,0:T(8,128)(2,1)}, u32[]{:S(2)}, u32[]{:S(2)}) collective-permute-start(bf16[256,640]{1,0:T(8,128)(2,1)} %get-tuple-element.170.refs_0_), channel_id=1, source_target_pairs={{0,4},{2,6},{1,5},{3,7},{8,12},{10,14},{9,13},{11,15},{16,20},{18,... | collective-permute-start | bytes 983048 | tf_op jit(solution)/shard_map/ppermute | solution.py:772
  127.4 37.6 %collective-permute-start.25 = (bf16[4,40,2048]{2,1,0:T(8,128)(2,1)S(1)}, bf16[4,40,2048]{2,1,0:T(8,128)(2,1)S(1)}, u32[]{:S(2)}, u32[]{:S(2)}) collective-permute-start(bf16[4,40,2048]{2,1,0:T(8,128)(2,1)S(1)} %constant_dynamic-slice_fusion.9), channel_id=1, source_target_pairs={{0,1},{1,0},{2,3},{3,2},{4,5},{5,4},{6,7},{7,6},{8,9},{9,8},{10,11... | collective-permute-start | bytes 1966088 | tf_op jit(solution)/shard_map/ppermute | solution.py:725
  137.2 27.7 %collective-permute-start.23 = (bf16[256,640]{1,0:T(8,128)(2,1)}, bf16[256,640]{1,0:T(8,128)(2,1)}, u32[]{:S(2)}, u32[]{:S(2)}) collective-permute-start(bf16[256,640]{1,0:T(8,128)(2,1)} %get-tuple-element.170.refs_0_), channel_id=1, source_target_pairs={{0,6},{1,7},{8,14},{9,15},{16,22},{17,23},{24,30},{25,31}} | collective-permute-start | bytes 983048 | tf_op jit(solution)/shard_map/ppermute | solution.py:772
  166.1 29.9 %collective-permute-start.31 = (bf16[4,2,40,2048]{3,2,1,0:T(8,128)(2,1)}, bf16[4,2,40,2048]{3,2,1,0:T(8,128)(2,1)S(1)}, u32[]{:S(2)}, u32[]{:S(2)}) collective-permute-start(bf16[4,2,40,2048]{3,2,1,0:T(8,128)(2,1)} %maximum_select_fusion.3), channel_id=1, source_target_pairs={{0,16},{16,0},{1,17},{17,1},{2,18},{18,2},{3,19},{19,3},{4,20},{20... | collective-permute-start | bytes 3932168 | tf_op jit(solution)/shard_map/ppermute | solution.py:725
  168.0 17.0 %collective-permute-start.29 = (bf16[256,640]{1,0:T(8,128)(2,1)}, bf16[256,640]{1,0:T(8,128)(2,1)S(1)}, u32[]{:S(2)}, u32[]{:S(2)}) collective-permute-start(bf16[256,640]{1,0:T(8,128)(2,1)} %collective-permute-done.22.refs_4_), channel_id=1, source_target_pairs={{0,1},{1,0},{2,3},{3,2},{4,5},{5,4},{6,7},{7,6},{8,9},{9,8},{10,11... | collective-permute-start | bytes 983048 | tf_op jit(solution)/shard_map/ppermute | solution.py:725
  169.1 20.5 %collective-permute-start.30 = (bf16[256,640]{1,0:T(8,128)(2,1)}, bf16[256,640]{1,0:T(8,128)(2,1)S(1)}, u32[]{:S(2)}, u32[]{:S(2)}) collective-permute-start(bf16[256,640]{1,0:T(8,128)(2,1)} %collective-permute-done.23.refs_6_), channel_id=1, source_target_pairs={{0,1},{1,0},{2,3},{3,2},{4,5},{5,4},{6,7},{7,6},{8,9},{9,8},{10,11... | collective-permute-start | bytes 983048 | tf_op jit(solution)/shard_map/ppermute | solution.py:725
  197.7 31.2 %collective-permute-start.32 = (bf16[2,4,2,40,2048]{4,3,2,1,0:T(8,128)(2,1)}, bf16[2,4,2,40,2048]{4,3,2,1,0:T(8,128)(2,1)}, u32[]{:S(2)}, u32[]{:S(2)}) collective-permute-start(bf16[2,4,2,40,2048]{4,3,2,1,0:T(8,128)(2,1)} %maximum_select_fusion.1), channel_id=1, source_target_pairs={{0,8},{8,0},{1,9},{9,1},{2,10},{10,2},{3,11},{11,3},{4,12},{12,4},... | collective-permute-start | bytes 7864328 | tf_op jit(solution)/shard_map/ppermute | solution.py:725
  201.1 22.7 %collective-permute-start.33 = (bf16[3,256,768]{2,1,0:T(8,128)(2,1)}, bf16[3,256,768]{2,1,0:T(8,128)(2,1)}, u32[]{:S(2)}, u32[]{:S(2)}) collective-permute-start(bf16[3,256,768]{2,1,0:T(8,128)(2,1)} %pad_maximum_fusion.3), channel_id=1, source_target_pairs={{1,8},{8,1},{3,10},{10,3},{5,12},{12,5},{7,14},{14,7},{17,24},{24,... | collective-permute-start | bytes 3538952 | tf_op jit(solution)/shard_map/ppermute | solution.py:765
  202.8 26.2 %collective-permute-start.34 = (bf16[256,2048]{1,0:T(8,128)(2,1)}, bf16[256,2048]{1,0:T(8,128)(2,1)}, u32[]{:S(2)}, u32[]{:S(2)}) collective-permute-start(bf16[256,2048]{1,0:T(8,128)(2,1)} %collective-permute-done.27.refs_6_), channel_id=1, source_target_pairs={{0,16},{16,0},{1,17},{17,1},{2,18},{18,2},{3,19},{19,3},{4,20},{20... | collective-permute-start | bytes 3145736 | tf_op jit(solution)/shard_map/ppermute | solution.py:725
  229.0 374.2 %reduce-scatter.3.cloned.1.call-start = ((), (), s32[]{:S(2)}) async-start(), calls=%async_computation.2 | async-start | bytes 6881280 | tf_op jit(solution)/shard_map/reduce_scatter | solution.py:993
  236.1 25.2 %collective-permute-start.35 = (bf16[256,2048]{1,0:T(8,128)(2,1)S(1)}, bf16[256,2048]{1,0:T(8,128)(2,1)S(1)}, u32[]{:S(2)}, u32[]{:S(2)}) collective-permute-start(bf16[256,2048]{1,0:T(8,128)(2,1)S(1)} %multiply_convert_fusion.refs_0_), channel_id=1, source_target_pairs={{0,16},{16,0},{1,17},{17,1},{2,18},{18,2},{3,19},{19,3},{4,20},{20... | collective-permute-start | bytes 3145736 | tf_op jit(solution)/shard_map/ppermute | solution.py:725
  237.0 25.4 %collective-permute-start.36 = (bf16[256,2048]{1,0:T(8,128)(2,1)S(1)}, bf16[256,2048]{1,0:T(8,128)(2,1)S(1)}, u32[]{:S(2)}, u32[]{:S(2)}) collective-permute-start(bf16[256,2048]{1,0:T(8,128)(2,1)S(1)} %multiply_convert_fusion.refs_0_), channel_id=1, source_target_pairs={{0,1},{1,0},{2,3},{3,2},{4,5},{5,4},{6,7},{7,6},{8,9},{9,8},{10,11... | collective-permute-start | bytes 3145736 | tf_op jit(solution)/shard_map/ppermute | solution.py:725
  354.5 355.4 %reduce-scatter.5.cloned.1.call-start = ((), (), s32[]{:S(2)}) async-start(), calls=%async_computation.3 | async-start | bytes 5898240 | tf_op jit(solution)/shard_map/reduce_scatter | solution.py:993
  399.2 37.9 %collective-permute-start.44 = (bf16[4,3,256,768]{3,2,1,0:T(8,128)(2,1)}, bf16[4,3,256,768]{3,2,1,0:T(8,128)(2,1)}, u32[]{:S(2)}, u32[]{:S(2)}) collective-permute-start(bf16[4,3,256,768]{3,2,1,0:T(8,128)(2,1)} %get-tuple-element.230), channel_id=1, source_target_pairs={{0,8},{8,0},{1,9},{9,1},{2,10},{10,2},{3,11},{11,3},{4,12},{12,4},... | collective-permute-start | bytes 14155784 | tf_op jit(solution)/shard_map/ppermute | solution.py:725
  419.1 25.2 %collective-permute-start.43 = (bf16[256,2048]{1,0:T(8,128)(2,1)}, bf16[256,2048]{1,0:T(8,128)(2,1)}, u32[]{:S(2)}, u32[]{:S(2)}) collective-permute-start(bf16[256,2048]{1,0:T(8,128)(2,1)} %pad_maximum_fusion.5), channel_id=1, source_target_pairs={{0,1},{1,0},{2,3},{3,2},{4,5},{5,4},{6,7},{7,6},{8,9},{9,8},{10,11... | collective-permute-start | bytes 3145736 | tf_op jit(solution)/shard_map/ppermute | solution.py:725
  422.5 24.2 %collective-permute-start.42 = (bf16[256,2048]{1,0:T(8,128)(2,1)}, bf16[256,2048]{1,0:T(8,128)(2,1)}, u32[]{:S(2)}, u32[]{:S(2)}) collective-permute-start(bf16[256,2048]{1,0:T(8,128)(2,1)} %pad_maximum_fusion.4), channel_id=1, source_target_pairs={{0,16},{16,0},{1,17},{17,1},{2,18},{18,2},{3,19},{19,3},{4,20},{20... | collective-permute-start | bytes 3145736 | tf_op jit(solution)/shard_map/ppermute | solution.py:725
  448.9 31.9 %collective-permute-start.45 = (bf16[256,1024]{1,0:T(8,128)(2,1)}, bf16[256,1024]{1,0:T(8,128)(2,1)}, u32[]{:S(2)}, u32[]{:S(2)}) collective-permute-start(bf16[256,1024]{1,0:T(8,128)(2,1)} %get-tuple-element.366), channel_id=1, source_target_pairs={{0,16},{16,0},{1,17},{17,1},{2,18},{18,2},{3,19},{19,3},{4,20},{20... | collective-permute-start | bytes 1572872 | tf_op jit(solution)/shard_map/ppermute | solution.py:725
  449.9 32.1 %collective-permute-start.46 = (bf16[256,1024]{1,0:T(8,128)(2,1)}, bf16[256,1024]{1,0:T(8,128)(2,1)}, u32[]{:S(2)}, u32[]{:S(2)}) collective-permute-start(bf16[256,1024]{1,0:T(8,128)(2,1)} %get-tuple-element.365), channel_id=1, source_target_pairs={{0,1},{1,0},{2,3},{3,2},{4,5},{5,4},{6,7},{7,6},{8,9},{9,8},{10,11... | collective-permute-start | bytes 1572872 | tf_op jit(solution)/shard_map/ppermute | solution.py:725
  489.7 29.3 %collective-permute-start.49 = (bf16[2,4,2,40,2048]{4,3,1,2,0:T(8,128)(2,1)}, bf16[2,4,2,40,2048]{4,3,1,2,0:T(8,128)(2,1)}, u32[]{:S(2)}, u32[]{:S(2)}) collective-permute-start(bf16[2,4,2,40,2048]{4,3,1,2,0:T(8,128)(2,1)} %bitcast.206), channel_id=1, source_target_pairs={{0,8},{8,0},{1,9},{9,1},{2,10},{10,2},{3,11},{11,3},{4,12},{12,4},... | collective-permute-start | bytes 7864328 | tf_op jit(solution)/shard_map/ppermute | solution.py:725
  495.2 28.7 %collective-permute-start.48 = (bf16[256,2048]{1,0:T(8,128)(2,1)}, bf16[256,2048]{1,0:T(8,128)(2,1)}, u32[]{:S(2)}, u32[]{:S(2)}) collective-permute-start(bf16[256,2048]{1,0:T(8,128)(2,1)} %pad_maximum_fusion.7), channel_id=1, source_target_pairs={{0,1},{1,0},{2,3},{3,2},{4,5},{5,4},{6,7},{7,6},{8,9},{9,8},{10,11... | collective-permute-start | bytes 3145736 | tf_op jit(solution)/shard_map/ppermute | solution.py:725
  498.4 26.7 %collective-permute-start.47 = (bf16[256,2048]{1,0:T(8,128)(2,1)}, bf16[256,2048]{1,0:T(8,128)(2,1)}, u32[]{:S(2)}, u32[]{:S(2)}) collective-permute-start(bf16[256,2048]{1,0:T(8,128)(2,1)} %pad_maximum_fusion.6), channel_id=1, source_target_pairs={{0,16},{16,0},{1,17},{17,1},{2,18},{18,2},{3,19},{19,3},{4,20},{20... | collective-permute-start | bytes 3145736 | tf_op jit(solution)/shard_map/ppermute | solution.py:725
  528.7 31.2 %collective-permute-start.63 = (bf16[4,2,40,2048]{3,2,0,1:T(8,128)(2,1)S(1)}, bf16[4,2,40,2048]{3,2,0,1:T(8,128)(2,1)S(1)}, u32[]{:S(2)}, u32[]{:S(2)}) collective-permute-start(bf16[4,2,40,2048]{3,2,0,1:T(8,128)(2,1)S(1)} %dynamic-slice_bitcast_fusion), channel_id=1, source_target_pairs={{0,16},{16,0},{1,17},{17,1},{2,18},{18,2},{3,19},{19,3},{4,20},{20... | collective-permute-start | bytes 3932168 | tf_op jit(solution)/shard_map/ppermute | solution.py:725
  531.9 29.5 %collective-permute-start.61 = (bf16[2,4,2,64,640]{4,3,1,2,0:T(8,128)(2,1)S(1)}, bf16[2,4,2,64,640]{4,3,1,2,0:T(8,128)(2,1)S(1)}, u32[]{:S(2)}, u32[]{:S(2)}) collective-permute-start(bf16[2,4,2,64,640]{4,3,1,2,0:T(8,128)(2,1)S(1)} %bitcast.231), channel_id=1, source_target_pairs={{0,8},{8,0},{1,9},{9,1},{2,10},{10,2},{3,11},{11,3},{4,12},{12,4},... | collective-permute-start | bytes 3932168 | tf_op jit(solution)/shard_map/ppermute | solution.py:725
  535.1 45.8 %collective-permute-start.54 = (bf16[128,640]{1,0:T(8,128)(2,1)S(1)}, bf16[128,640]{1,0:T(8,128)(2,1)S(1)}, u32[]{:S(2)}, u32[]{:S(2)}) collective-permute-start(bf16[128,640]{1,0:T(8,128)(2,1)S(1)} %copy-done.36), channel_id=1, source_target_pairs={{2,0},{4,2},{6,4},{3,1},{5,3},{7,5},{10,8},{12,10},{14,12},{11,9},... | collective-permute-start | bytes 491528 | tf_op jit(solution)/shard_map/ppermute | solution.py:772
  536.4 66.1 %collective-permute-start.55 = (bf16[128,640]{1,0:T(8,128)(2,1)S(1)}, bf16[128,640]{1,0:T(8,128)(2,1)S(1)}, u32[]{:S(2)}, u32[]{:S(2)}) collective-permute-start(bf16[128,640]{1,0:T(8,128)(2,1)S(1)} %copy-done.35), channel_id=1, source_target_pairs={{4,0},{6,2},{5,1},{7,3},{12,8},{14,10},{13,9},{15,11},{20,16},{22,... | collective-permute-start | bytes 491528 | tf_op jit(solution)/shard_map/ppermute | solution.py:772
  537.7 65.5 %collective-permute-start.56 = (bf16[128,640]{1,0:T(8,128)(2,1)S(1)}, bf16[128,640]{1,0:T(8,128)(2,1)}, u32[]{:S(2)}, u32[]{:S(2)}) collective-permute-start(bf16[128,640]{1,0:T(8,128)(2,1)S(1)} %copy-done.34), channel_id=1, source_target_pairs={{6,0},{7,1},{14,8},{15,9},{22,16},{23,17},{30,24},{31,25}} | collective-permute-start | bytes 491528 | tf_op jit(solution)/shard_map/ppermute | solution.py:772
  604.4 31.2 %collective-permute-start.69 = (bf16[4,40,2048]{2,1,0:T(8,128)(2,1)S(1)}, bf16[4,40,2048]{2,1,0:T(8,128)(2,1)S(1)}, u32[]{:S(2)}, u32[]{:S(2)}) collective-permute-start(bf16[4,40,2048]{2,1,0:T(8,128)(2,1)S(1)} %dynamic-slice_bitcast_fusion.2), channel_id=1, source_target_pairs={{0,1},{1,0},{2,3},{3,2},{4,5},{5,4},{6,7},{7,6},{8,9},{9,8},{10,11... | collective-permute-start | bytes 1966088 | tf_op jit(solution)/shard_map/ppermute | solution.py:725
  606.2 27.9 %collective-permute-start.68 = (bf16[2,4,64,640]{3,2,1,0:T(8,128)(2,1)S(1)}, bf16[2,4,64,640]{3,2,1,0:T(8,128)(2,1)S(1)}, u32[]{:S(2)}, u32[]{:S(2)}) collective-permute-start(bf16[2,4,64,640]{3,2,1,0:T(8,128)(2,1)S(1)} %dynamic-slice_bitcast_fusion.3), channel_id=1, source_target_pairs={{0,1},{1,0},{2,3},{3,2},{4,5},{5,4},{6,7},{7,6},{8,9},{9,8},{10,11... | collective-permute-start | bytes 1966088 | tf_op jit(solution)/shard_map/ppermute | solution.py:725
  611.1 27.5 %collective-permute-start.67 = (bf16[4,2,64,640]{3,2,0,1:T(8,128)(2,1)S(1)}, bf16[4,2,64,640]{3,2,0,1:T(8,128)(2,1)S(1)}, u32[]{:S(2)}, u32[]{:S(2)}) collective-permute-start(bf16[4,2,64,640]{3,2,0,1:T(8,128)(2,1)S(1)} %dynamic-slice_bitcast_fusion.4), channel_id=1, source_target_pairs={{0,16},{16,0},{1,17},{17,1},{2,18},{18,2},{3,19},{19,3},{4,20},{20... | collective-permute-start | bytes 1966088 | tf_op jit(solution)/shard_map/ppermute | solution.py:725
  611.7 27.9 %collective-permute-start.64 = (bf16[128,640]{1,0:T(8,128)(2,1)S(1)}, bf16[128,640]{1,0:T(8,128)(2,1)S(1)}, u32[]{:S(2)}, u32[]{:S(2)}) collective-permute-start(bf16[128,640]{1,0:T(8,128)(2,1)S(1)} %copy-done.39), channel_id=1, source_target_pairs={{2,0},{4,2},{6,4},{3,1},{5,3},{7,5},{10,8},{12,10},{14,12},{11,9},... | collective-permute-start | bytes 491528 | tf_op jit(solution)/shard_map/ppermute | solution.py:772
  613.0 26.6 %collective-permute-start.65 = (bf16[128,640]{1,0:T(8,128)(2,1)S(1)}, bf16[128,640]{1,0:T(8,128)(2,1)S(1)}, u32[]{:S(2)}, u32[]{:S(2)}) collective-permute-start(bf16[128,640]{1,0:T(8,128)(2,1)S(1)} %copy-done.38), channel_id=1, source_target_pairs={{4,0},{6,2},{5,1},{7,3},{12,8},{14,10},{13,9},{15,11},{20,16},{22,... | collective-permute-start | bytes 491528 | tf_op jit(solution)/shard_map/ppermute | solution.py:772
  635.6 55.9 %collective-permute-start.84 = (bf16[3,256,896]{2,1,0:T(8,128)(2,1)}, bf16[3,256,896]{2,1,0:T(8,128)(2,1)}, u32[]{:S(2)}, u32[]{:S(2)}) collective-permute-start(bf16[3,256,896]{2,1,0:T(8,128)(2,1)} %bitcast.61), channel_id=1, source_target_pairs={{1,8},{8,1},{3,10},{10,3},{5,12},{12,5},{7,14},{14,7},{17,24},{24,... | collective-permute-start | bytes 4128776 | tf_op jit(solution)/shard_map/ppermute | solution.py:765
  651.5 26.4 %collective-permute-start.70 = (bf16[2,4,2,64,640]{4,3,1,0,2:T(8,128)(2,1)}, bf16[2,4,2,64,640]{4,3,1,0,2:T(8,128)(2,1)}, u32[]{:S(2)}, u32[]{:S(2)}) collective-permute-start(bf16[2,4,2,64,640]{4,3,1,0,2:T(8,128)(2,1)} %bitcast.207), channel_id=1, source_target_pairs={{0,8},{8,0},{1,9},{9,1},{2,10},{10,2},{3,11},{11,3},{4,12},{12,4},... | collective-permute-start | bytes 3932168 | tf_op jit(solution)/shard_map/ppermute | solution.py:725
  700.7 21.1 %collective-permute-start.76 = (bf16[64,1280]{1,0:T(8,128)(2,1)}, bf16[64,1280]{1,0:T(8,128)(2,1)S(1)}, u32[]{:S(2)}, u32[]{:S(2)}) collective-permute-start(bf16[64,1280]{1,0:T(8,128)(2,1)} %get-tuple-element.369), channel_id=1, source_target_pairs={{0,2},{2,4},{4,6},{6,0},{1,3},{3,5},{5,7},{7,1},{8,10},{10,12},{12... | collective-permute-start | bytes 491528 | tf_op jit(solution)/shard_map/ppermute | solution.py:730
  702.3 22.5 %collective-permute-start.77 = (bf16[64,1280]{1,0:T(8,128)(2,1)}, bf16[64,1280]{1,0:T(8,128)(2,1)}, u32[]{:S(2)}, u32[]{:S(2)}) collective-permute-start(bf16[64,1280]{1,0:T(8,128)(2,1)} %get-tuple-element.370), channel_id=1, source_target_pairs={{0,4},{2,6},{4,0},{6,2},{1,5},{3,7},{5,1},{7,3},{8,12},{10,14},{12... | collective-permute-start | bytes 491528 | tf_op jit(solution)/shard_map/ppermute | solution.py:730
  704.1 21.6 %collective-permute-start.78 = (bf16[64,1280]{1,0:T(8,128)(2,1)}, bf16[64,1280]{1,0:T(8,128)(2,1)}, u32[]{:S(2)}, u32[]{:S(2)}) collective-permute-start(bf16[64,1280]{1,0:T(8,128)(2,1)} %get-tuple-element.371), channel_id=1, source_target_pairs={{0,6},{2,0},{4,2},{6,4},{1,7},{3,1},{5,3},{7,5},{8,14},{10,8},{12,... | collective-permute-start | bytes 491528 | tf_op jit(solution)/shard_map/ppermute | solution.py:730
  (111 other events, 1092.9 us)
Sparse Core Ops, SparseCore 0:
  95.5 119.9 all-gather.4
  229.1 121.0 all-gather.6
  354.6 128.5 reduce-scatter.2
  485.4 123.2 reduce-scatter.4
